TPU v7x, 128 devices: a whole 4x4x4 slice. The times are simulated.
128 devices in a mesh: prow: 8 (over x, core), pcol: 16 (over y, z).
Axes of the slice: x: 4, y: 4, z: 4, core: 2. Of those that a mesh axis runs over, the one named last changes fastest.
Arguments:
- children: bfloat16 [131072, 6144], P(('prow', 'pcol')), may hold values from -6 to 6
- row_owner: int32 [1024, 1], P(('prow', 'pcol')), may hold values from 0 to 7; in each aligned block of 8 rows (0 to 7, 8 to 15, ...) at most 2 rows name the same one
- row_local: int32 [1024], P(('prow', 'pcol')), may hold values from 0 to 87
- row_within: int32 [1024, 128], P(('prow', 'pcol')), may hold values from 0 to 127, each once within a row
- column_tile: int32 [2, 48], replicated, may hold values from 0 to 63, as said below
- column_within: int32 [2, 48, 128], replicated, may hold values from 0 to 127, each once within a row
- pivot_rows: int32 [128], replicated, may hold values from 0 to 90111, as said below
- lower_inverse: bfloat16 [128, 128], replicated, as said below
- upper_inverse: bfloat16 [128, 128], replicated, as said below
Outputs:
- updated: bfloat16 [90112, 8192], P('prow', 'pcol')
Inputs may be any that keep to these rules, and one draw needn't show every extreme that they name: `row_owner`: among the 8 entries of one device no value appears more than 2 times, and on some device one value appears exactly 2 times. `row_within`: each row of 128 entries is a permutation of 0 to 127. `column_tile`: each row names 48 different slab tiles, and in each row all 4 tiles q * 4 to (q + 1) * 4 - 1 of some index q of pcol are named. `column_within`: each last-dimension row is a permutation of 0 to 127. `pivot_rows`: 128 different front rows. `lower_inverse`: zero above the diagonal, positive diagonal. `upper_inverse`: zero below the diagonal, positive diagonal.
All inputs are finite; a program needn't handle non-finite values.
Results may differ from a plain program's by a relative error of at most 0.0065.
Values may be sent and summed in bfloat16 or wider, within the bound.
No kernel may reach another device: no remote copies, remote signals or barrier semaphores. Data moves between devices by JAX's collectives and lax.ppermute only.
A program may use at most 320 MiB of HBM per device.

v0:
```python
import jax
import jax.numpy as jnp
from jax import lax
from jax.sharding import PartitionSpec as P

FRONT = 90112
SLAB = 8192


def from_root(value, axis, source):
    kept = jnp.where(lax.axis_index(axis) == source, value, 0).astype(value.dtype)
    return lax.psum(kept, axis)


def one_hot_rows(positions, count):
    slot_ids = jnp.arange(count, dtype=jnp.int32)
    return (positions[..., None] == slot_ids).astype(jnp.bfloat16)


def on_device(
    children,
    row_owner,
    row_local,
    row_within,
    column_tile,
    column_within,
    pivot_rows,
    lower_inverse,
    upper_inverse,
):
    tile_size = lower_inverse.shape[0]
    row_groups = lax.axis_size("prow")
    col_groups = lax.axis_size("pcol")
    local_rows = FRONT // row_groups
    local_cols = SLAB // col_groups
    front_tiles = local_rows // tile_size
    slab_tiles_here = local_cols // tile_size
    own_tiles = row_local.shape[0]
    capacity = max(2, 2 * own_tiles // row_groups)
    child_col_tiles = children.shape[1] // tile_size
    my_prow = lax.axis_index("prow")
    child_index = my_prow // (row_groups // 2)
    my_col_tile = jnp.take(column_tile, child_index, axis=0)
    my_col_within = jnp.take(column_within, child_index, axis=0)
    tile_blocks = children.reshape(own_tiles, tile_size, child_col_tiles, tile_size)
    moved_tiles = jnp.einsum(
        "tiuk,ukj->tuij",
        tile_blocks,
        one_hot_rows(my_col_within, tile_size),
        preferred_element_type=jnp.float32,
    ).astype(jnp.bfloat16)
    owners = row_owner[:, 0]
    owner_hits = (owners[:, None] == jnp.arange(row_groups, dtype=jnp.int32)[None, :]).astype(
        jnp.int32
    )
    slot_rank = jnp.sum((jnp.cumsum(owner_hits, axis=0) - owner_hits) * owner_hits, axis=1)
    target_device = my_col_tile // slab_tiles_here
    target_slot = my_col_tile % slab_tiles_here
    outgoing = jnp.zeros(
        (row_groups, col_groups, capacity, tile_size, slab_tiles_here, tile_size), jnp.bfloat16
    )
    outgoing = outgoing.at[
        owners[:, None], target_device[None, :], slot_rank[:, None], :, target_slot[None, :], :
    ].set(moved_tiles)
    outgoing = outgoing.reshape(row_groups, col_groups, capacity * tile_size, local_cols)
    row_marks = jnp.full(
        (row_groups, col_groups, capacity, tile_size), front_tiles * tile_size, jnp.int32
    )
    row_target = row_local[:, None] * tile_size + row_within
    row_marks = row_marks.at[owners, :, slot_rank].set(
        jnp.broadcast_to(row_target[:, None, :], (own_tiles, col_groups, tile_size))
    )
    arrived, arrived_marks = (
        lax.all_to_all(
            outgoing.reshape(row_groups * col_groups, capacity * tile_size, local_cols),
            ("prow", "pcol"),
            split_axis=0,
            concat_axis=0,
            tiled=True,
        ),
        lax.all_to_all(
            row_marks.reshape(row_groups * col_groups, capacity, tile_size),
            ("prow", "pcol"),
            split_axis=0,
            concat_axis=0,
            tiled=True,
        ),
    )
    arrived = arrived.reshape(row_groups, col_groups * capacity, tile_size, local_cols)
    arrived_marks = arrived_marks.reshape(row_groups, col_groups * capacity, tile_size)

    def collect(source_group, running_sum):
        source_piece = lax.dynamic_index_in_dim(arrived, source_group, 0, keepdims=False)
        piece_marks = lax.dynamic_index_in_dim(arrived_marks, source_group, 0, keepdims=False)
        where_tile = piece_marks[:, 0] // tile_size
        placed = jnp.einsum(
            "sic,sir->src",
            source_piece,
            one_hot_rows(piece_marks % tile_size, tile_size),
            preferred_element_type=jnp.float32,
        )
        return running_sum.at[where_tile].add(placed, mode="drop")

    front_sum = lax.fori_loop(
        0, row_groups, collect, jnp.zeros((front_tiles, tile_size, local_cols), jnp.float32)
    )
    front_local = front_sum.reshape(local_rows, local_cols).astype(jnp.bfloat16)
    pivot_owner = pivot_rows // local_rows
    pivot_local = pivot_rows % local_rows
    is_mine = pivot_owner == my_prow
    picked = jnp.where(
        is_mine[:, None], jnp.take(front_local, pivot_local, axis=0).astype(jnp.float32), 0.0
    )
    pivot_block = lax.psum(picked.astype(jnp.bfloat16), "prow")
    upper_rows = jnp.dot(lower_inverse, pivot_block, preferred_element_type=jnp.float32).astype(
        jnp.bfloat16
    )
    panel_cols = from_root(front_local[:, :tile_size], "pcol", 0)
    lower_panel = jnp.dot(panel_cols, upper_inverse, preferred_element_type=jnp.float32).astype(
        jnp.bfloat16
    )
    schur_part = (
        front_local.astype(jnp.float32)
        - jnp.dot(lower_panel, upper_rows, preferred_element_type=jnp.float32)
    ).astype(jnp.bfloat16)
    pivot_slot = jnp.where(is_mine, pivot_local, local_rows)
    schur_part = schur_part.at[pivot_slot].set(upper_rows, mode="drop")
    panel_fill = jnp.where(lax.axis_index("pcol") == 0, lower_panel, schur_part[:, :tile_size])
    return schur_part.at[:, :tile_size].set(panel_fill)


def solution(mesh):
    placed = (
        P(("prow", "pcol"), None),
        P(("prow", "pcol"), None),
        P(("prow", "pcol")),
        P(("prow", "pcol"), None),
        P(),
        P(),
        P(),
        P(),
        P(),
    )
    return jax.shard_map(
        on_device, mesh=mesh, in_specs=placed, out_specs=P("prow", "pcol"), check_vma=False
    )
```

profile of v0, /device:TPU:1, one launch (start us, length us, event | category | flops | bytes accessed | tf_op | source)
XLA Modules:
  0.0 1191.5 jit_solution(16727761320901192359)
XLA Ops:
  11.8 11.5 all-to-all-start
  24.7 11.6 copy.39
  36.3 14.1 %convert_bitcast_fusion = bf16[8,48,128,128]{2,3,0,1:T(8,128)(2,1)} fusion(bf16[8,128,48,128]{3,2,1,0:T(8,128)(2,1)} %bitcast.62, s32[48,128]{1,0:T(8,128)S(1)} %select_bitcast_fusion), kind=kOutput, calls=%fused_computation.26 | convolution fusion | flops 1617690624 | bytes 25190400 | tf_op jit(solution)/shard_map/tiuk,ukj->tuij/dot_general | solution.py:46
  50.4 16.7 %copy.33 = bf16[8,48,128,128]{3,2,1,0:T(8,128)(2,1)} copy(bf16[8,48,128,128]{2,3,0,1:T(8,128)(2,1)} %convert_bitcast_fusion) | data formatting | bytes 25165824 | tf_op jit(solution)/shard_map/convert_element_type | solution.py:51
  67.3 11.2 broadcast_in_dim.112
  78.6 68.4 %scatter_fusion.2 = bf16[8,16,2,128,4,128]{5,3,4,2,1,0:T(8,128)(2,1)} fusion(bf16[8,16,2,128,4,128]{5,3,4,2,1,0:T(8,128)(2,1)} %broadcast_in_dim.112, s32[384]{0:T(512)S(1)} %reshape.188, bf16[384,128,128]{2,1,0:T(8,128)(2,1)} %bitcast.63), kind=kCustom, calls=%fused_computation.3 | custom fusion | bytes 37754880 | tf_op jit(solution)/shard_map/scatter | solution.py:64
  147.0 37.7 %copy.34 = bf16[8,16,2,128,4,128]{5,4,3,2,1,0:T(4,128)(2,1)} copy(bf16[8,16,2,128,4,128]{5,3,4,2,1,0:T(8,128)(2,1)} %scatter_fusion.2) | data formatting | bytes 67108864 | tf_op jit(solution)/shard_map/scatter | solution.py:64
  184.7 48.5 %reshape_reshape.3 = bf16[128,256,512]{2,1,0:T(8,128)(2,1)} reshape(bf16[8,16,2,128,4,128]{5,4,3,2,1,0:T(4,128)(2,1)} %copy.34) | data formatting | bytes 67108864 | tf_op jit(solution)/shard_map/reshape;reshape | solution.py:75
  233.2 10.3 all-to-all-start.1
  243.8 481.7 %all-to-all-done.1 = bf16[128,256,512]{2,1,0:T(8,128)(2,1)} async-done(((bf16[128,256,512]{2,1,0:T(8,128)(2,1)}), bf16[128,256,512]{2,1,0:T(8,128)(2,1)}, u32[]{:S(2)}, u32[]{:S(2)}) %all-to-all-start.1) | async-done | bytes 33554464 | tf_op jit(solution)/shard_map/all_to_all | solution.py:74
  725.4 10.6 broadcast_in_dim.109
  736.0 194.9 %while.18 = (s32[]{:T(128)}, f32[88,128,512]{2,1,0:T(8,128)}, s32[8,32,128]{2,1,0:T(8,128)S(1)}, bf16[8,32,128,512]{3,2,1,0:T(8,128)(2,1)}, s32[]{:T(128)}) while((s32[]{:T(128)}, f32[88,128,512]{2,1,0:T(8,128)}, s32[8,32,128]{2,1,0:T(8,128)S(1)}, bf16[8,32,128,512]{3,2,1,0:T(8,128)(2,1)}, s32[]{:T(128)}) %tuple.68), condition=%wide.region_6.7_spmd, body=%wide.region_4.6_spmd.sunk | while | flops 539537984 | bytes 37897152 | solution.py:104
  743.0 17.3 %scatter_fusion = f32[88,128,512]{2,1,0:T(8,128)} fusion(f32[88,128,512]{2,1,0:T(8,128)} %get-tuple-element.218, s32[32]{0:T(128)S(1)} %fusion.31, f32[32,128,512]{2,1,0:T(8,128)} %fusion.32), kind=kCustom, calls=%fused_computation.1.clone.1 | custom fusion | flops 2097152 | bytes 25165952 | tf_op jit(solution)/shard_map/while/body/eval_jaxpr/scatter-add | solution.py:102
  767.4 17.2 %scatter_fusion = f32[88,128,512]{2,1,0:T(8,128)} fusion(f32[88,128,512]{2,1,0:T(8,128)} %get-tuple-element.218, s32[32]{0:T(128)S(1)} %fusion.31, f32[32,128,512]{2,1,0:T(8,128)} %fusion.32), kind=kCustom, calls=%fused_computation.1.clone.1 | custom fusion | flops 2097152 | bytes 25165952 | tf_op jit(solution)/shard_map/while/body/eval_jaxpr/scatter-add | solution.py:102
  791.7 17.2 %scatter_fusion = f32[88,128,512]{2,1,0:T(8,128)} fusion(f32[88,128,512]{2,1,0:T(8,128)} %get-tuple-element.218, s32[32]{0:T(128)S(1)} %fusion.31, f32[32,128,512]{2,1,0:T(8,128)} %fusion.32), kind=kCustom, calls=%fused_computation.1.clone.1 | custom fusion | flops 2097152 | bytes 25165952 | tf_op jit(solution)/shard_map/while/body/eval_jaxpr/scatter-add | solution.py:102
  815.9 17.3 %scatter_fusion = f32[88,128,512]{2,1,0:T(8,128)} fusion(f32[88,128,512]{2,1,0:T(8,128)} %get-tuple-element.218, s32[32]{0:T(128)S(1)} %fusion.31, f32[32,128,512]{2,1,0:T(8,128)} %fusion.32), kind=kCustom, calls=%fused_computation.1.clone.1 | custom fusion | flops 2097152 | bytes 25165952 | tf_op jit(solution)/shard_map/while/body/eval_jaxpr/scatter-add | solution.py:102
  840.2 17.4 %scatter_fusion = f32[88,128,512]{2,1,0:T(8,128)} fusion(f32[88,128,512]{2,1,0:T(8,128)} %get-tuple-element.218, s32[32]{0:T(128)S(1)} %fusion.31, f32[32,128,512]{2,1,0:T(8,128)} %fusion.32), kind=kCustom, calls=%fused_computation.1.clone.1 | custom fusion | flops 2097152 | bytes 25165952 | tf_op jit(solution)/shard_map/while/body/eval_jaxpr/scatter-add | solution.py:102
  864.6 17.5 %scatter_fusion = f32[88,128,512]{2,1,0:T(8,128)} fusion(f32[88,128,512]{2,1,0:T(8,128)} %get-tuple-element.218, s32[32]{0:T(128)S(1)} %fusion.31, f32[32,128,512]{2,1,0:T(8,128)} %fusion.32), kind=kCustom, calls=%fused_computation.1.clone.1 | custom fusion | flops 2097152 | bytes 25165952 | tf_op jit(solution)/shard_map/while/body/eval_jaxpr/scatter-add | solution.py:102
  889.1 17.4 %scatter_fusion = f32[88,128,512]{2,1,0:T(8,128)} fusion(f32[88,128,512]{2,1,0:T(8,128)} %get-tuple-element.218, s32[32]{0:T(128)S(1)} %fusion.31, f32[32,128,512]{2,1,0:T(8,128)} %fusion.32), kind=kCustom, calls=%fused_computation.1.clone.1 | custom fusion | flops 2097152 | bytes 25165952 | tf_op jit(solution)/shard_map/while/body/eval_jaxpr/scatter-add | solution.py:102
  913.6 17.3 %scatter_fusion = f32[88,128,512]{2,1,0:T(8,128)} fusion(f32[88,128,512]{2,1,0:T(8,128)} %get-tuple-element.218, s32[32]{0:T(128)S(1)} %fusion.31, f32[32,128,512]{2,1,0:T(8,128)} %fusion.32), kind=kCustom, calls=%fused_computation.1.clone.1 | custom fusion | flops 2097152 | bytes 25165952 | tf_op jit(solution)/shard_map/while/body/eval_jaxpr/scatter-add | solution.py:102
  930.9 12.4 %convert_element_type.45 = bf16[88,128,512]{2,1,0:T(8,128)(2,1)} convert(f32[88,128,512]{2,1,0:T(8,128)} %get-tuple-element.130) | non-fusion elementwise | flops 5767168 | bytes 34603008 | tf_op jit(solution)/shard_map/convert_element_type | solution.py:107
  954.7 103.1 %all-reduce.5.cloned.1.call-done = bf16[128,512]{1,0:T(8,128)(2,1)} async-done(((bf16[128,512]{1,0:T(8,128)(2,1)}), bf16[128,512]{1,0:T(8,128)(2,1)}) %all-reduce.5.cloned.1.call-update) | async-done | bytes 131088 | tf_op jit(solution)/shard_map/psum | solution.py:114
  1059.1 97.8 %all-reduce.3.cloned.1.call-done = bf16[11264,128]{1,0:T(8,128)(2,1)} async-done(((bf16[11264,128]{1,0:T(8,128)(2,1)}), bf16[11264,128]{1,0:T(8,128)(2,1)}) %all-reduce.3.cloned.1.call-update) | async-done | bytes 2883600 | tf_op jit(solution)/shard_map/psum | solution.py:12
  1168.3 12.3 %scatter_fusion.3 = bf16[11264,512]{1,0:T(8,128)(2,1)} fusion(bf16[11264,512]{1,0:T(8,128)(2,1)} %subtract_convert_fusion, s32[128]{0:T(128)S(1)} %get-tuple-element.173, bf16[128,512]{1,0:T(8,128)(2,1)S(1)} %copy.36), kind=kCustom, calls=%fused_computation.4 | custom fusion | bytes 393728 | tf_op jit(solution)/shard_map/scatter | solution.py:127
  (95 shorter events, 91.5 us)
Async XLA Ops:
  6.5 1150.3 %copy-start = (bf16[128,128]{1,0:T(8,128)(2,1)S(1)}, bf16[128,128]{1,0:T(8,128)(2,1)}, u32[]{:S(2)}) copy-start(bf16[128,128]{1,0:T(8,128)(2,1)} %param.21) | copy-start | bytes 98308
  11.8 221.4 %all-to-all-start = ((s32[128,2,128]{2,1,0:T(2,128)}), s32[128,2,128]{2,1,0:T(2,128)S(1)}, u32[]{:S(2)}, u32[]{:S(2)}) async-start(s32[128,2,128]{2,1,0:T(2,128)} %copy.31), calls=%async_computation | async-start | bytes 262144 | tf_op jit(solution)/shard_map/all_to_all | solution.py:81
  24.7 11.6 copy-start.2
  50.4 16.7 %copy-start.4 = (s32[2,48]{1,0:T(2,128)S(1)}, s32[2,48]{1,0:T(2,128)}, u32[]{:S(2)}) copy-start(s32[2,48]{1,0:T(2,128)} %param.17) | copy-start | bytes 1156
  233.2 10.5 copy-start.3
  233.2 492.2 %all-to-all-start.1 = ((bf16[128,256,512]{2,1,0:T(8,128)(2,1)}), bf16[128,256,512]{2,1,0:T(8,128)(2,1)}, u32[]{:S(2)}, u32[]{:S(2)}) async-start(bf16[128,256,512]{2,1,0:T(8,128)(2,1)} %reshape_reshape.3), calls=%async_computation.1 | async-start | bytes 67108864 | tf_op jit(solution)/shard_map/all_to_all | solution.py:74
  243.4 814.4 %all-reduce.5.cloned.1.call-start = ((), (), s32[]{:S(2)}) async-start(), calls=%async_computation.3 | async-start | bytes 262144 | tf_op jit(solution)/shard_map/psum | solution.py:114
  930.9 127.0 %copy-start.1 = (bf16[128,128]{1,0:T(8,128)(2,1)S(1)}, bf16[128,128]{1,0:T(8,128)(2,1)}, u32[]{:S(2)}) copy-start(bf16[128,128]{1,0:T(8,128)(2,1)} %param.20) | copy-start | bytes 98308
  950.7 206.2 %all-reduce.3.cloned.1.call-start = ((), (), s32[]{:S(2)}) async-start(), calls=%async_computation.2 | async-start | bytes 5767168 | tf_op jit(solution)/shard_map/psum | solution.py:12
Sparse Core Ops, SparseCore 0:
  950.8 106.9 all-reduce.4
  1061.6 95.2 all-reduce.2
where the time goes:
time: 1200 us; the launch traced here: 1190 us
  waiting for transfers between devices  683 us (57%)
  local copies, waits for them, and re-layouts  227 us (19%)
  other arithmetic  165 us (14%)
  matrix products  81.4 us (7%)
  starting transfers between devices  22.2 us (2%)
  between operations  13.6 us (1%)
    all_to_all x1, waiting for transfers between devices, on_device(): lax.all_to_all(outgoing.reshape(row_groups * col_groups, capacity * tile_...  482 us
    scatter-add x8, other arithmetic, collect(): return running_sum.at[where_tile].add(placed, mode='drop')  138 us
    scatter x2, local copies, waits for them, and re-layouts, on_device(): outgoing = outgoing.at[owners[:, None], target_device[None, :], slot_rank...  106 us
    psum x1, waiting for transfers between devices, on_device(): pivot_block = lax.psum(picked.astype(jnp.bfloat16), 'prow')  103 us
    psum x1, waiting for transfers between devices, from_root(): return lax.psum(kept, axis)  97.8 us
    dot_general x8, matrix products, collect(): jnp.einsum('sic,sir->src', source_piece, one_hot_rows(piece_marks % tile_...  54.8 us
    another operation x1, local copies, waits for them, and re-layouts, on_device(): outgoing.reshape(row_groups * col_groups, capacity * tile_size, local_cols)  48.5 us
  transfers between devices with their start and end apart: 4, of which 3 were waited for; matrix products, arithmetic and copies ran while one was open for 18% of the time, Pallas kernels for 0%

commit v1 on v0

v1 whole, which is shorter than its diff:
```python
import functools

import jax
import jax.numpy as jnp
from jax import lax
from jax.experimental import pallas as pl
from jax.experimental.pallas import tpu as pltpu
from jax.sharding import PartitionSpec as P

TILE = 128
FRONT = 90112
SLAB = 8192
N_PROW = 8
N_PCOL = 16
N_DEV = N_PROW * N_PCOL
FRONT_TILES = FRONT // TILE // N_PROW
LOCAL_ROWS = FRONT_TILES * TILE
SLOTS = SLAB // TILE // N_PCOL
OWN_TILES = 8
RANKS = 2
CHUNKS = ((0, 1), (1, 1), (2, 2))
GROUP = 8
ROW_BLOCK = 704
MIB = 1 << 20


def one_hot_t(index_row):
    slot = lax.broadcasted_iota(jnp.int32, (TILE, TILE), 0)
    return jnp.where(slot == index_row, 1.0, 0.0).astype(jnp.bfloat16)


def pack_kernel(first, src, present, owner, rank, x_ref, cw_ref, rw_ref, out_ref, perm):
    group, slot = pl.program_id(0), pl.program_id(1)

    @pl.when((group == 0) & (slot == 0))
    def _():
        for t in range(OWN_TILES):
            perm[t] = one_hot_t(rw_ref[t : t + 1, :])

    here = present[group * SLOTS + first + slot]

    @pl.when(here == 0)
    def _():
        out_ref[...] = jnp.zeros_like(out_ref)

    @pl.when(here != 0)
    def _():
        moved = lax.dot_general(
            x_ref[...],
            one_hot_t(cw_ref[0]),
            (((1,), (1,)), ((), ())),
            preferred_element_type=jnp.float32,
        ).astype(jnp.bfloat16)
        for t in range(OWN_TILES):
            tile = jnp.dot(
                perm[t], moved[t * TILE : (t + 1) * TILE], preferred_element_type=jnp.float32
            )
            out_ref[owner[t], 0, rank[t], 0] = tile.astype(jnp.bfloat16)


def pack(first, width, src, present, owner, rank, children, col_within, row_within):
    def source(q, s, src, present, owner, rank):
        return src[q * SLOTS + first + s]

    return pl.pallas_call(
        functools.partial(pack_kernel, first),
        out_shape=jax.ShapeDtypeStruct(
            (N_PROW, N_PCOL, RANKS, width, TILE, TILE), jnp.bfloat16
        ),
        grid_spec=pltpu.PrefetchScalarGridSpec(
            num_scalar_prefetch=4,
            grid=(N_PCOL, width),
            in_specs=[
                pl.BlockSpec((OWN_TILES * TILE, TILE), lambda *a: (0, source(*a))),
                pl.BlockSpec((1, 1, TILE), lambda *a: (source(*a), 0, 0)),
                pl.BlockSpec((OWN_TILES, TILE), lambda *a: (0, 0)),
            ],
            out_specs=pl.BlockSpec(
                (N_PROW, 1, RANKS, 1, TILE, TILE), lambda q, s, *a: (0, q, 0, s, 0, 0)
            ),
            scratch_shapes=[pltpu.VMEM((OWN_TILES, TILE, TILE), jnp.bfloat16)],
        ),
        compiler_params=pltpu.CompilerParams(vmem_limit_bytes=24 * MIB),
        cost_estimate=pl.CostEstimate(
            flops=4 * N_PCOL * width * OWN_TILES * TILE**3,
            bytes_accessed=3 * N_PCOL * width * OWN_TILES * TILE * TILE * 2,
            transcendentals=0,
        ),
    )(src, present, owner, rank, children, col_within, row_within)


def accumulate_kernel(width, bins, pivots, x_ref, front_ref, pivot_ref, acc, picked):
    step = pl.program_id(0)
    cols = width * TILE

    @pl.when(step == 0)
    def _():
        @pl.loop(0, FRONT_TILES)
        def _(i):
            acc[pl.ds(pl.multiple_of(i * TILE, TILE), TILE), :] = jnp.zeros(
                (TILE, cols), jnp.float32
            )

    @pl.loop(0, GROUP)
    def _(g):
        for r in range(RANKS):
            place = bins[(step * GROUP + g) * RANKS + r]

            @pl.when(place >= 0)
            def _():
                rows = pl.ds(pl.multiple_of(place * TILE, TILE), TILE)
                for c in range(width):
                    acc[rows, c * TILE : (c + 1) * TILE] += x_ref[g, r, c].astype(
                        jnp.float32
                    )

    @pl.when(step == pl.num_programs(0) - 1)
    def _():
        @pl.loop(0, FRONT_TILES)
        def _(i):
            rows = pl.ds(pl.multiple_of(i * TILE, TILE), TILE)
            front_ref[rows, :] = acc[rows, :].astype(jnp.bfloat16)

        @pl.loop(0, TILE)
        def _(j):
            row = pivots[j]
            mine = (row >= 0).astype(jnp.float32)
            value = acc[pl.ds(jnp.maximum(row, 0), 1), :]
            picked[pl.ds(j, 1), :] = value * mine

        pivot_ref[...] = picked[...].astype(jnp.bfloat16)


def accumulate(width, bins, pivots, arrived):
    cols = width * TILE
    return pl.pallas_call(
        functools.partial(accumulate_kernel, width),
        out_shape=[
            jax.ShapeDtypeStruct((LOCAL_ROWS, cols), jnp.bfloat16),
            jax.ShapeDtypeStruct((TILE, cols), jnp.bfloat16),
        ],
        grid_spec=pltpu.PrefetchScalarGridSpec(
            num_scalar_prefetch=2,
            grid=(N_DEV // GROUP,),
            in_specs=[
                pl.BlockSpec((GROUP, RANKS, width, TILE, TILE), lambda i, *a: (i, 0, 0, 0, 0))
            ],
            out_specs=[
                pl.BlockSpec((LOCAL_ROWS, cols), lambda i, *a: (0, 0)),
                pl.BlockSpec((TILE, cols), lambda i, *a: (0, 0)),
            ],
            scratch_shapes=[
                pltpu.VMEM((LOCAL_ROWS, cols), jnp.float32),
                pltpu.VMEM((TILE, cols), jnp.float32),
            ],
        ),
        compiler_params=pltpu.CompilerParams(vmem_limit_bytes=48 * MIB),
        cost_estimate=pl.CostEstimate(
            flops=N_DEV * RANKS * TILE * cols,
            bytes_accessed=(N_DEV * RANKS * TILE + LOCAL_ROWS) * cols * 2,
            transcendentals=0,
        ),
    )(bins, pivots, arrived)


def update_kernel(n_chunks, is_first, *refs):
    fronts, (panel_ref, pivot_ref, row_ref, linv_ref, uinv_ref, out_ref, upper) = (
        refs[:n_chunks],
        refs[n_chunks:],
    )
    step = pl.program_id(0)

    @pl.when(step == 0)
    def _():
        block = pivot_ref[0].astype(jnp.float32)
        for p in range(1, N_PROW):
            block = block + pivot_ref[p].astype(jnp.float32)
        upper[...] = jnp.dot(
            linv_ref[...], block.astype(jnp.bfloat16), preferred_element_type=jnp.float32
        ).astype(jnp.bfloat16)

    lower = (
        jnp.dot(panel_ref[...], uinv_ref[...], preferred_element_type=jnp.float32)
        .astype(jnp.bfloat16)
        .astype(jnp.float32)
    )
    rows = lax.broadcasted_iota(jnp.int32, (ROW_BLOCK, TILE), 0) + step * ROW_BLOCK
    chosen = jnp.where(rows == row_ref[...], 1.0, 0.0)
    replaced = jnp.max(chosen, axis=1, keepdims=True)
    kept = 1.0 - replaced
    factor = jnp.where(replaced > 0.0, chosen, -lower).astype(jnp.bfloat16)
    at = 0
    for k in range(n_chunks):
        cols = fronts[k].shape[1]
        product = jnp.dot(
            factor, upper[:, at : at + cols], preferred_element_type=jnp.float32
        )
        result = jnp.where(replaced > 0.0, product, fronts[k][...].astype(jnp.float32) + product)
        out_ref[:, at : at + cols] = result.astype(jnp.bfloat16)
        at += cols

    @pl.when(is_first[0] != 0)
    def _():
        out_ref[:, 0:TILE] = lower.astype(jnp.bfloat16)


def update(is_first, fronts, panel, pivots, rows, linv, uinv):
    cols = SLOTS * TILE
    whole = lambda *shape: pl.BlockSpec(shape, lambda i, *a: (0,) * len(shape))
    return pl.pallas_call(
        functools.partial(update_kernel, len(fronts)),
        out_shape=jax.ShapeDtypeStruct((LOCAL_ROWS, cols), jnp.bfloat16),
        grid_spec=pltpu.PrefetchScalarGridSpec(
            num_scalar_prefetch=1,
            grid=(LOCAL_ROWS // ROW_BLOCK,),
            in_specs=[
                pl.BlockSpec((ROW_BLOCK, f.shape[1]), lambda i, *a: (i, 0)) for f in fronts
            ]
            + [
                pl.BlockSpec((ROW_BLOCK, TILE), lambda i, *a: (i, 0)),
                whole(N_PROW, TILE, cols),
                whole(1, TILE),
                whole(TILE, TILE),
                whole(TILE, TILE),
            ],
            out_specs=pl.BlockSpec((ROW_BLOCK, cols), lambda i, *a: (i, 0)),
            scratch_shapes=[pltpu.VMEM((TILE, cols), jnp.bfloat16)],
        ),
        compiler_params=pltpu.CompilerParams(vmem_limit_bytes=32 * MIB),
        cost_estimate=pl.CostEstimate(
            flops=2 * LOCAL_ROWS * TILE * (cols + TILE),
            bytes_accessed=2 * LOCAL_ROWS * cols * 2,
            transcendentals=0,
        ),
    )(is_first, *fronts, panel, pivots, rows, linv, uinv)


def spread_panel(panel, my_pcol):
    pieces = panel.reshape(N_PCOL, LOCAL_ROWS // N_PCOL, TILE)
    piece = pieces[0]
    for q in range(1, N_PCOL):
        got = lax.ppermute(pieces[q], "pcol", [(0, q)])
        piece = jnp.where(my_pcol == q, got, piece)
    whole = jnp.zeros_like(pieces)
    whole = lax.dynamic_update_index_in_dim(whole, piece, my_pcol, 0)
    for i in range(1, N_PCOL):
        got = lax.ppermute(piece, "pcol", [(q, q ^ i) for q in range(N_PCOL)])
        whole = lax.dynamic_update_index_in_dim(whole, got, my_pcol ^ i, 0)
    return whole.reshape(LOCAL_ROWS, TILE)


def on_device(
    children,
    row_owner,
    row_local,
    row_within,
    column_tile,
    column_within,
    pivot_rows,
    lower_inverse,
    upper_inverse,
):
    my_prow = lax.axis_index("prow")
    my_pcol = lax.axis_index("pcol")
    child = my_prow // (N_PROW // 2)
    col_tile = jnp.take(column_tile, child, axis=0)
    col_within = jnp.take(column_within, child, axis=0)
    n_src = col_tile.shape[0]
    hits = (col_tile[:, None] == jnp.arange(SLAB // TILE, dtype=jnp.int32)[None, :]).astype(
        jnp.int32
    )
    src = jnp.sum(hits * jnp.arange(n_src, dtype=jnp.int32)[:, None], axis=0)
    present = jnp.sum(hits, axis=0)
    order = jnp.arange(OWN_TILES, dtype=jnp.int32)
    earlier = order[None, :] < order[:, None]
    owners = row_owner[:, 0]
    rank = jnp.sum(((owners[:, None] == owners[None, :]) & earlier).astype(jnp.int32), axis=1)

    codes = jnp.pad(
        (owners * FRONT_TILES + row_local)[None, :], ((0, 0), (0, TILE - OWN_TILES))
    )
    codes = lax.all_to_all(
        jnp.broadcast_to(codes[None], (N_DEV, 8, TILE)),
        ("prow", "pcol"),
        split_axis=0,
        concat_axis=0,
        tiled=True,
    )[:, 0, :OWN_TILES]
    mine = codes // FRONT_TILES == my_prow
    nth = jnp.sum((mine[:, None, :] & earlier[None]).astype(jnp.int32), axis=2)
    want = jnp.arange(RANKS, dtype=jnp.int32)[None, :, None]
    is_it = mine[:, None, :] & (nth[:, None, :] == want)
    bins = jnp.max(
        jnp.where(is_it, (codes % FRONT_TILES)[:, None, :], -1), axis=2
    ).reshape(-1)

    pivot_local = jnp.where(
        pivot_rows // LOCAL_ROWS == my_prow, pivot_rows % LOCAL_ROWS, -1
    ).astype(jnp.int32)

    fronts, picks = [], []
    panel = None
    for first, width in CHUNKS:
        sent = pack(
            first,
            width,
            src,
            present,
            owners,
            rank,
            children,
            col_within.reshape(n_src, 1, TILE),
            row_within,
        )
        arrived = lax.all_to_all(
            sent.reshape(N_DEV, RANKS, width, TILE, TILE),
            ("prow", "pcol"),
            split_axis=0,
            concat_axis=0,
            tiled=True,
        )
        front, picked = accumulate(width, bins, pivot_local, arrived)
        fronts.append(front)
        picks.append(picked)
        if first == 0:
            panel = spread_panel(front[:, :TILE], my_pcol)
    picked = jnp.concatenate(picks, axis=1)
    pivots = lax.all_to_all(
        jnp.broadcast_to(picked[None], (N_PROW,) + picked.shape),
        "prow",
        split_axis=0,
        concat_axis=0,
        tiled=True,
    )
    return update(
        (my_pcol == 0).astype(jnp.int32).reshape(1),
        fronts,
        panel,
        pivots,
        pivot_local.reshape(1, TILE),
        lower_inverse,
        upper_inverse,
    )


def solution(mesh):
    placed = (
        P(("prow", "pcol"), None),
        P(("prow", "pcol"), None),
        P(("prow", "pcol")),
        P(("prow", "pcol"), None),
        P(),
        P(),
        P(),
        P(),
        P(),
    )
    return jax.shard_map(
        on_device, mesh=mesh, in_specs=placed, out_specs=P("prow", "pcol"), check_vma=False
    )
```

time: 1200 us -> 637 us (0.53)
  waiting for transfers between devices: 683 us -> 375 us
  local copies, waits for them, and re-layouts: 227 us -> 44.4 us
  other arithmetic: 165 us -> 5.39 us
  starting transfers between devices: 22.2 us -> 123 us
  Pallas kernels: 0 us -> 88.3 us
  matrix products: 81.4 us -> 0 us
  between operations: 13.6 us -> 0.57 us
    all_to_all x2 -> x5, waiting for transfers between devices: 482 us -> 182 us  [the longest x3 169 us: on_device(): lax.all_to_all(sent.reshape(N_DEV, RANKS, width, TILE, TILE), ('prow', 'p...]
    psum x2 -> x0, waiting for transfers between devices: 201 us -> none  [the longest x1 103 us: on_device(): pivot_block = lax.psum(picked.astype(jnp.bfloat16), 'prow')]
    ppermute x0 -> x30, waiting for transfers between devices: none -> 193 us  [the longest x15 191 us: spread_panel(): got = lax.ppermute(pieces[q], 'pcol', [(0, q)])]
    scatter-add x8 -> x0, other arithmetic: 138 us -> none  [collect(): return running_sum.at[where_tile].add(placed, mode='drop')]
    scatter x5 -> x0, local copies, waits for them, and re-layouts: 119 us -> none  [the longest x2 106 us: on_device(): outgoing = outgoing.at[owners[:, None], target_device[None, :], slot_rank...]
    pallas_call x0 -> x7, Pallas kernels: none -> 88.3 us  [the longest x3 42.7 us: accumulate(): pl.pallas_call(functools.partial(accumulate_kernel, width), out_shape=[ja...]
    dot_general x12 -> x0, matrix products: 81.4 us -> none  [the longest x8 54.8 us: collect(): jnp.einsum('sic,sir->src', source_piece, one_hot_rows(piece_marks % tile_...]
    ppermute x0 -> x30, starting transfers between devices: none -> 64.2 us  [the longest x15 33.3 us: spread_panel(): got = lax.ppermute(piece, 'pcol', [(q, q ^ i) for q in range(N_PCOL)])]
  transfers between devices with their start and end apart: 4 -> 35, of which waited for: 3 -> 14; matrix products, arithmetic and copies ran while one was open for 18% -> 1% of each run, Pallas kernels for 0% -> 12%
where the time goes in v1:
time: 637 us; the launch traced here: 636 us
  waiting for transfers between devices  375 us (59%)
  starting transfers between devices  123 us (19%)
  Pallas kernels  88.3 us (14%)
  local copies, waits for them, and re-layouts  44.4 us (7%)
    ppermute x15, waiting for transfers between devices, spread_panel(): got = lax.ppermute(pieces[q], 'pcol', [(0, q)])  191 us
    all_to_all x3, waiting for transfers between devices, on_device(): lax.all_to_all(sent.reshape(N_DEV, RANKS, width, TILE, TILE), ('prow', 'p...  169 us
    pallas_call x3, Pallas kernels, accumulate(): pl.pallas_call(functools.partial(accumulate_kernel, width), out_shape=[ja...  42.7 us
    unnamed x55, local copies, waits for them, and re-layouts  39.2 us
    all_to_all x3, starting transfers between devices, on_device(): lax.all_to_all(sent.reshape(N_DEV, RANKS, width, TILE, TILE), ('prow', 'p...  34.1 us
    ppermute x15, starting transfers between devices, spread_panel(): got = lax.ppermute(piece, 'pcol', [(q, q ^ i) for q in range(N_PCOL)])  33.3 us
    pallas_call x3, Pallas kernels, pack(): pl.pallas_call(functools.partial(pack_kernel, first), out_shape=jax.Shape...  32.1 us
    ppermute x15, starting transfers between devices, spread_panel(): got = lax.ppermute(pieces[q], 'pcol', [(0, q)])  30.9 us
  transfers between devices with their start and end apart: 35, of which 14 were waited for; matrix products, arithmetic and copies ran while one was open for 1% of the time, Pallas kernels for 12%

profile of v1, /device:TPU:1, one launch (start us, length us, event | category | flops | bytes accessed | tf_op | source)
XLA Modules:
  0.0 635.8 jit_solution(4101452813913560296)
XLA Ops:
  1.5 11.5 %all-to-all-start = ((s32[128,8,128]{2,1,0:T(8,128)}), s32[128,8,128]{2,1,0:T(8,128)S(1)}, u32[]{:S(2)}, u32[]{:S(2)}) async-start(s32[128,8,128]{2,1,0:T(8,128)} %broadcast_in_dim.120), calls=%async_computation | async-start | bytes 1048576 | tf_op jit(solution)/shard_map/all_to_all | solution.py:282
  15.5 4.6 copy-done
  21.4 8.5 %shard_map.91 = bf16[8,16,2,1,128,128]{5,4,3,2,1,0:T(8,128)(2,1)S(1)} custom-call(s32[64]{0:T(128)S(1)} %get-tuple-element.40.src, s32[64]{0:T(128)S(1)} %get-tuple-element.39.present, s32[8]{0:T(128)S(1)} %bitcast.60, s32[8]{0:T(128)S(1)} %convert_reduce_fusion.2.rank, bf16[1024,6144]{1,0:T(8,128)(2,1)S(1)} %copy-done, s32[48,1,128]{2,1,0:T(1,128)S(1)} %bitcast.56, ...), custom_call_target="tpu_custom_call" | custom-call | flops 1073741824 | bytes 12582912 | tf_op jit(solution)/shard_map/pallas_call | solution.py:65
  33.4 10.2 %all-to-all-start.1 = ((bf16[128,2,1,128,128]{4,3,2,1,0:T(8,128)(2,1)}), bf16[128,2,1,128,128]{4,3,2,1,0:T(8,128)(2,1)}, u32[]{:S(2)}, u32[]{:S(2)}) async-start(bf16[128,2,1,128,128]{4,3,2,1,0:T(8,128)(2,1)} %bitcast.54), calls=%async_computation.1 | async-start | bytes 16777216 | tf_op jit(solution)/shard_map/all_to_all | solution.py:315
  43.6 4.6 copy-done.1
  48.2 7.8 %shard_map.93 = bf16[8,16,2,1,128,128]{5,4,3,2,1,0:T(8,128)(2,1)S(1)} custom-call(s32[64]{0:T(128)S(1)} %get-tuple-element.40.src, s32[64]{0:T(128)S(1)} %get-tuple-element.39.present, s32[8]{0:T(128)S(1)} %bitcast.61, s32[8]{0:T(128)S(1)} %convert_reduce_fusion.2.rank, bf16[1024,6144]{1,0:T(8,128)(2,1)S(1)} %copy-done.1, s32[48,1,128]{2,1,0:T(1,128)S(1)} %bitcast.57, ...), custom_call_target="tpu_custom_call" | custom-call | flops 1073741824 | bytes 12582912 | tf_op jit(solution)/shard_map/pallas_call | solution.py:65
  59.3 89.5 %all-to-all-done.1.x_ref = bf16[128,2,1,128,128]{4,3,2,1,0:T(8,128)(2,1)} async-done(((bf16[128,2,1,128,128]{4,3,2,1,0:T(8,128)(2,1)}), bf16[128,2,1,128,128]{4,3,2,1,0:T(8,128)(2,1)}, u32[]{:S(2)}, u32[]{:S(2)}) %all-to-all-start.1) | async-done | bytes 8388640 | tf_op jit(solution)/shard_map/all_to_all | solution.py:315
  148.8 11.9 %all-to-all-start.2 = ((bf16[128,2,1,128,128]{4,3,2,1,0:T(8,128)(2,1)}), bf16[128,2,1,128,128]{4,3,2,1,0:T(8,128)(2,1)}, u32[]{:S(2)}, u32[]{:S(2)}) async-start(bf16[128,2,1,128,128]{4,3,2,1,0:T(8,128)(2,1)} %bitcast.53), calls=%async_computation.2 | async-start | bytes 16777216 | tf_op jit(solution)/shard_map/all_to_all | solution.py:315
  160.7 4.6 copy-done.2
  165.3 15.7 %shard_map.95 = bf16[8,16,2,2,128,128]{5,4,3,2,1,0:T(8,128)(2,1)S(1)} custom-call(s32[64]{0:T(128)S(1)} %get-tuple-element.40.src, s32[64]{0:T(128)S(1)} %get-tuple-element.39.present, s32[8]{0:T(128)S(1)} %bitcast.62, s32[8]{0:T(128)S(1)} %convert_reduce_fusion.2.rank, bf16[1024,6144]{1,0:T(8,128)(2,1)S(1)} %copy-done.2, s32[48,1,128]{2,1,0:T(1,128)S(1)} %bitcast.58, ...), custom_call_target="tpu_custom_call" | custom-call | flops 2147483648 | bytes 25165824 | tf_op jit(solution)/shard_map/pallas_call | solution.py:65
  181.1 5.8 copy-done.3
  186.8 79.1 %all-to-all-done.2.x_ref = bf16[128,2,1,128,128]{4,3,2,1,0:T(8,128)(2,1)} async-done(((bf16[128,2,1,128,128]{4,3,2,1,0:T(8,128)(2,1)}), bf16[128,2,1,128,128]{4,3,2,1,0:T(8,128)(2,1)}, u32[]{:S(2)}, u32[]{:S(2)}) %all-to-all-start.2) | async-done | bytes 8388640 | tf_op jit(solution)/shard_map/all_to_all | solution.py:315
  265.9 11.9 %all-to-all-start.3 = ((bf16[128,2,2,128,128]{4,3,2,1,0:T(8,128)(2,1)}), bf16[128,2,2,128,128]{4,3,2,1,0:T(8,128)(2,1)}, u32[]{:S(2)}, u32[]{:S(2)}) async-start(bf16[128,2,2,128,128]{4,3,2,1,0:T(8,128)(2,1)} %bitcast.52), calls=%async_computation.3 | async-start | bytes 33554432 | tf_op jit(solution)/shard_map/all_to_all | solution.py:315
  278.4 13.1 %shard_map.92 = (bf16[11264,128]{1,0:T(8,128)(2,1)S(1)}, bf16[128,128]{1,0:T(8,128)(2,1)S(1)}) custom-call(s32[256]{0:T(256)S(1)} %reshape.91.bins, s32[128]{0:T(128)S(1)} %compare_select_fusion.pivots, bf16[128,2,1,128,128]{4,3,2,1,0:T(8,128)(2,1)} %all-to-all-done.1.x_ref), custom_call_target="tpu_custom_call" | custom-call | flops 4194304 | bytes 11272192 | tf_op jit(solution)/shard_map/pallas_call | solution.py:136
  293.3 7.5 %collective-permute-start = (bf16[704,128]{1,0:T(8,128)(2,1)S(1)}, bf16[704,128]{1,0:T(8,128)(2,1)S(1)}, u32[]{:S(2)}, u32[]{:S(2)}) collective-permute-start(bf16[704,128]{1,0:T(8,128)(2,1)S(1)} %get-tuple-element.57), channel_id=1, source_target_pairs={{0,15},{16,31},{32,47},{48,63},{64,79},{80,95},{96,111},{112,127}} | collective-permute-start | bytes 540680 | tf_op jit(solution)/shard_map/ppermute | solution.py:242
  307.3 113.1 %collective-permute-done = bf16[704,128]{1,0:T(8,128)(2,1)S(1)} collective-permute-done((bf16[704,128]{1,0:T(8,128)(2,1)S(1)}, bf16[704,128]{1,0:T(8,128)(2,1)S(1)}, u32[]{:S(2)}, u32[]{:S(2)}) %collective-permute-start) | collective-permute-done | bytes 180256 | tf_op jit(solution)/shard_map/ppermute | solution.py:242
  422.3 21.2 %collective-permute-done.1 = bf16[704,128]{1,0:T(8,128)(2,1)S(1)} collective-permute-done((bf16[704,128]{1,0:T(8,128)(2,1)S(1)}, bf16[704,128]{1,0:T(8,128)(2,1)S(1)}, u32[]{:S(2)}, u32[]{:S(2)}) %collective-permute-start.1) | collective-permute-done | bytes 180256 | tf_op jit(solution)/shard_map/ppermute | solution.py:242
  445.5 38.2 %collective-permute-done.10 = bf16[704,128]{1,0:T(8,128)(2,1)S(1)} collective-permute-done((bf16[704,128]{1,0:T(8,128)(2,1)S(1)}, bf16[704,128]{1,0:T(8,128)(2,1)S(1)}, u32[]{:S(2)}, u32[]{:S(2)}) %collective-permute-start.10) | collective-permute-done | bytes 180256 | tf_op jit(solution)/shard_map/ppermute | solution.py:242
  518.9 13.1 %shard_map.94 = (bf16[11264,128]{1,0:T(8,128)(2,1)S(1)}, bf16[128,128]{1,0:T(8,128)(2,1)S(1)}) custom-call(s32[256]{0:T(256)S(1)} %reshape.91.bins, s32[128]{0:T(128)S(1)} %compare_select_fusion.pivots, bf16[128,2,1,128,128]{4,3,2,1,0:T(8,128)(2,1)} %all-to-all-done.2.x_ref), custom_call_target="tpu_custom_call" | custom-call | flops 4194304 | bytes 11272192 | tf_op jit(solution)/shard_map/pallas_call | solution.py:136
  558.2 6.0 collective-permute-start.28
  568.0 16.4 %shard_map.96 = (bf16[11264,256]{1,0:T(8,128)(2,1)S(1)}, bf16[128,256]{1,0:T(8,128)(2,1)S(1)}) custom-call(s32[256]{0:T(256)S(1)} %reshape.91.bins, s32[128]{0:T(128)S(1)} %compare_select_fusion.pivots, bf16[128,2,2,128,128]{4,3,2,1,0:T(8,128)(2,1)} %all-to-all-done.3.x_ref), custom_call_target="tpu_custom_call" | custom-call | flops 8388608 | bytes 22544384 | tf_op jit(solution)/shard_map/pallas_call | solution.py:136
  588.0 12.7 %all-to-all-start.4 = ((bf16[8,128,512]{2,1,0:T(8,128)(2,1)}), bf16[8,128,512]{2,1,0:T(8,128)(2,1)}, u32[]{:S(2)}, u32[]{:S(2)}) async-start(bf16[8,128,512]{2,1,0:T(8,128)(2,1)} %broadcast_in_dim.146), calls=%async_computation.4 | async-start | bytes 2097152 | tf_op jit(solution)/shard_map/all_to_all | solution.py:328
  602.8 13.2 %all-to-all-done.4.refs_4_ = bf16[8,128,512]{2,1,0:T(8,128)(2,1)} async-done(((bf16[8,128,512]{2,1,0:T(8,128)(2,1)}), bf16[8,128,512]{2,1,0:T(8,128)(2,1)}, u32[]{:S(2)}, u32[]{:S(2)}) %all-to-all-start.4) | async-done | bytes 1048608 | tf_op jit(solution)/shard_map/all_to_all | solution.py:328
  622.2 13.6 %shard_map.97 = bf16[11264,512]{1,0:T(8,128)(2,1)} custom-call(s32[1]{0:T(128)} %bitcast.is_first, bf16[11264,128]{1,0:T(8,128)(2,1)S(1)} %copy-done.7, bf16[11264,128]{1,0:T(8,128)(2,1)S(1)} %copy-done.11, bf16[11264,256]{1,0:T(8,128)(2,1)S(1)} %copy-done.9, bf16[11264,128]{1,0:T(8,128)(2,1)S(1)} %bitcast.55, bf16[8,128,512]{2,1,0:T(8,128)(2,1)} %all-to-all-done.4.refs_4_, ...), custom_call_target="tpu_custom_call" | custom-call | flops 1845493760 | bytes 23068672 | tf_op jit(solution)/shard_map/pallas_call | solution.py:210
  (145 shorter events, 101.5 us)
Async XLA Ops:
  1.5 31.8 %all-to-all-start = ((s32[128,8,128]{2,1,0:T(8,128)}), s32[128,8,128]{2,1,0:T(8,128)S(1)}, u32[]{:S(2)}, u32[]{:S(2)}) async-start(s32[128,8,128]{2,1,0:T(8,128)} %broadcast_in_dim.120), calls=%async_computation | async-start | bytes 1048576 | tf_op jit(solution)/shard_map/all_to_all | solution.py:282
  33.4 115.4 %all-to-all-start.1 = ((bf16[128,2,1,128,128]{4,3,2,1,0:T(8,128)(2,1)}), bf16[128,2,1,128,128]{4,3,2,1,0:T(8,128)(2,1)}, u32[]{:S(2)}, u32[]{:S(2)}) async-start(bf16[128,2,1,128,128]{4,3,2,1,0:T(8,128)(2,1)} %bitcast.54), calls=%async_computation.1 | async-start | bytes 16777216 | tf_op jit(solution)/shard_map/all_to_all | solution.py:315
  148.8 117.1 %all-to-all-start.2 = ((bf16[128,2,1,128,128]{4,3,2,1,0:T(8,128)(2,1)}), bf16[128,2,1,128,128]{4,3,2,1,0:T(8,128)(2,1)}, u32[]{:S(2)}, u32[]{:S(2)}) async-start(bf16[128,2,1,128,128]{4,3,2,1,0:T(8,128)(2,1)} %bitcast.53), calls=%async_computation.2 | async-start | bytes 16777216 | tf_op jit(solution)/shard_map/all_to_all | solution.py:315
  265.9 302.1 %all-to-all-start.3 = ((bf16[128,2,2,128,128]{4,3,2,1,0:T(8,128)(2,1)}), bf16[128,2,2,128,128]{4,3,2,1,0:T(8,128)(2,1)}, u32[]{:S(2)}, u32[]{:S(2)}) async-start(bf16[128,2,2,128,128]{4,3,2,1,0:T(8,128)(2,1)} %bitcast.52), calls=%async_computation.3 | async-start | bytes 33554432 | tf_op jit(solution)/shard_map/all_to_all | solution.py:315
  293.3 127.1 %collective-permute-start = (bf16[704,128]{1,0:T(8,128)(2,1)S(1)}, bf16[704,128]{1,0:T(8,128)(2,1)S(1)}, u32[]{:S(2)}, u32[]{:S(2)}) collective-permute-start(bf16[704,128]{1,0:T(8,128)(2,1)S(1)} %get-tuple-element.57), channel_id=1, source_target_pairs={{0,15},{16,31},{32,47},{48,63},{64,79},{80,95},{96,111},{112,127}} | collective-permute-start | bytes 540680 | tf_op jit(solution)/shard_map/ppermute | solution.py:242
  300.8 142.8 %collective-permute-start.1 = (bf16[704,128]{1,0:T(8,128)(2,1)S(1)}, bf16[704,128]{1,0:T(8,128)(2,1)S(1)}, u32[]{:S(2)}, u32[]{:S(2)}) collective-permute-start(bf16[704,128]{1,0:T(8,128)(2,1)S(1)} %get-tuple-element.56), channel_id=1, source_target_pairs={{0,14},{16,30},{32,46},{48,62},{64,78},{80,94},{96,110},{112,126}} | collective-permute-start | bytes 540680 | tf_op jit(solution)/shard_map/ppermute | solution.py:242
  302.1 181.6 %collective-permute-start.10 = (bf16[704,128]{1,0:T(8,128)(2,1)S(1)}, bf16[704,128]{1,0:T(8,128)(2,1)S(1)}, u32[]{:S(2)}, u32[]{:S(2)}) collective-permute-start(bf16[704,128]{1,0:T(8,128)(2,1)S(1)} %get-tuple-element.47), channel_id=1, source_target_pairs={{0,5},{16,21},{32,37},{48,53},{64,69},{80,85},{96,101},{112,117}} | collective-permute-start | bytes 540680 | tf_op jit(solution)/shard_map/ppermute | solution.py:242
  303.4 186.5 %collective-permute-start.11 = (bf16[704,128]{1,0:T(8,128)(2,1)S(1)}, bf16[704,128]{1,0:T(8,128)(2,1)}, u32[]{:S(2)}, u32[]{:S(2)}) collective-permute-start(bf16[704,128]{1,0:T(8,128)(2,1)S(1)} %get-tuple-element.46), channel_id=1, source_target_pairs={{0,4},{16,20},{32,36},{48,52},{64,68},{80,84},{96,100},{112,116}} | collective-permute-start | bytes 540680 | tf_op jit(solution)/shard_map/ppermute | solution.py:242
  305.3 186.5 %collective-permute-start.12 = (bf16[704,128]{1,0:T(8,128)(2,1)S(1)}, bf16[704,128]{1,0:T(8,128)(2,1)}, u32[]{:S(2)}, u32[]{:S(2)}) collective-permute-start(bf16[704,128]{1,0:T(8,128)(2,1)S(1)} %get-tuple-element.45), channel_id=1, source_target_pairs={{0,3},{16,19},{32,35},{48,51},{64,67},{80,83},{96,99},{112,115}} | collective-permute-start | bytes 540680 | tf_op jit(solution)/shard_map/ppermute | solution.py:242
  420.4 73.4 %collective-permute-start.13 = (bf16[704,128]{1,0:T(8,128)(2,1)S(1)}, bf16[704,128]{1,0:T(8,128)(2,1)}, u32[]{:S(2)}, u32[]{:S(2)}) collective-permute-start(bf16[704,128]{1,0:T(8,128)(2,1)S(1)} %get-tuple-element.44), channel_id=1, source_target_pairs={{0,2},{16,18},{32,34},{48,50},{64,66},{80,82},{96,98},{112,114}} | collective-permute-start | bytes 540680 | tf_op jit(solution)/shard_map/ppermute | solution.py:242
  443.5 51.5 %collective-permute-start.14 = (bf16[704,128]{1,0:T(8,128)(2,1)S(1)}, bf16[704,128]{1,0:T(8,128)(2,1)}, u32[]{:S(2)}, u32[]{:S(2)}) collective-permute-start(bf16[704,128]{1,0:T(8,128)(2,1)S(1)} %get-tuple-element.43), channel_id=1, source_target_pairs={{0,1},{16,17},{32,33},{48,49},{64,65},{80,81},{96,97},{112,113}} | collective-permute-start | bytes 540680 | tf_op jit(solution)/shard_map/ppermute | solution.py:242
  483.7 12.7 %collective-permute-start.2 = (bf16[704,128]{1,0:T(8,128)(2,1)S(1)}, bf16[704,128]{1,0:T(8,128)(2,1)}, u32[]{:S(2)}, u32[]{:S(2)}) collective-permute-start(bf16[704,128]{1,0:T(8,128)(2,1)S(1)} %get-tuple-element.55), channel_id=1, source_target_pairs={{0,13},{16,29},{32,45},{48,61},{64,77},{80,93},{96,109},{112,125}} | collective-permute-start | bytes 540680 | tf_op jit(solution)/shard_map/ppermute | solution.py:242
  497.7 14.0 %collective-permute-start.8 = (bf16[704,128]{1,0:T(8,128)(2,1)S(1)}, bf16[704,128]{1,0:T(8,128)(2,1)S(1)}, u32[]{:S(2)}, u32[]{:S(2)}) collective-permute-start(bf16[704,128]{1,0:T(8,128)(2,1)S(1)} %get-tuple-element.49), channel_id=1, source_target_pairs={{0,7},{16,23},{32,39},{48,55},{64,71},{80,87},{96,103},{112,119}} | collective-permute-start | bytes 540680 | tf_op jit(solution)/shard_map/ppermute | solution.py:242
  499.0 16.6 %collective-permute-start.9 = (bf16[704,128]{1,0:T(8,128)(2,1)S(1)}, bf16[704,128]{1,0:T(8,128)(2,1)}, u32[]{:S(2)}, u32[]{:S(2)}) collective-permute-start(bf16[704,128]{1,0:T(8,128)(2,1)S(1)} %get-tuple-element.48), channel_id=1, source_target_pairs={{0,6},{16,22},{32,38},{48,54},{64,70},{80,86},{96,102},{112,118}} | collective-permute-start | bytes 540680 | tf_op jit(solution)/shard_map/ppermute | solution.py:242
  518.9 18.9 %collective-permute-start.15 = (bf16[704,128]{1,0:T(8,128)(2,1)}, bf16[704,128]{1,0:T(8,128)(2,1)S(1)}, u32[]{:S(2)}, u32[]{:S(2)}) collective-permute-start(bf16[704,128]{1,0:T(8,128)(2,1)} %get-tuple-element.42), channel_id=1, source_target_pairs={{0,1},{1,0},{2,3},{3,2},{4,5},{5,4},{6,7},{7,6},{8,9},{9,8},{10,11... | collective-permute-start | bytes 540680 | tf_op jit(solution)/shard_map/ppermute | solution.py:247
  537.8 12.1 %collective-permute-start.20 = (bf16[704,128]{1,0:T(8,128)(2,1)}, bf16[704,128]{1,0:T(8,128)(2,1)S(1)}, u32[]{:S(2)}, u32[]{:S(2)}) collective-permute-start(bf16[704,128]{1,0:T(8,128)(2,1)} %get-tuple-element.42), channel_id=1, source_target_pairs={{0,6},{1,7},{2,4},{3,5},{4,2},{5,3},{6,0},{7,1},{8,14},{9,15},{10,... | collective-permute-start | bytes 540680 | tf_op jit(solution)/shard_map/ppermute | solution.py:247
  543.5 14.7 %collective-permute-start.23 = (bf16[704,128]{1,0:T(8,128)(2,1)}, bf16[704,128]{1,0:T(8,128)(2,1)S(1)}, u32[]{:S(2)}, u32[]{:S(2)}) collective-permute-start(bf16[704,128]{1,0:T(8,128)(2,1)} %get-tuple-element.42), channel_id=1, source_target_pairs={{0,9},{1,8},{2,11},{3,10},{4,13},{5,12},{6,15},{7,14},{8,1},{9,0},... | collective-permute-start | bytes 540680 | tf_op jit(solution)/shard_map/ppermute | solution.py:247
  545.7 18.5 %collective-permute-start.24 = (bf16[704,128]{1,0:T(8,128)(2,1)}, bf16[704,128]{1,0:T(8,128)(2,1)S(1)}, u32[]{:S(2)}, u32[]{:S(2)}) collective-permute-start(bf16[704,128]{1,0:T(8,128)(2,1)} %get-tuple-element.42), channel_id=1, source_target_pairs={{0,10},{1,11},{2,8},{3,9},{4,14},{5,15},{6,12},{7,13},{8,2},{9,3},... | collective-permute-start | bytes 540680 | tf_op jit(solution)/shard_map/ppermute | solution.py:247
  549.8 18.1 %collective-permute-start.25 = (bf16[704,128]{1,0:T(8,128)(2,1)}, bf16[704,128]{1,0:T(8,128)(2,1)S(1)}, u32[]{:S(2)}, u32[]{:S(2)}) collective-permute-start(bf16[704,128]{1,0:T(8,128)(2,1)} %get-tuple-element.42), channel_id=1, source_target_pairs={{0,11},{1,10},{2,9},{3,8},{4,15},{5,14},{6,13},{7,12},{8,3},{9,2},... | collective-permute-start | bytes 540680 | tf_op jit(solution)/shard_map/ppermute | solution.py:247
  553.4 47.4 %collective-permute-start.26 = (bf16[704,128]{1,0:T(8,128)(2,1)}, bf16[704,128]{1,0:T(8,128)(2,1)S(1)}, u32[]{:S(2)}, u32[]{:S(2)}) collective-permute-start(bf16[704,128]{1,0:T(8,128)(2,1)} %get-tuple-element.42), channel_id=1, source_target_pairs={{0,12},{1,13},{2,14},{3,15},{4,8},{5,9},{6,10},{7,11},{8,4},{9,5},... | collective-permute-start | bytes 540680 | tf_op jit(solution)/shard_map/ppermute | solution.py:247
  554.5 46.3 %collective-permute-start.27 = (bf16[704,128]{1,0:T(8,128)(2,1)}, bf16[704,128]{1,0:T(8,128)(2,1)S(1)}, u32[]{:S(2)}, u32[]{:S(2)}) collective-permute-start(bf16[704,128]{1,0:T(8,128)(2,1)} %get-tuple-element.42), channel_id=1, source_target_pairs={{0,13},{1,12},{2,15},{3,14},{4,9},{5,8},{6,11},{7,10},{8,5},{9,4},... | collective-permute-start | bytes 540680 | tf_op jit(solution)/shard_map/ppermute | solution.py:247
  558.2 42.6 %collective-permute-start.28 = (bf16[704,128]{1,0:T(8,128)(2,1)}, bf16[704,128]{1,0:T(8,128)(2,1)}, u32[]{:S(2)}, u32[]{:S(2)}) collective-permute-start(bf16[704,128]{1,0:T(8,128)(2,1)} %get-tuple-element.42), channel_id=1, source_target_pairs={{0,14},{1,15},{2,12},{3,13},{4,10},{5,11},{6,8},{7,9},{8,6},{9,7},... | collective-permute-start | bytes 540680 | tf_op jit(solution)/shard_map/ppermute | solution.py:247
  564.2 37.5 %collective-permute-start.29 = (bf16[704,128]{1,0:T(8,128)(2,1)}, bf16[704,128]{1,0:T(8,128)(2,1)}, u32[]{:S(2)}, u32[]{:S(2)}) collective-permute-start(bf16[704,128]{1,0:T(8,128)(2,1)} %get-tuple-element.42), channel_id=1, source_target_pairs={{0,15},{1,14},{2,13},{3,12},{4,11},{5,10},{6,9},{7,8},{8,7},{9,6},... | collective-permute-start | bytes 540680 | tf_op jit(solution)/shard_map/ppermute | solution.py:247
  588.0 27.9 %all-to-all-start.4 = ((bf16[8,128,512]{2,1,0:T(8,128)(2,1)}), bf16[8,128,512]{2,1,0:T(8,128)(2,1)}, u32[]{:S(2)}, u32[]{:S(2)}) async-start(bf16[8,128,512]{2,1,0:T(8,128)(2,1)} %broadcast_in_dim.146), calls=%async_computation.4 | async-start | bytes 2097152 | tf_op jit(solution)/shard_map/all_to_all | solution.py:328
  (38 other events, 293.5 us)

commit v2 on v1

--- a/solution.py
+++ b/solution.py
@@ -18,8 +18,10 @@
 SLOTS = SLAB // TILE // N_PCOL
 OWN_TILES = 8
 RANKS = 2
-CHUNKS = ((0, 1), (1, 1), (2, 2))
+WIDE_CHUNKS = ((0, 1), (1, 1), (2, 2))
+CHUNKS = ((0, 1), (2, 2), (1, 1))
 GROUP = 8
+STEPS = 8
 ROW_BLOCK = 704
 MIB = 1 << 20
 
@@ -29,7 +31,7 @@
     return jnp.where(slot == index_row, 1.0, 0.0).astype(jnp.bfloat16)
 
 
-def pack_kernel(first, src, present, owner, rank, x_ref, cw_ref, rw_ref, out_ref, perm):
+def pack_kernel(first, ranks, src, present, owner, rank, x_ref, cw_ref, rw_ref, out_ref, perm):
     group, slot = pl.program_id(0), pl.program_id(1)
 
     @pl.when((group == 0) & (slot == 0))
@@ -55,17 +57,23 @@
             tile = jnp.dot(
                 perm[t], moved[t * TILE : (t + 1) * TILE], preferred_element_type=jnp.float32
             )
-            out_ref[owner[t], 0, rank[t], 0] = tile.astype(jnp.bfloat16)
-
-
-def pack(first, width, src, present, owner, rank, children, col_within, row_within):
+            if ranks == RANKS:
+                out_ref[owner[t], 0, rank[t], 0] = tile.astype(jnp.bfloat16)
+            else:
+
+                @pl.when(rank[t] == 0)
+                def _():
+                    out_ref[owner[t], 0, 0, 0] = tile.astype(jnp.bfloat16)
+
+
+def pack(first, width, ranks, src, present, owner, rank, children, col_within, row_within):
     def source(q, s, src, present, owner, rank):
         return src[q * SLOTS + first + s]
 
     return pl.pallas_call(
-        functools.partial(pack_kernel, first),
+        functools.partial(pack_kernel, first, ranks),
         out_shape=jax.ShapeDtypeStruct(
-            (N_PROW, N_PCOL, RANKS, width, TILE, TILE), jnp.bfloat16
+            (N_PROW, N_PCOL, ranks, width, TILE, TILE), jnp.bfloat16
         ),
         grid_spec=pltpu.PrefetchScalarGridSpec(
             num_scalar_prefetch=4,
@@ -76,17 +84,143 @@
                 pl.BlockSpec((OWN_TILES, TILE), lambda *a: (0, 0)),
             ],
             out_specs=pl.BlockSpec(
-                (N_PROW, 1, RANKS, 1, TILE, TILE), lambda q, s, *a: (0, q, 0, s, 0, 0)
+                (N_PROW, 1, ranks, 1, TILE, TILE), lambda q, s, *a: (0, q, 0, s, 0, 0)
             ),
             scratch_shapes=[pltpu.VMEM((OWN_TILES, TILE, TILE), jnp.bfloat16)],
         ),
-        compiler_params=pltpu.CompilerParams(vmem_limit_bytes=24 * MIB),
+        compiler_params=pltpu.CompilerParams(vmem_limit_bytes=56 * MIB),
         cost_estimate=pl.CostEstimate(
             flops=4 * N_PCOL * width * OWN_TILES * TILE**3,
             bytes_accessed=3 * N_PCOL * width * OWN_TILES * TILE * TILE * 2,
             transcendentals=0,
         ),
     )(src, present, owner, rank, children, col_within, row_within)
+
+
+def pack_second_kernel(per_step, src, present, which, x_ref, cw_ref, rw_ref, out_ref):
+    perm = one_hot_t(rw_ref[pl.ds(which[0], 1), :])
+    for k in range(per_step):
+        slot = pl.program_id(0) * per_step + k
+        col = src[slot]
+        block = x_ref[:, pl.ds(pl.multiple_of(col * TILE, TILE), TILE)]
+        moved = lax.dot_general(
+            block,
+            one_hot_t(cw_ref[pl.ds(col, 1), :]),
+            (((1,), (1,)), ((), ())),
+            preferred_element_type=jnp.float32,
+        ).astype(jnp.bfloat16)
+        tile = jnp.dot(perm, moved, preferred_element_type=jnp.float32)
+        keep = jnp.full((TILE, TILE), present[slot], jnp.int32) != 0
+        out_ref[k] = jnp.where(keep, tile, 0.0).astype(jnp.bfloat16)
+
+
+def pack_second(src, present, which, children, col_within, row_within):
+    n_slots, per_step = SLAB // TILE, 16
+    return pl.pallas_call(
+        functools.partial(pack_second_kernel, per_step),
+        out_shape=jax.ShapeDtypeStruct((n_slots, TILE, TILE), jnp.bfloat16),
+        grid_spec=pltpu.PrefetchScalarGridSpec(
+            num_scalar_prefetch=3,
+            grid=(n_slots // per_step,),
+            in_specs=[
+                pl.BlockSpec((TILE, children.shape[1]), lambda i, s, p, w: (w[0], 0)),
+                pl.BlockSpec(col_within.shape, lambda i, *a: (0, 0)),
+                pl.BlockSpec((OWN_TILES, TILE), lambda i, *a: (0, 0)),
+            ],
+            out_specs=pl.BlockSpec((per_step, TILE, TILE), lambda i, *a: (i, 0, 0)),
+        ),
+        compiler_params=pltpu.CompilerParams(vmem_limit_bytes=56 * MIB),
+        cost_estimate=pl.CostEstimate(
+            flops=4 * n_slots * TILE**3,
+            bytes_accessed=2 * n_slots * TILE * TILE * 2,
+            transcendentals=0,
+        ),
+    )(src, present, which, children, col_within, row_within)
+
+
+def sum_kernel(width, counts, bins, seconds, pivots, x_ref, *refs):
+    parts, (front_ref, pivot_ref, acc, picked) = refs[: len(counts)], refs[len(counts) :]
+    step = pl.program_id(0)
+    cols = width * TILE
+    per_step = N_DEV // STEPS
+
+    @pl.when(step == 0)
+    def _():
+        @pl.loop(0, FRONT_TILES)
+        def _(i):
+            acc[pl.ds(pl.multiple_of(i * TILE, TILE), TILE), :] = jnp.zeros(
+                (TILE, cols), jnp.float32
+            )
+
+    def add(place, source, index):
+        @pl.when(place >= 0)
+        def _():
+            rows = pl.ds(pl.multiple_of(place * TILE, TILE), TILE)
+            for c in range(width):
+                acc[rows, c * TILE : (c + 1) * TILE] += source[index, c].astype(jnp.float32)
+
+    for g in range(per_step):
+        add(bins[step * per_step + g], x_ref, g)
+    at = 0
+    for part, count in zip(parts, counts):
+        for g in range(count // STEPS):
+            add(seconds[at + step * (count // STEPS) + g], part, g)
+        at += count
+
+    @pl.when(step == STEPS - 1)
+    def _():
+        @pl.loop(0, FRONT_TILES)
+        def _(i):
+            rows = pl.ds(pl.multiple_of(i * TILE, TILE), TILE)
+            front_ref[rows, :] = acc[rows, :].astype(jnp.bfloat16)
+
+        @pl.loop(0, TILE)
+        def _(j):
+            row = pivots[j]
+            mine = (row >= 0).astype(jnp.float32)
+            value = acc[pl.ds(jnp.maximum(row, 0), 1), :]
+            picked[pl.ds(j, 1), :] = value * mine
+
+        pivot_ref[...] = picked[...].astype(jnp.bfloat16)
+
+
+def sum_chunk(first, width, bins, seconds, pivots, arrived, parts):
+    cols = width * TILE
+    counts = [p.shape[0] for p in parts]
+    return pl.pallas_call(
+        functools.partial(sum_kernel, width, counts),
+        out_shape=[
+            jax.ShapeDtypeStruct((LOCAL_ROWS, cols), jnp.bfloat16),
+            jax.ShapeDtypeStruct((TILE, cols), jnp.bfloat16),
+        ],
+        grid_spec=pltpu.PrefetchScalarGridSpec(
+            num_scalar_prefetch=3,
+            grid=(STEPS,),
+            in_specs=[
+                pl.BlockSpec((N_DEV // STEPS, width, TILE, TILE), lambda i, *a: (i, 0, 0, 0))
+            ]
+            + [
+                pl.BlockSpec(
+                    (n // STEPS, width, TILE, TILE), lambda i, *a: (i, first // width, 0, 0)
+                )
+                for n in counts
+            ],
+            out_specs=[
+                pl.BlockSpec((LOCAL_ROWS, cols), lambda i, *a: (0, 0)),
+                pl.BlockSpec((TILE, cols), lambda i, *a: (0, 0)),
+            ],
+            scratch_shapes=[
+                pltpu.VMEM((LOCAL_ROWS, cols), jnp.float32),
+                pltpu.VMEM((TILE, cols), jnp.float32),
+            ],
+        ),
+        compiler_params=pltpu.CompilerParams(vmem_limit_bytes=56 * MIB),
+        cost_estimate=pl.CostEstimate(
+            flops=N_DEV * RANKS * TILE * cols,
+            bytes_accessed=(N_DEV * RANKS * TILE + LOCAL_ROWS) * cols * 2,
+            transcendentals=0,
+        ),
+    )(bins, seconds, pivots, arrived, *parts)
 
 
 def accumulate_kernel(width, bins, pivots, x_ref, front_ref, pivot_ref, acc, picked):
@@ -154,7 +288,7 @@
                 pltpu.VMEM((TILE, cols), jnp.float32),
             ],
         ),
-        compiler_params=pltpu.CompilerParams(vmem_limit_bytes=48 * MIB),
+        compiler_params=pltpu.CompilerParams(vmem_limit_bytes=56 * MIB),
         cost_estimate=pl.CostEstimate(
             flops=N_DEV * RANKS * TILE * cols,
             bytes_accessed=(N_DEV * RANKS * TILE + LOCAL_ROWS) * cols * 2,
@@ -173,7 +307,7 @@
     @pl.when(step == 0)
     def _():
         block = pivot_ref[0].astype(jnp.float32)
-        for p in range(1, N_PROW):
+        for p in range(1, pivot_ref.shape[0]):
             block = block + pivot_ref[p].astype(jnp.float32)
         upper[...] = jnp.dot(
             linv_ref[...], block.astype(jnp.bfloat16), preferred_element_type=jnp.float32
@@ -218,7 +352,7 @@
             ]
             + [
                 pl.BlockSpec((ROW_BLOCK, TILE), lambda i, *a: (i, 0)),
-                whole(N_PROW, TILE, cols),
+                whole(*pivots.shape),
                 whole(1, TILE),
                 whole(TILE, TILE),
                 whole(TILE, TILE),
@@ -226,13 +360,37 @@
             out_specs=pl.BlockSpec((ROW_BLOCK, cols), lambda i, *a: (i, 0)),
             scratch_shapes=[pltpu.VMEM((TILE, cols), jnp.bfloat16)],
         ),
-        compiler_params=pltpu.CompilerParams(vmem_limit_bytes=32 * MIB),
+        compiler_params=pltpu.CompilerParams(vmem_limit_bytes=56 * MIB),
         cost_estimate=pl.CostEstimate(
             flops=2 * LOCAL_ROWS * TILE * (cols + TILE),
             bytes_accessed=2 * LOCAL_ROWS * cols * 2,
             transcendentals=0,
         ),
     )(is_first, *fronts, panel, pivots, rows, linv, uinv)
+
+
+def exchange(parts, axes):
+    return lax.all_to_all(parts, axes, split_axis=0, concat_axis=0, tiled=True)
+
+
+def gather_prow(own):
+    def shifted(value, by):
+        return lax.ppermute(value, "prow", [(p, (p + 2 * by) % N_PROW) for p in range(N_PROW)])
+
+    half = own.shape[0] // 2
+    before, after = shifted(own, 1), shifted(own, -1)
+    far_low = shifted(before[:half], 1)
+    far_high = shifted(after[half:], -1)
+    here = [own, before, after, far_low, far_high]
+    there = [lax.ppermute(v, "prow", [(p, p ^ 1) for p in range(N_PROW)]) for v in here]
+    named = [(0, 2 * half), (0, 2 * half), (0, 2 * half), (0, half), (half, half)]
+    shifts = [0, -1, 1, -2, 2]
+    places = [
+        (flip, shift, begin, count)
+        for flip in (0, 1)
+        for shift, (begin, count) in zip(shifts, named)
+    ]
+    return here + there, places
 
 
 def spread_panel(panel, my_pcol):
@@ -290,57 +448,84 @@
     nth = jnp.sum((mine[:, None, :] & earlier[None]).astype(jnp.int32), axis=2)
     want = jnp.arange(RANKS, dtype=jnp.int32)[None, :, None]
     is_it = mine[:, None, :] & (nth[:, None, :] == want)
-    bins = jnp.max(
-        jnp.where(is_it, (codes % FRONT_TILES)[:, None, :], -1), axis=2
-    ).reshape(-1)
+    bins = jnp.max(jnp.where(is_it, (codes % FRONT_TILES)[:, None, :], -1), axis=2)
+
+    second = rank == 1
+    which = jnp.min(jnp.where(second, order, OWN_TILES - 1)).reshape(1)
+    owner_of = codes // FRONT_TILES
+    again = jnp.sum(
+        ((owner_of[:, :, None] == owner_of[:, None, :]) & earlier[None]).astype(jnp.int32), axis=2
+    )
+    is_second = again == 1
+    more = jnp.max(jnp.sum(is_second.astype(jnp.int32), axis=1)) > 1
+    seconds = jnp.max(
+        jnp.where(is_second & mine, codes % FRONT_TILES, -1), axis=1
+    ).reshape(N_PROW, N_PCOL)
 
     pivot_local = jnp.where(
         pivot_rows // LOCAL_ROWS == my_prow, pivot_rows % LOCAL_ROWS, -1
     ).astype(jnp.int32)
-
-    fronts, picks = [], []
+    is_first = (my_pcol == 0).astype(jnp.int32).reshape(1)
+    pivot_line = pivot_local.reshape(1, TILE)
+    col_line = col_within.reshape(n_src, 1, TILE)
+
+    sent = pack_second(src, present, which, children, col_within, row_within)
+    own = exchange(sent.reshape(N_PCOL, SLOTS, TILE, TILE), "pcol")
+    parts, places = gather_prow(own)
+    places = jnp.concatenate(
+        [
+            jnp.take(seconds, ((my_prow ^ flip) + 2 * shift) % N_PROW, axis=0)[
+                begin : begin + count
+            ]
+            for flip, shift, begin, count in places
+        ]
+    )
+
+    fronts, picks = {}, {}
     panel = None
     for first, width in CHUNKS:
         sent = pack(
-            first,
-            width,
-            src,
-            present,
-            owners,
-            rank,
-            children,
-            col_within.reshape(n_src, 1, TILE),
-            row_within,
+            first, width, 1, src, present, owners, rank, children, col_line, row_within
         )
-        arrived = lax.all_to_all(
-            sent.reshape(N_DEV, RANKS, width, TILE, TILE),
-            ("prow", "pcol"),
-            split_axis=0,
-            concat_axis=0,
-            tiled=True,
+        arrived = exchange(sent.reshape(N_DEV, width, TILE, TILE), ("prow", "pcol"))
+        fronts[first], picks[first] = sum_chunk(
+            first, width, bins[:, 0], places, pivot_local, arrived, parts
         )
-        front, picked = accumulate(width, bins, pivot_local, arrived)
-        fronts.append(front)
-        picks.append(picked)
         if first == 0:
-            panel = spread_panel(front[:, :TILE], my_pcol)
-    picked = jnp.concatenate(picks, axis=1)
-    pivots = lax.all_to_all(
-        jnp.broadcast_to(picked[None], (N_PROW,) + picked.shape),
-        "prow",
-        split_axis=0,
-        concat_axis=0,
-        tiled=True,
-    )
-    return update(
-        (my_pcol == 0).astype(jnp.int32).reshape(1),
-        fronts,
-        panel,
-        pivots,
-        pivot_local.reshape(1, TILE),
-        lower_inverse,
-        upper_inverse,
-    )
+            panel = spread_panel(fronts[first][:, :TILE], my_pcol)
+    fronts = [fronts[k] for k in sorted(fronts)]
+    pivots = jnp.concatenate([picks[k] for k in sorted(picks)], axis=1)
+    for bit in (1, 2):
+        pivots = pivots + lax.ppermute(pivots, "prow", [(p, p ^ bit) for p in range(N_PROW)])
+    pivots = jnp.stack(
+        [pivots, lax.ppermute(pivots, "prow", [(p, p ^ 4) for p in range(N_PROW)])]
+    )
+
+    def narrow():
+        return update(
+            is_first, fronts, panel, pivots, pivot_line, lower_inverse, upper_inverse
+        )
+
+    def wide():
+        fronts, picks = [], []
+        for first, width in WIDE_CHUNKS:
+            sent = pack(
+                first, width, RANKS, src, present, owners, rank, children, col_line, row_within
+            )
+            arrived = exchange(
+                sent.reshape(N_DEV, RANKS, width, TILE, TILE), ("prow", "pcol")
+            )
+            front, picked = accumulate(width, bins.reshape(-1), pivot_local, arrived)
+            fronts.append(front)
+            picks.append(picked)
+        panel = spread_panel(fronts[0][:, :TILE], my_pcol)
+        picked = jnp.concatenate(picks, axis=1)
+        pivots = exchange(jnp.broadcast_to(picked[None], (N_PROW,) + picked.shape), "prow")
+        return update(
+            is_first, fronts, panel, pivots, pivot_line, lower_inverse, upper_inverse
+        )
+
+    return lax.cond(more, wide, narrow)
 
 
 def solution(mesh):

time: 637 us -> 564 us (0.89)
  waiting for transfers between devices: 375 us -> 201 us
  Pallas kernels: 88.3 us -> 156 us
  starting transfers between devices: 123 us -> 166 us
  local copies, waits for them, and re-layouts: 44.4 us -> 28.8 us
    ppermute x15, waiting for transfers between devices: 191 us -> 1.68 us  [spread_panel(): got = lax.ppermute(pieces[q], 'pcol', [(0, q)])]
    ppermute x0 -> x12, waiting for transfers between devices: none -> 140 us  [the longest x4 139 us: shifted(): lax.ppermute(value, 'prow', [(p, (p + 2 * by) % N_PROW) for p in range(N_...]
    all_to_all x4, waiting for transfers between devices: 182 us -> 46.7 us  [exchange(): return lax.all_to_all(parts, axes, split_axis=0, concat_axis=0, tiled=True)]
    pallas_call x6 -> x7, Pallas kernels: 74.7 us -> 138 us  [the longest x3 86.5 us: pack(): pl.pallas_call(functools.partial(pack_kernel, first, ranks), out_shape=ja...]
    ppermute x0 -> x12, starting transfers between devices: none -> 61.1 us  [the longest x5 38.2 us: gather_prow(): lax.ppermute(v, 'prow', [(p, p ^ 1) for p in range(N_PROW)])]
    unnamed x55 -> x49, local copies, waits for them, and re-layouts: 39.2 us -> 1.72 us
    all_to_all x4, starting transfers between devices: 46.8 us -> 27.9 us  [exchange(): return lax.all_to_all(parts, axes, split_axis=0, concat_axis=0, tiled=True)]
    dynamic_update_slice x15, local copies, waits for them, and re-layouts: 2.24 us -> 13.3 us  [spread_panel(): whole = lax.dynamic_update_index_in_dim(whole, got, my_pcol ^ i, 0)]
  transfers between devices with their start and end apart: 35 -> 47, of which waited for: 14 -> 11; matrix products, arithmetic and copies ran while one was open for 1% -> 3% of each run, Pallas kernels for 12% -> 25%
where the time goes in v2:
time: 564 us; the launch traced here: 561 us
  waiting for transfers between devices  201 us (36%)
  starting transfers between devices  166 us (29%)
  Pallas kernels  156 us (28%)
  local copies, waits for them, and re-layouts  28.8 us (5%)
  other arithmetic  7.7 us (1%)
    ppermute x4, waiting for transfers between devices, shifted(): lax.ppermute(value, 'prow', [(p, (p + 2 * by) % N_PROW) for p in range(N_...  139 us
    pallas_call x3, Pallas kernels, pack(): pl.pallas_call(functools.partial(pack_kernel, first, ranks), out_shape=ja...  86.5 us
    all_to_all x4, waiting for transfers between devices, exchange(): return lax.all_to_all(parts, axes, split_axis=0, concat_axis=0, tiled=True)  46.7 us
    ppermute x5, starting transfers between devices, gather_prow(): lax.ppermute(v, 'prow', [(p, p ^ 1) for p in range(N_PROW)])  38.2 us
    pallas_call x3, Pallas kernels, sum_chunk(): pl.pallas_call(functools.partial(sum_kernel, width, counts), out_shape=[j...  36.3 us
    ppermute x15, starting transfers between devices, spread_panel(): got = lax.ppermute(pieces[q], 'pcol', [(0, q)])  34.3 us
    ppermute x15, starting transfers between devices, spread_panel(): got = lax.ppermute(piece, 'pcol', [(q, q ^ i) for q in range(N_PCOL)])  31.5 us
    all_to_all x4, starting transfers between devices, exchange(): return lax.all_to_all(parts, axes, split_axis=0, concat_axis=0, tiled=True)  27.9 us
  transfers between devices with their start and end apart: 47, of which 11 were waited for; matrix products, arithmetic and copies ran while one was open for 3% of the time, Pallas kernels for 25%

profile of v2, /device:TPU:1, one launch (start us, length us, event | category | flops | bytes accessed | tf_op | source)
XLA Modules:
  0.0 561.3 jit_solution(10871718989586613103)
XLA Ops:
  1.5 11.5 %all-to-all-start.4 = ((s32[128,8,128]{2,1,0:T(8,128)}), s32[128,8,128]{2,1,0:T(8,128)S(1)}, u32[]{:S(2)}, u32[]{:S(2)}) async-start(s32[128,8,128]{2,1,0:T(8,128)} %broadcast_in_dim.196), calls=%async_computation.4 | async-start | bytes 1048576 | tf_op jit(solution)/shard_map/all_to_all | solution.py:440
  16.8 15.0 %shard_map.94 = bf16[64,128,128]{2,1,0:T(8,128)(2,1)} custom-call(s32[64]{0:T(128)S(1)} %get-tuple-element.405.src, s32[64]{0:T(128)S(1)} %get-tuple-element.404.present, s32[1]{0:T(128)} %bitcast.60.which, bf16[1024,6144]{1,0:T(8,128)(2,1)} %x_ref.7, s32[48,128]{1,0:T(8,128)} %fusion.21.cw_ref, s32[8,128]{1,0:T(8,128)} %rw_ref.7), custom_call_target="tpu_custom_call" | custom-call | flops 536870912 | bytes 4194304 | tf_op jit(solution)/shard_map/pallas_call | solution.py:119
  32.6 7.2 %all-to-all-start.6 = ((bf16[16,4,128,128]{3,2,1,0:T(8,128)(2,1)}), bf16[16,4,128,128]{3,2,1,0:T(8,128)(2,1)S(1)}, u32[]{:S(2)}, u32[]{:S(2)}) async-start(bf16[16,4,128,128]{3,2,1,0:T(8,128)(2,1)} %bitcast.152), calls=%async_computation.6 | async-start | bytes 4194304 | tf_op jit(solution)/shard_map/all_to_all | solution.py:373
  39.9 23.6 %shard_map.96 = bf16[8,16,1,1,128,128]{5,4,3,2,1,0:T(8,128)(2,1)} custom-call(s32[64]{0:T(128)S(1)} %get-tuple-element.405.src, s32[64]{0:T(128)S(1)} %get-tuple-element.404.present, s32[8]{0:T(128)S(1)} %bitcast.160, s32[8]{0:T(128)S(1)} %convert_reduce_fusion.3.rank, bf16[1024,6144]{1,0:T(8,128)(2,1)} %x_ref.7, s32[48,1,128]{2,1,0:T(1,128)S(1)} %bitcast.153, ...), custom_call_target="tpu_custom_call" | custom-call | flops 1073741824 | bytes 12582912 | tf_op jit(solution)/shard_map/pallas_call | solution.py:73
  69.1 8.7 %all-to-all-start.7 = ((bf16[128,1,128,128]{3,2,1,0:T(8,128)(2,1)}), bf16[128,1,128,128]{3,2,1,0:T(8,128)(2,1)}, u32[]{:S(2)}, u32[]{:S(2)}) async-start(bf16[128,1,128,128]{3,2,1,0:T(8,128)(2,1)} %bitcast.148), calls=%async_computation.7 | async-start | bytes 8388608 | tf_op jit(solution)/shard_map/all_to_all | solution.py:373
  77.8 22.3 %shard_map.93 = bf16[8,16,1,1,128,128]{5,4,3,2,1,0:T(8,128)(2,1)} custom-call(s32[64]{0:T(128)S(1)} %get-tuple-element.405.src, s32[64]{0:T(128)S(1)} %get-tuple-element.404.present, s32[8]{0:T(128)S(1)} %bitcast.161, s32[8]{0:T(128)S(1)} %convert_reduce_fusion.3.rank, bf16[1024,6144]{1,0:T(8,128)(2,1)} %x_ref.7, s32[48,1,128]{2,1,0:T(1,128)S(1)} %bitcast.154, ...), custom_call_target="tpu_custom_call" | custom-call | flops 1073741824 | bytes 12582912 | tf_op jit(solution)/shard_map/pallas_call | solution.py:73
  100.1 29.7 %all-to-all-done.7.x_ref = bf16[128,1,128,128]{3,2,1,0:T(8,128)(2,1)} async-done(((bf16[128,1,128,128]{3,2,1,0:T(8,128)(2,1)}), bf16[128,1,128,128]{3,2,1,0:T(8,128)(2,1)}, u32[]{:S(2)}, u32[]{:S(2)}) %all-to-all-start.7) | async-done | bytes 4194336 | tf_op jit(solution)/shard_map/all_to_all | solution.py:373
  129.8 6.0 %all-to-all-start.5 = ((bf16[128,1,128,128]{3,2,1,0:T(8,128)(2,1)}), bf16[128,1,128,128]{3,2,1,0:T(8,128)(2,1)}, u32[]{:S(2)}, u32[]{:S(2)}) async-start(bf16[128,1,128,128]{3,2,1,0:T(8,128)(2,1)} %bitcast.149), calls=%async_computation.5 | async-start | bytes 8388608 | tf_op jit(solution)/shard_map/all_to_all | solution.py:373
  135.8 40.6 %shard_map.98 = bf16[8,16,1,2,128,128]{5,4,3,2,1,0:T(8,128)(2,1)} custom-call(s32[64]{0:T(128)S(1)} %get-tuple-element.405.src, s32[64]{0:T(128)S(1)} %get-tuple-element.404.present, s32[8]{0:T(128)S(1)} %bitcast.162, s32[8]{0:T(128)S(1)} %convert_reduce_fusion.3.rank, bf16[1024,6144]{1,0:T(8,128)(2,1)} %x_ref.7, s32[48,1,128]{2,1,0:T(1,128)S(1)} %bitcast.155, ...), custom_call_target="tpu_custom_call" | custom-call | flops 2147483648 | bytes 25165824 | tf_op jit(solution)/shard_map/pallas_call | solution.py:73
  176.5 11.4 %all-to-all-done.5.x_ref = bf16[128,1,128,128]{3,2,1,0:T(8,128)(2,1)} async-done(((bf16[128,1,128,128]{3,2,1,0:T(8,128)(2,1)}), bf16[128,1,128,128]{3,2,1,0:T(8,128)(2,1)}, u32[]{:S(2)}, u32[]{:S(2)}) %all-to-all-start.5) | async-done | bytes 4194336 | tf_op jit(solution)/shard_map/all_to_all | solution.py:373
  187.8 6.0 %all-to-all-start.8 = ((bf16[128,2,128,128]{3,2,1,0:T(8,128)(2,1)}), bf16[128,2,128,128]{3,2,1,0:T(8,128)(2,1)}, u32[]{:S(2)}, u32[]{:S(2)}) async-start(bf16[128,2,128,128]{3,2,1,0:T(8,128)(2,1)} %bitcast.145), calls=%async_computation.8 | async-start | bytes 16777216 | tf_op jit(solution)/shard_map/all_to_all | solution.py:373
  196.6 134.7 %collective-permute-done.30.refs_1_ = bf16[16,4,128,128]{3,2,1,0:T(8,128)(2,1)} collective-permute-done((bf16[16,4,128,128]{3,2,1,0:T(8,128)(2,1)S(1)}, bf16[16,4,128,128]{3,2,1,0:T(8,128)(2,1)}, u32[]{:S(2)}, u32[]{:S(2)}) %collective-permute-start.30) | collective-permute-done | bytes 2097184 | tf_op jit(solution)/shard_map/ppermute | solution.py:378
  344.8 13.7 %collective-permute-start.36 = (bf16[16,4,128,128]{3,2,1,0:T(8,128)(2,1)}, bf16[16,4,128,128]{3,2,1,0:T(8,128)(2,1)}, u32[]{:S(2)}, u32[]{:S(2)}) collective-permute-start(bf16[16,4,128,128]{3,2,1,0:T(8,128)(2,1)} %collective-permute-done.31.refs_2_), channel_id=1, source_target_pairs={{0,16},{16,0},{32,48},{48,32},{64,80},{80,64},{96,112},{112,96},{1... | collective-permute-start | bytes 6291464 | tf_op jit(solution)/shard_map/ppermute | solution.py:385
  364.2 14.4 %collective-permute-start.37 = (bf16[8,4,128,128]{3,2,1,0:T(8,128)(2,1)S(1)}, bf16[8,4,128,128]{3,2,1,0:T(8,128)(2,1)}, u32[]{:S(2)}, u32[]{:S(2)}) collective-permute-start(bf16[8,4,128,128]{3,2,1,0:T(8,128)(2,1)S(1)} %collective-permute-done.32.refs_3_), channel_id=1, source_target_pairs={{0,16},{16,0},{32,48},{48,32},{64,80},{80,64},{96,112},{112,96},{1... | collective-permute-start | bytes 3145736 | tf_op jit(solution)/shard_map/ppermute | solution.py:385
  378.6 8.9 %collective-permute-start.38 = (bf16[8,4,128,128]{3,2,1,0:T(8,128)(2,1)}, bf16[8,4,128,128]{3,2,1,0:T(8,128)(2,1)}, u32[]{:S(2)}, u32[]{:S(2)}) collective-permute-start(bf16[8,4,128,128]{3,2,1,0:T(8,128)(2,1)} %collective-permute-done.33.refs_4_), channel_id=1, source_target_pairs={{0,16},{16,0},{32,48},{48,32},{64,80},{80,64},{96,112},{112,96},{1... | collective-permute-start | bytes 3145736 | tf_op jit(solution)/shard_map/ppermute | solution.py:385
  390.9 10.0 %shard_map.95 = (bf16[11264,128]{1,0:T(8,128)(2,1)S(1)}, bf16[128,128]{1,0:T(8,128)(2,1)}) custom-call(s32[128]{0:T(128)} %slice_bitcast_fusion.bins, s32[128]{0:T(128)} %concatenate.9.seconds, s32[128]{0:T(128)S(1)} %compare_select_fusion.1.pivots, bf16[128,1,128,128]{3,2,1,0:T(8,128)(2,1)} %all-to-all-done.5.x_ref, bf16[16,4,128,128]{3,2,1,0:T(8,128)(2,1)} %copy-done, ...), custom_call_target="tpu_custom_call" | custom-call | flops 4194304 | bytes 11272192 | tf_op jit(solution)/shard_map/pallas_call | solution.py:190
  402.0 6.9 %collective-permute-start.39 = (bf16[704,128]{1,0:T(8,128)(2,1)S(1)}, bf16[704,128]{1,0:T(8,128)(2,1)S(1)}, u32[]{:S(2)}, u32[]{:S(2)}) collective-permute-start(bf16[704,128]{1,0:T(8,128)(2,1)S(1)} %get-tuple-element.437), channel_id=1, source_target_pairs={{0,15},{16,31},{32,47},{48,63},{64,79},{80,95},{96,111},{112,127}} | collective-permute-start | bytes 540680 | tf_op jit(solution)/shard_map/ppermute | solution.py:400
  428.2 11.2 %shard_map.97 = (bf16[11264,128]{1,0:T(8,128)(2,1)}, bf16[128,128]{1,0:T(8,128)(2,1)}) custom-call(s32[128]{0:T(128)} %slice_bitcast_fusion.bins, s32[128]{0:T(128)} %concatenate.9.seconds, s32[128]{0:T(128)S(1)} %compare_select_fusion.1.pivots, bf16[128,1,128,128]{3,2,1,0:T(8,128)(2,1)} %all-to-all-done.7.x_ref, bf16[16,4,128,128]{3,2,1,0:T(8,128)(2,1)} %copy-done, ...), custom_call_target="tpu_custom_call" | custom-call | flops 4194304 | bytes 11272192 | tf_op jit(solution)/shard_map/pallas_call | solution.py:190
  450.0 15.2 %shard_map.99 = (bf16[11264,256]{1,0:T(8,128)(2,1)}, bf16[128,256]{1,0:T(8,128)(2,1)}) custom-call(s32[128]{0:T(128)} %slice_bitcast_fusion.bins, s32[128]{0:T(128)} %concatenate.9.seconds, s32[128]{0:T(128)S(1)} %compare_select_fusion.1.pivots, bf16[128,2,128,128]{3,2,1,0:T(8,128)(2,1)} %all-to-all-done.8.x_ref, bf16[16,4,128,128]{3,2,1,0:T(8,128)(2,1)} %copy-done, ...), custom_call_target="tpu_custom_call" | custom-call | flops 8388608 | bytes 22544384 | tf_op jit(solution)/shard_map/pallas_call | solution.py:190
  486.0 5.6 %collective-permute-start.63 = (bf16[704,128]{1,0:T(8,128)(2,1)S(1)}, bf16[704,128]{1,0:T(8,128)(2,1)S(1)}, u32[]{:S(2)}, u32[]{:S(2)}) collective-permute-start(bf16[704,128]{1,0:T(8,128)(2,1)S(1)} %select_select_fusion.1), channel_id=1, source_target_pairs={{0,10},{1,11},{2,8},{3,9},{4,14},{5,15},{6,12},{7,13},{8,2},{9,3},... | collective-permute-start | bytes 540680 | tf_op jit(solution)/shard_map/ppermute | solution.py:405
  491.7 6.8 %collective-permute-start.71 = (bf16[128,512]{1,0:T(8,128)(2,1)S(1)}, bf16[128,512]{1,0:T(8,128)(2,1)S(1)}, u32[]{:S(2)}, u32[]{:S(2)}) collective-permute-start(bf16[128,512]{1,0:T(8,128)(2,1)S(1)} %add.238), channel_id=1, source_target_pairs={{0,64},{16,80},{32,96},{48,112},{64,0},{80,16},{96,32},{112,48},{1... | collective-permute-start | bytes 393224 | tf_op jit(solution)/shard_map/ppermute | solution.py:501
  498.5 5.8 %collective-permute-start.64 = (bf16[704,128]{1,0:T(8,128)(2,1)S(1)}, bf16[704,128]{1,0:T(8,128)(2,1)}, u32[]{:S(2)}, u32[]{:S(2)}) collective-permute-start(bf16[704,128]{1,0:T(8,128)(2,1)S(1)} %select_select_fusion.1), channel_id=1, source_target_pairs={{0,11},{1,10},{2,9},{3,8},{4,15},{5,14},{6,13},{7,12},{8,3},{9,2},... | collective-permute-start | bytes 540680 | tf_op jit(solution)/shard_map/ppermute | solution.py:405
  526.1 35.2 %conditional.1 = (bf16[11264,512]{1,0:T(8,128)(2,1)}) conditional(s32[]{:T(128)} %convert_element_type.21, (bf16[704,128]{1,0:T(8,128)(2,1)S(1)}, s32[]{:T(128)}, bf16[704,128]{1,0:T(8,128)(2,1)}, bf16[704,128]{1,0:T(8,128)(2,1)}, bf16[704,128]{1,0:T(8,128)(2,1)}, /*index=5*/bf16[704,128]{1,0:T(8,128)(2,1)}, bf16[704,128]{1,0:T(8,128)(2,1)}, ...), branch_computations={%region_10.12_spmd, %region_11.13_spmd} | conditional | flops 6158983168 | bytes 280144672 | solution.py:528
  543.4 17.9 %branch_0_fun.1 = bf16[11264,512]{1,0:T(8,128)(2,1)} custom-call(s32[1]{0:T(128)} %get-tuple-element.295.is_first, bf16[11264,128]{1,0:T(8,128)(2,1)} %copy-done.2, bf16[11264,128]{1,0:T(8,128)(2,1)} %get-tuple-element.297.refs_1_, bf16[11264,256]{1,0:T(8,128)(2,1)} %get-tuple-element.298.refs_2_, bf16[11264,128]{1,0:T(8,128)(2,1)} %bitcast.150, ...), custom_call_target="tpu_custom_call" | custom-call | flops 1845493760 | bytes 23068672 | tf_op jit(solution)/shard_map/cond/branch_0_fun/pallas_call | solution.py:344
  (192 shorter events, 126.9 us)
Async XLA Ops:
  1.5 30.3 %all-to-all-start.4 = ((s32[128,8,128]{2,1,0:T(8,128)}), s32[128,8,128]{2,1,0:T(8,128)S(1)}, u32[]{:S(2)}, u32[]{:S(2)}) async-start(s32[128,8,128]{2,1,0:T(8,128)} %broadcast_in_dim.196), calls=%async_computation.4 | async-start | bytes 1048576 | tf_op jit(solution)/shard_map/all_to_all | solution.py:440
  32.6 36.5 %all-to-all-start.6 = ((bf16[16,4,128,128]{3,2,1,0:T(8,128)(2,1)}), bf16[16,4,128,128]{3,2,1,0:T(8,128)(2,1)S(1)}, u32[]{:S(2)}, u32[]{:S(2)}) async-start(bf16[16,4,128,128]{3,2,1,0:T(8,128)(2,1)} %bitcast.152), calls=%async_computation.6 | async-start | bytes 4194304 | tf_op jit(solution)/shard_map/all_to_all | solution.py:373
  69.1 60.7 %all-to-all-start.7 = ((bf16[128,1,128,128]{3,2,1,0:T(8,128)(2,1)}), bf16[128,1,128,128]{3,2,1,0:T(8,128)(2,1)}, u32[]{:S(2)}, u32[]{:S(2)}) async-start(bf16[128,1,128,128]{3,2,1,0:T(8,128)(2,1)} %bitcast.148), calls=%async_computation.7 | async-start | bytes 8388608 | tf_op jit(solution)/shard_map/all_to_all | solution.py:373
  129.8 58.0 %all-to-all-start.5 = ((bf16[128,1,128,128]{3,2,1,0:T(8,128)(2,1)}), bf16[128,1,128,128]{3,2,1,0:T(8,128)(2,1)}, u32[]{:S(2)}, u32[]{:S(2)}) async-start(bf16[128,1,128,128]{3,2,1,0:T(8,128)(2,1)} %bitcast.149), calls=%async_computation.5 | async-start | bytes 8388608 | tf_op jit(solution)/shard_map/all_to_all | solution.py:373
  187.8 262.2 %all-to-all-start.8 = ((bf16[128,2,128,128]{3,2,1,0:T(8,128)(2,1)}), bf16[128,2,128,128]{3,2,1,0:T(8,128)(2,1)}, u32[]{:S(2)}, u32[]{:S(2)}) async-start(bf16[128,2,128,128]{3,2,1,0:T(8,128)(2,1)} %bitcast.145), calls=%async_computation.8 | async-start | bytes 16777216 | tf_op jit(solution)/shard_map/all_to_all | solution.py:373
  193.8 137.5 %collective-permute-start.30 = (bf16[16,4,128,128]{3,2,1,0:T(8,128)(2,1)S(1)}, bf16[16,4,128,128]{3,2,1,0:T(8,128)(2,1)}, u32[]{:S(2)}, u32[]{:S(2)}) collective-permute-start(bf16[16,4,128,128]{3,2,1,0:T(8,128)(2,1)S(1)} %all-to-all-done.6.refs_0_), channel_id=1, source_target_pairs={{0,32},{16,48},{32,64},{48,80},{64,96},{80,112},{96,0},{112,16},{1... | collective-permute-start | bytes 6291464 | tf_op jit(solution)/shard_map/ppermute | solution.py:378
  195.3 140.4 %collective-permute-start.31 = (bf16[16,4,128,128]{3,2,1,0:T(8,128)(2,1)S(1)}, bf16[16,4,128,128]{3,2,1,0:T(8,128)(2,1)}, u32[]{:S(2)}, u32[]{:S(2)}) collective-permute-start(bf16[16,4,128,128]{3,2,1,0:T(8,128)(2,1)S(1)} %all-to-all-done.6.refs_0_), channel_id=1, source_target_pairs={{0,96},{16,112},{32,0},{48,16},{64,32},{80,48},{96,64},{112,80},{1... | collective-permute-start | bytes 6291464 | tf_op jit(solution)/shard_map/ppermute | solution.py:378
  333.6 30.5 %collective-permute-start.32 = (bf16[8,4,128,128]{3,2,1,0:T(8,128)(2,1)}, bf16[8,4,128,128]{3,2,1,0:T(8,128)(2,1)S(1)}, u32[]{:S(2)}, u32[]{:S(2)}) collective-permute-start(bf16[8,4,128,128]{3,2,1,0:T(8,128)(2,1)} %slice.202), channel_id=1, source_target_pairs={{0,32},{16,48},{32,64},{48,80},{64,96},{80,112},{96,0},{112,16},{1... | collective-permute-start | bytes 3145736 | tf_op jit(solution)/shard_map/ppermute | solution.py:378
  338.0 40.5 %collective-permute-start.33 = (bf16[8,4,128,128]{3,2,1,0:T(8,128)(2,1)}, bf16[8,4,128,128]{3,2,1,0:T(8,128)(2,1)}, u32[]{:S(2)}, u32[]{:S(2)}) collective-permute-start(bf16[8,4,128,128]{3,2,1,0:T(8,128)(2,1)} %slice.203), channel_id=1, source_target_pairs={{0,96},{16,112},{32,0},{48,16},{64,32},{80,48},{96,64},{112,80},{1... | collective-permute-start | bytes 3145736 | tf_op jit(solution)/shard_map/ppermute | solution.py:378
  343.6 46.0 %collective-permute-start.34 = (bf16[16,4,128,128]{3,2,1,0:T(8,128)(2,1)S(1)}, bf16[16,4,128,128]{3,2,1,0:T(8,128)(2,1)}, u32[]{:S(2)}, u32[]{:S(2)}) collective-permute-start(bf16[16,4,128,128]{3,2,1,0:T(8,128)(2,1)S(1)} %all-to-all-done.6.refs_0_), channel_id=1, source_target_pairs={{0,16},{16,0},{32,48},{48,32},{64,80},{80,64},{96,112},{112,96},{1... | collective-permute-start | bytes 6291464 | tf_op jit(solution)/shard_map/ppermute | solution.py:385
  344.8 46.1 %collective-permute-start.35 = (bf16[16,4,128,128]{3,2,1,0:T(8,128)(2,1)}, bf16[16,4,128,128]{3,2,1,0:T(8,128)(2,1)}, u32[]{:S(2)}, u32[]{:S(2)}) collective-permute-start(bf16[16,4,128,128]{3,2,1,0:T(8,128)(2,1)} %collective-permute-done.30.refs_1_), channel_id=1, source_target_pairs={{0,16},{16,0},{32,48},{48,32},{64,80},{80,64},{96,112},{112,96},{1... | collective-permute-start | bytes 6291464 | tf_op jit(solution)/shard_map/ppermute | solution.py:385
  344.8 46.1 %collective-permute-start.36 = (bf16[16,4,128,128]{3,2,1,0:T(8,128)(2,1)}, bf16[16,4,128,128]{3,2,1,0:T(8,128)(2,1)}, u32[]{:S(2)}, u32[]{:S(2)}) collective-permute-start(bf16[16,4,128,128]{3,2,1,0:T(8,128)(2,1)} %collective-permute-done.31.refs_2_), channel_id=1, source_target_pairs={{0,16},{16,0},{32,48},{48,32},{64,80},{80,64},{96,112},{112,96},{1... | collective-permute-start | bytes 6291464 | tf_op jit(solution)/shard_map/ppermute | solution.py:385
  364.2 25.5 %collective-permute-start.37 = (bf16[8,4,128,128]{3,2,1,0:T(8,128)(2,1)S(1)}, bf16[8,4,128,128]{3,2,1,0:T(8,128)(2,1)}, u32[]{:S(2)}, u32[]{:S(2)}) collective-permute-start(bf16[8,4,128,128]{3,2,1,0:T(8,128)(2,1)S(1)} %collective-permute-done.32.refs_3_), channel_id=1, source_target_pairs={{0,16},{16,0},{32,48},{48,32},{64,80},{80,64},{96,112},{112,96},{1... | collective-permute-start | bytes 3145736 | tf_op jit(solution)/shard_map/ppermute | solution.py:385
  416.8 22.7 %collective-permute-start.44 = (bf16[704,128]{1,0:T(8,128)(2,1)}, bf16[704,128]{1,0:T(8,128)(2,1)}, u32[]{:S(2)}, u32[]{:S(2)}) collective-permute-start(bf16[704,128]{1,0:T(8,128)(2,1)} %get-tuple-element.432), channel_id=1, source_target_pairs={{0,10},{16,26},{32,42},{48,58},{64,74},{80,90},{96,106},{112,122}} | collective-permute-start | bytes 540680 | tf_op jit(solution)/shard_map/ppermute | solution.py:400
  418.7 22.7 %collective-permute-start.45 = (bf16[704,128]{1,0:T(8,128)(2,1)}, bf16[704,128]{1,0:T(8,128)(2,1)}, u32[]{:S(2)}, u32[]{:S(2)}) collective-permute-start(bf16[704,128]{1,0:T(8,128)(2,1)} %get-tuple-element.431), channel_id=1, source_target_pairs={{0,9},{16,25},{32,41},{48,57},{64,73},{80,89},{96,105},{112,121}} | collective-permute-start | bytes 540680 | tf_op jit(solution)/shard_map/ppermute | solution.py:400
  420.7 22.7 %collective-permute-start.46 = (bf16[704,128]{1,0:T(8,128)(2,1)}, bf16[704,128]{1,0:T(8,128)(2,1)}, u32[]{:S(2)}, u32[]{:S(2)}) collective-permute-start(bf16[704,128]{1,0:T(8,128)(2,1)} %get-tuple-element.430), channel_id=1, source_target_pairs={{0,8},{16,24},{32,40},{48,56},{64,72},{80,88},{96,104},{112,120}} | collective-permute-start | bytes 540680 | tf_op jit(solution)/shard_map/ppermute | solution.py:400
  424.3 21.0 %collective-permute-start.47 = (bf16[704,128]{1,0:T(8,128)(2,1)}, bf16[704,128]{1,0:T(8,128)(2,1)}, u32[]{:S(2)}, u32[]{:S(2)}) collective-permute-start(bf16[704,128]{1,0:T(8,128)(2,1)} %get-tuple-element.429), channel_id=1, source_target_pairs={{0,7},{16,23},{32,39},{48,55},{64,71},{80,87},{96,103},{112,119}} | collective-permute-start | bytes 540680 | tf_op jit(solution)/shard_map/ppermute | solution.py:400
  426.3 21.0 %collective-permute-start.48 = (bf16[704,128]{1,0:T(8,128)(2,1)}, bf16[704,128]{1,0:T(8,128)(2,1)}, u32[]{:S(2)}, u32[]{:S(2)}) collective-permute-start(bf16[704,128]{1,0:T(8,128)(2,1)} %get-tuple-element.428), channel_id=1, source_target_pairs={{0,6},{16,22},{32,38},{48,54},{64,70},{80,86},{96,102},{112,118}} | collective-permute-start | bytes 540680 | tf_op jit(solution)/shard_map/ppermute | solution.py:400
  439.4 26.7 %collective-permute-start.49 = (bf16[704,128]{1,0:T(8,128)(2,1)}, bf16[704,128]{1,0:T(8,128)(2,1)}, u32[]{:S(2)}, u32[]{:S(2)}) collective-permute-start(bf16[704,128]{1,0:T(8,128)(2,1)} %get-tuple-element.427), channel_id=1, source_target_pairs={{0,5},{16,21},{32,37},{48,53},{64,69},{80,85},{96,101},{112,117}} | collective-permute-start | bytes 540680 | tf_op jit(solution)/shard_map/ppermute | solution.py:400
  441.4 25.7 %collective-permute-start.50 = (bf16[704,128]{1,0:T(8,128)(2,1)}, bf16[704,128]{1,0:T(8,128)(2,1)}, u32[]{:S(2)}, u32[]{:S(2)}) collective-permute-start(bf16[704,128]{1,0:T(8,128)(2,1)} %get-tuple-element.426), channel_id=1, source_target_pairs={{0,4},{16,20},{32,36},{48,52},{64,68},{80,84},{96,100},{112,116}} | collective-permute-start | bytes 540680 | tf_op jit(solution)/shard_map/ppermute | solution.py:400
  443.4 23.7 %collective-permute-start.51 = (bf16[704,128]{1,0:T(8,128)(2,1)}, bf16[704,128]{1,0:T(8,128)(2,1)}, u32[]{:S(2)}, u32[]{:S(2)}) collective-permute-start(bf16[704,128]{1,0:T(8,128)(2,1)} %get-tuple-element.425), channel_id=1, source_target_pairs={{0,3},{16,19},{32,35},{48,51},{64,67},{80,83},{96,99},{112,115}} | collective-permute-start | bytes 540680 | tf_op jit(solution)/shard_map/ppermute | solution.py:400
  445.3 21.7 %collective-permute-start.52 = (bf16[704,128]{1,0:T(8,128)(2,1)}, bf16[704,128]{1,0:T(8,128)(2,1)}, u32[]{:S(2)}, u32[]{:S(2)}) collective-permute-start(bf16[704,128]{1,0:T(8,128)(2,1)} %get-tuple-element.424), channel_id=1, source_target_pairs={{0,2},{16,18},{32,34},{48,50},{64,66},{80,82},{96,98},{112,114}} | collective-permute-start | bytes 540680 | tf_op jit(solution)/shard_map/ppermute | solution.py:400
  484.0 20.3 %collective-permute-start.61 = (bf16[704,128]{1,0:T(8,128)(2,1)S(1)}, bf16[704,128]{1,0:T(8,128)(2,1)S(1)}, u32[]{:S(2)}, u32[]{:S(2)}) collective-permute-start(bf16[704,128]{1,0:T(8,128)(2,1)S(1)} %select_select_fusion.1), channel_id=1, source_target_pairs={{0,8},{1,9},{2,10},{3,11},{4,12},{5,13},{6,14},{7,15},{8,0},{9,1},... | collective-permute-start | bytes 540680 | tf_op jit(solution)/shard_map/ppermute | solution.py:405
  486.0 20.4 %collective-permute-start.63 = (bf16[704,128]{1,0:T(8,128)(2,1)S(1)}, bf16[704,128]{1,0:T(8,128)(2,1)S(1)}, u32[]{:S(2)}, u32[]{:S(2)}) collective-permute-start(bf16[704,128]{1,0:T(8,128)(2,1)S(1)} %select_select_fusion.1), channel_id=1, source_target_pairs={{0,10},{1,11},{2,8},{3,9},{4,14},{5,15},{6,12},{7,13},{8,2},{9,3},... | collective-permute-start | bytes 540680 | tf_op jit(solution)/shard_map/ppermute | solution.py:405
  (52 other events, 1214.5 us)

commit v3 on v2

--- a/solution.py
+++ b/solution.py
@@ -53,17 +53,12 @@
             (((1,), (1,)), ((), ())),
             preferred_element_type=jnp.float32,
         ).astype(jnp.bfloat16)
-        for t in range(OWN_TILES):
+        for t in reversed(range(OWN_TILES)):
             tile = jnp.dot(
                 perm[t], moved[t * TILE : (t + 1) * TILE], preferred_element_type=jnp.float32
             )
-            if ranks == RANKS:
-                out_ref[owner[t], 0, rank[t], 0] = tile.astype(jnp.bfloat16)
-            else:
-
-                @pl.when(rank[t] == 0)
-                def _():
-                    out_ref[owner[t], 0, 0, 0] = tile.astype(jnp.bfloat16)
+            place = rank[t] if ranks == RANKS else 0
+            out_ref[owner[t], 0, place, 0] = tile.astype(jnp.bfloat16)
 
 
 def pack(first, width, ranks, src, present, owner, rank, children, col_within, row_within):
@@ -297,8 +292,8 @@
     )(bins, pivots, arrived)
 
 
-def update_kernel(n_chunks, is_first, *refs):
-    fronts, (panel_ref, pivot_ref, row_ref, linv_ref, uinv_ref, out_ref, upper) = (
+def update_kernel(n_chunks, my_pcol, *refs):
+    fronts, (low_ref, high_ref, pivot_ref, row_ref, linv_ref, uinv_ref, out_ref, upper) = (
         refs[:n_chunks],
         refs[n_chunks:],
     )
@@ -313,15 +308,15 @@
             linv_ref[...], block.astype(jnp.bfloat16), preferred_element_type=jnp.float32
         ).astype(jnp.bfloat16)
 
+    panel = jnp.concatenate([low_ref[0, 0], high_ref[0, 0]], axis=0)
     lower = (
-        jnp.dot(panel_ref[...], uinv_ref[...], preferred_element_type=jnp.float32)
+        jnp.dot(panel, uinv_ref[...], preferred_element_type=jnp.float32)
         .astype(jnp.bfloat16)
         .astype(jnp.float32)
     )
     rows = lax.broadcasted_iota(jnp.int32, (ROW_BLOCK, TILE), 0) + step * ROW_BLOCK
     chosen = jnp.where(rows == row_ref[...], 1.0, 0.0)
     replaced = jnp.max(chosen, axis=1, keepdims=True)
-    kept = 1.0 - replaced
     factor = jnp.where(replaced > 0.0, chosen, -lower).astype(jnp.bfloat16)
     at = 0
     for k in range(n_chunks):
@@ -333,13 +328,20 @@
         out_ref[:, at : at + cols] = result.astype(jnp.bfloat16)
         at += cols
 
-    @pl.when(is_first[0] != 0)
+    @pl.when(my_pcol[0] == 0)
     def _():
         out_ref[:, 0:TILE] = lower.astype(jnp.bfloat16)
 
 
-def update(is_first, fronts, panel, pivots, rows, linv, uinv):
-    cols = SLOTS * TILE
+def update(my_pcol, fronts, panel, pivots, rows, linv, uinv):
+    cols, half = SLOTS * TILE, ROW_BLOCK // 2
+
+    def low(i, my_pcol):
+        return (i ^ my_pcol[0]) // 4, (i ^ my_pcol[0]) % 4, 0, 0
+
+    def high(i, my_pcol):
+        return (i ^ my_pcol[0]) % 4, (i ^ my_pcol[0]) // 4, 0, 0
+
     whole = lambda *shape: pl.BlockSpec(shape, lambda i, *a: (0,) * len(shape))
     return pl.pallas_call(
         functools.partial(update_kernel, len(fronts)),
@@ -351,7 +353,8 @@
                 pl.BlockSpec((ROW_BLOCK, f.shape[1]), lambda i, *a: (i, 0)) for f in fronts
             ]
             + [
-                pl.BlockSpec((ROW_BLOCK, TILE), lambda i, *a: (i, 0)),
+                pl.BlockSpec((1, 1, half, TILE), low),
+                pl.BlockSpec((1, 1, half, TILE), high),
                 whole(*pivots.shape),
                 whole(1, TILE),
                 whole(TILE, TILE),
@@ -366,7 +369,18 @@
             bytes_accessed=2 * LOCAL_ROWS * cols * 2,
             transcendentals=0,
         ),
-    )(is_first, *fronts, panel, pivots, rows, linv, uinv)
+    )(my_pcol, *fronts, *panel, pivots, rows, linv, uinv)
+
+
+def after(value, *others):
+    anywhere = pl.BlockSpec(memory_space=pl.ANY)
+    return pl.pallas_call(
+        lambda *refs: None,
+        out_shape=jax.ShapeDtypeStruct(value.shape, value.dtype),
+        in_specs=[anywhere] * (1 + len(others)),
+        out_specs=anywhere,
+        input_output_aliases={0: 0},
+    )(value, *others)
 
 
 def exchange(parts, axes):
@@ -393,18 +407,29 @@
     return here + there, places
 
 
-def spread_panel(panel, my_pcol):
-    pieces = panel.reshape(N_PCOL, LOCAL_ROWS // N_PCOL, TILE)
+def scatter_panel(panel, my_pcol):
+    pieces = panel.reshape(N_PCOL, ROW_BLOCK, TILE)
     piece = pieces[0]
     for q in range(1, N_PCOL):
         got = lax.ppermute(pieces[q], "pcol", [(0, q)])
         piece = jnp.where(my_pcol == q, got, piece)
-    whole = jnp.zeros_like(pieces)
-    whole = lax.dynamic_update_index_in_dim(whole, piece, my_pcol, 0)
-    for i in range(1, N_PCOL):
-        got = lax.ppermute(piece, "pcol", [(q, q ^ i) for q in range(N_PCOL)])
-        whole = lax.dynamic_update_index_in_dim(whole, got, my_pcol ^ i, 0)
-    return whole.reshape(LOCAL_ROWS, TILE)
+    return piece
+
+
+def gather_panel(piece):
+    def along(value, stride):
+        return jnp.stack(
+            [value]
+            + [
+                lax.ppermute(
+                    value, "pcol", [(q, q ^ (stride * i)) for q in range(N_PCOL)]
+                )
+                for i in range(1, 4)
+            ]
+        )
+
+    half = ROW_BLOCK // 2
+    return along(along(piece[:half], 1), 4), along(along(piece[half:], 4), 1)
 
 
 def on_device(
@@ -434,8 +459,16 @@
     owners = row_owner[:, 0]
     rank = jnp.sum(((owners[:, None] == owners[None, :]) & earlier).astype(jnp.int32), axis=1)
 
+    second = rank == 1
+    which = jnp.min(jnp.where(second, order, OWN_TILES - 1)).reshape(1)
+    col_line = col_within.reshape(n_src, 1, TILE)
+    sent = pack_second(src, present, which, children, col_within, row_within)
+    own = exchange(sent.reshape(N_PCOL, SLOTS, TILE, TILE), "pcol")
+    parts, places = gather_prow(own)
+
+    code = after(owners * FRONT_TILES + row_local, own)
     codes = jnp.pad(
-        (owners * FRONT_TILES + row_local)[None, :], ((0, 0), (0, TILE - OWN_TILES))
+        code[None, :], ((0, 0), (0, TILE - OWN_TILES))
     )
     codes = lax.all_to_all(
         jnp.broadcast_to(codes[None], (N_DEV, 8, TILE)),
@@ -450,8 +483,6 @@
     is_it = mine[:, None, :] & (nth[:, None, :] == want)
     bins = jnp.max(jnp.where(is_it, (codes % FRONT_TILES)[:, None, :], -1), axis=2)
 
-    second = rank == 1
-    which = jnp.min(jnp.where(second, order, OWN_TILES - 1)).reshape(1)
     owner_of = codes // FRONT_TILES
     again = jnp.sum(
         ((owner_of[:, :, None] == owner_of[:, None, :]) & earlier[None]).astype(jnp.int32), axis=2
@@ -465,13 +496,8 @@
     pivot_local = jnp.where(
         pivot_rows // LOCAL_ROWS == my_prow, pivot_rows % LOCAL_ROWS, -1
     ).astype(jnp.int32)
-    is_first = (my_pcol == 0).astype(jnp.int32).reshape(1)
+    pcol_line = my_pcol.astype(jnp.int32).reshape(1)
     pivot_line = pivot_local.reshape(1, TILE)
-    col_line = col_within.reshape(n_src, 1, TILE)
-
-    sent = pack_second(src, present, which, children, col_within, row_within)
-    own = exchange(sent.reshape(N_PCOL, SLOTS, TILE, TILE), "pcol")
-    parts, places = gather_prow(own)
     places = jnp.concatenate(
         [
             jnp.take(seconds, ((my_prow ^ flip) + 2 * shift) % N_PROW, axis=0)[
@@ -482,17 +508,23 @@
     )
 
     fronts, picks = {}, {}
-    panel = None
+    panel, ahead = None, parts[1:3]
     for first, width in CHUNKS:
         sent = pack(
             first, width, 1, src, present, owners, rank, children, col_line, row_within
         )
+        if ahead:
+            sent = after(sent, *ahead)
         arrived = exchange(sent.reshape(N_DEV, width, TILE, TILE), ("prow", "pcol"))
         fronts[first], picks[first] = sum_chunk(
             first, width, bins[:, 0], places, pivot_local, arrived, parts
         )
         if first == 0:
-            panel = spread_panel(fronts[first][:, :TILE], my_pcol)
+            piece = scatter_panel(fronts[first][:, :TILE], my_pcol)
+            panel = gather_panel(piece)
+            ahead = [arrived, *parts]
+        else:
+            ahead = [arrived, piece]
     fronts = [fronts[k] for k in sorted(fronts)]
     pivots = jnp.concatenate([picks[k] for k in sorted(picks)], axis=1)
     for bit in (1, 2):
@@ -503,7 +535,7 @@
 
     def narrow():
         return update(
-            is_first, fronts, panel, pivots, pivot_line, lower_inverse, upper_inverse
+            pcol_line, fronts, panel, pivots, pivot_line, lower_inverse, upper_inverse
         )
 
     def wide():
@@ -518,11 +550,11 @@
             front, picked = accumulate(width, bins.reshape(-1), pivot_local, arrived)
             fronts.append(front)
             picks.append(picked)
-        panel = spread_panel(fronts[0][:, :TILE], my_pcol)
+        panel = gather_panel(scatter_panel(fronts[0][:, :TILE], my_pcol))
         picked = jnp.concatenate(picks, axis=1)
         pivots = exchange(jnp.broadcast_to(picked[None], (N_PROW,) + picked.shape), "prow")
         return update(
-            is_first, fronts, panel, pivots, pivot_line, lower_inverse, upper_inverse
+            pcol_line, fronts, panel, pivots, pivot_line, lower_inverse, upper_inverse
         )
 
     return lax.cond(more, wide, narrow)

time: 564 us -> 513 us (0.910)
  starting transfers between devices: 166 us -> 101 us
  blocking collectives: 0 us -> 35.2 us
  Pallas kernels: 156 us -> 125 us
  waiting for transfers between devices: 201 us -> 223 us
  local copies, waits for them, and re-layouts: 28.8 us -> 10.4 us
    ppermute x30 -> x27, waiting for transfers between devices: 14.3 us -> 131 us  [the longest x15 78.1 us: scatter_panel(): got = lax.ppermute(pieces[q], 'pcol', [(0, q)])]
    ppermute x4, waiting for transfers between devices: 139 us -> 91.3 us  [shifted(): lax.ppermute(value, 'prow', [(p, (p + 2 * by) % N_PROW) for p in range(N_...]
    all_to_all x4 -> x3, waiting for transfers between devices: 46.7 us -> 0.01 us  [exchange(): return lax.all_to_all(parts, axes, split_axis=0, concat_axis=0, tiled=True)]
    ppermute x5, starting transfers between devices: 38.2 us -> 2.61 us  [gather_prow(): lax.ppermute(v, 'prow', [(p, p ^ 1) for p in range(N_PROW)])]
    all_to_all x0 -> x1, blocking collectives: none -> 35.2 us  [exchange(): return lax.all_to_all(parts, axes, split_axis=0, concat_axis=0, tiled=True)]
    pallas_call x3, Pallas kernels: 86.5 us -> 57.1 us  [pack(): pl.pallas_call(functools.partial(pack_kernel, first, ranks), out_shape=ja...]
    ppermute x30 -> x27, starting transfers between devices: 65.8 us -> 44.4 us  [the longest x15 28.9 us: scatter_panel(): got = lax.ppermute(pieces[q], 'pcol', [(0, q)])]
    dynamic_update_slice x16 -> x0, local copies, waits for them, and re-layouts: 13.4 us -> none  [the longest x15 13.3 us: spread_panel(): whole = lax.dynamic_update_index_in_dim(whole, got, my_pcol ^ i, 0)]
  transfers between devices with their start and end apart: 47 -> 43, of which waited for: 11 -> 11; matrix products, arithmetic and copies ran while one was open for 3% -> 3% of each run, Pallas kernels for 25% -> 18%
where the time goes in v3:
time: 513 us; the launch traced here: 509 us
  waiting for transfers between devices  223 us (43%)
  Pallas kernels  125 us (24%)
  starting transfers between devices  101 us (20%)
  blocking collectives  35.2 us (7%)
  other arithmetic  12.5 us (2%)
  local copies, waits for them, and re-layouts  10.4 us (2%)
    ppermute x4, waiting for transfers between devices, shifted(): lax.ppermute(value, 'prow', [(p, (p + 2 * by) % N_PROW) for p in range(N_...  91.3 us
    ppermute x15, waiting for transfers between devices, scatter_panel(): got = lax.ppermute(pieces[q], 'pcol', [(0, q)])  78.1 us
    pallas_call x3, Pallas kernels, pack(): pl.pallas_call(functools.partial(pack_kernel, first, ranks), out_shape=ja...  57.1 us
    ppermute x12, waiting for transfers between devices, along(): lax.ppermute(value, 'pcol', [(q, q ^ stride * i) for q in range(N_PCOL)])  52.6 us
    pallas_call x3, Pallas kernels, sum_chunk(): pl.pallas_call(functools.partial(sum_kernel, width, counts), out_shape=[j...  36.1 us
    all_to_all x1, blocking collectives, exchange(): return lax.all_to_all(parts, axes, split_axis=0, concat_axis=0, tiled=True)  35.2 us
    all_to_all x3, starting transfers between devices, exchange(): return lax.all_to_all(parts, axes, split_axis=0, concat_axis=0, tiled=True)  29.8 us
    ppermute x15, starting transfers between devices, scatter_panel(): got = lax.ppermute(pieces[q], 'pcol', [(0, q)])  28.9 us
  transfers between devices with their start and end apart: 43, of which 11 were waited for; matrix products, arithmetic and copies ran while one was open for 3% of the time, Pallas kernels for 18%

profile of v3, /device:TPU:1, one launch (start us, length us, event | category | flops | bytes accessed | tf_op | source)
XLA Modules:
  0.0 508.9 jit_solution(3529728133797224007)
XLA Ops:
  3.7 15.0 %shard_map.93 = bf16[64,128,128]{2,1,0:T(8,128)(2,1)} custom-call(s32[64]{0:T(128)S(1)} %get-tuple-element.152.src, s32[64]{0:T(128)S(1)} %get-tuple-element.151.present, s32[1]{0:T(128)} %bitcast.21.which, bf16[1024,6144]{1,0:T(8,128)(2,1)} %x_ref.7, s32[48,128]{1,0:T(8,128)} %fusion.25.cw_ref, s32[8,128]{1,0:T(8,128)} %rw_ref.7), custom_call_target="tpu_custom_call" | custom-call | flops 536870912 | bytes 4194304 | tf_op jit(solution)/shard_map/pallas_call | solution.py:114
  18.7 35.2 %all_to_all.41.refs_1_.refs_0_.refs_2_ = bf16[16,4,128,128]{3,2,1,0:T(8,128)(2,1)S(1)} all-to-all(bf16[16,4,128,128]{3,2,1,0:T(8,128)(2,1)} %bitcast.123), channel_id=1, replica_groups=mesh['prow'=8,'pcol'=16] {'pcol'}, dimensions={0} | all-to-all | bytes 4194304 | tf_op jit(solution)/shard_map/all_to_all | solution.py:387
  56.6 14.4 %shard_map.95.refs_0_ = bf16[8,16,1,1,128,128]{5,4,3,2,1,0:T(8,128)(2,1)} custom-call(s32[64]{0:T(128)S(1)} %get-tuple-element.152.src, s32[64]{0:T(128)S(1)} %get-tuple-element.151.present, s32[8]{0:T(128)S(1)} %bitcast.146, s32[8]{0:T(128)S(1)} %convert_reduce_fusion.4.rank, bf16[1024,6144]{1,0:T(8,128)(2,1)} %x_ref.7, s32[48,1,128]{2,1,0:T(1,128)S(1)} %bitcast.124, ...), custom_call_target="tpu_custom_call" | custom-call | flops 1073741824 | bytes 12582912 | tf_op jit(solution)/shard_map/pallas_call | solution.py:68
  71.0 28.7 %collective-permute-done.27.refs_1_.refs_3_ = bf16[16,4,128,128]{3,2,1,0:T(8,128)(2,1)} collective-permute-done((bf16[16,4,128,128]{3,2,1,0:T(8,128)(2,1)S(1)}, bf16[16,4,128,128]{3,2,1,0:T(8,128)(2,1)}, u32[]{:S(2)}, u32[]{:S(2)}) %collective-permute-start.27) | collective-permute-done | bytes 2097184 | tf_op jit(solution)/shard_map/ppermute | solution.py:392
  99.7 10.7 %all-to-all-start.6 = ((bf16[128,1,128,128]{3,2,1,0:T(8,128)(2,1)}), bf16[128,1,128,128]{3,2,1,0:T(8,128)(2,1)}, u32[]{:S(2)}, u32[]{:S(2)}) async-start(bf16[128,1,128,128]{3,2,1,0:T(8,128)(2,1)} %bitcast.120), calls=%async_computation.6 | async-start | bytes 8388608 | tf_op jit(solution)/shard_map/all_to_all | solution.py:387
  117.6 62.6 %collective-permute-done.29.refs_3_.refs_5_ = bf16[8,4,128,128]{3,2,1,0:T(8,128)(2,1)S(1)} collective-permute-done((bf16[8,4,128,128]{3,2,1,0:T(8,128)(2,1)S(1)}, bf16[8,4,128,128]{3,2,1,0:T(8,128)(2,1)S(1)}, u32[]{:S(2)}, u32[]{:S(2)}) %collective-permute-start.29) | collective-permute-done | bytes 1048608 | tf_op jit(solution)/shard_map/ppermute | solution.py:392
  183.0 9.7 %all-to-all-start.5 = ((s32[128,8,128]{2,1,0:T(8,128)}), s32[128,8,128]{2,1,0:T(8,128)}, u32[]{:S(2)}, u32[]{:S(2)}) async-start(s32[128,8,128]{2,1,0:T(8,128)} %broadcast_in_dim.89), calls=%async_computation.5 | async-start | bytes 1048576 | tf_op jit(solution)/shard_map/all_to_all | solution.py:473
  192.7 27.6 %shard_map.99.refs_0_ = bf16[8,16,1,2,128,128]{5,4,3,2,1,0:T(8,128)(2,1)} custom-call(s32[64]{0:T(128)S(1)} %get-tuple-element.152.src, s32[64]{0:T(128)S(1)} %get-tuple-element.151.present, s32[8]{0:T(128)S(1)} %bitcast.147, s32[8]{0:T(128)S(1)} %convert_reduce_fusion.4.rank, bf16[1024,6144]{1,0:T(8,128)(2,1)} %x_ref.7, s32[48,1,128]{2,1,0:T(1,128)S(1)} %bitcast.125, ...), custom_call_target="tpu_custom_call" | custom-call | flops 2147483648 | bytes 25165824 | tf_op jit(solution)/shard_map/pallas_call | solution.py:68
  220.4 9.2 %all-to-all-start.7 = ((bf16[128,2,128,128]{3,2,1,0:T(8,128)(2,1)}), bf16[128,2,128,128]{3,2,1,0:T(8,128)(2,1)}, u32[]{:S(2)}, u32[]{:S(2)}) async-start(bf16[128,2,128,128]{3,2,1,0:T(8,128)(2,1)} %bitcast.117), calls=%async_computation.7 | async-start | bytes 16777216 | tf_op jit(solution)/shard_map/all_to_all | solution.py:387
  232.6 10.0 %shard_map.97 = (bf16[11264,128]{1,0:T(8,128)(2,1)S(1)}, bf16[128,128]{1,0:T(8,128)(2,1)}) custom-call(s32[128]{0:T(128)} %slice_bitcast_fusion.2.bins, s32[128]{0:T(128)} %concatenate.9.seconds, s32[128]{0:T(128)S(1)} %compare_select_fusion.pivots, bf16[128,1,128,128]{3,2,1,0:T(8,128)(2,1)} %all-to-all-done.6.x_ref.refs_1_, ...), custom_call_target="tpu_custom_call" | custom-call | flops 4194304 | bytes 11272192 | tf_op jit(solution)/shard_map/pallas_call | solution.py:185
  243.6 7.5 %collective-permute-start.36 = (bf16[704,128]{1,0:T(8,128)(2,1)S(1)}, bf16[704,128]{1,0:T(8,128)(2,1)S(1)}, u32[]{:S(2)}, u32[]{:S(2)}) collective-permute-start(bf16[704,128]{1,0:T(8,128)(2,1)S(1)} %get-tuple-element.190), channel_id=1, source_target_pairs={{0,15},{16,31},{32,47},{48,63},{64,79},{80,95},{96,111},{112,127}} | collective-permute-start | bytes 540680 | tf_op jit(solution)/shard_map/ppermute | solution.py:414
  256.3 67.0 %collective-permute-done.36 = bf16[704,128]{1,0:T(8,128)(2,1)S(1)} collective-permute-done((bf16[704,128]{1,0:T(8,128)(2,1)S(1)}, bf16[704,128]{1,0:T(8,128)(2,1)S(1)}, u32[]{:S(2)}, u32[]{:S(2)}) %collective-permute-start.36) | collective-permute-done | bytes 180256 | tf_op jit(solution)/shard_map/ppermute | solution.py:414
  324.6 6.0 %collective-permute-done.37 = bf16[704,128]{1,0:T(8,128)(2,1)S(1)} collective-permute-done((bf16[704,128]{1,0:T(8,128)(2,1)S(1)}, bf16[704,128]{1,0:T(8,128)(2,1)S(1)}, u32[]{:S(2)}, u32[]{:S(2)}) %collective-permute-start.37) | collective-permute-done | bytes 180256 | tf_op jit(solution)/shard_map/ppermute | solution.py:414
  351.5 15.1 %shard_map.98.refs_0_ = bf16[8,16,1,1,128,128]{5,4,3,2,1,0:T(8,128)(2,1)} custom-call(s32[64]{0:T(128)S(1)} %get-tuple-element.152.src, s32[64]{0:T(128)S(1)} %get-tuple-element.151.present, s32[8]{0:T(128)S(1)} %bitcast.148, s32[8]{0:T(128)S(1)} %convert_reduce_fusion.4.rank, bf16[1024,6144]{1,0:T(8,128)(2,1)} %x_ref.7, s32[48,1,128]{2,1,0:T(1,128)S(1)} %bitcast.126, ...), custom_call_target="tpu_custom_call" | custom-call | flops 1073741824 | bytes 12582912 | tf_op jit(solution)/shard_map/pallas_call | solution.py:68
  367.7 9.9 %all-to-all-start.8 = ((bf16[128,1,128,128]{3,2,1,0:T(8,128)(2,1)}), bf16[128,1,128,128]{3,2,1,0:T(8,128)(2,1)}, u32[]{:S(2)}, u32[]{:S(2)}) async-start(bf16[128,1,128,128]{3,2,1,0:T(8,128)(2,1)} %bitcast.119), calls=%async_computation.8 | async-start | bytes 8388608 | tf_op jit(solution)/shard_map/all_to_all | solution.py:387
  382.1 44.5 %collective-permute-done.57 = bf16[352,128]{1,0:T(8,128)(2,1)S(1)} collective-permute-done((bf16[352,128]{1,0:T(8,128)(2,1)S(1)}, bf16[352,128]{1,0:T(8,128)(2,1)S(1)}, u32[]{:S(2)}, u32[]{:S(2)}) %collective-permute-start.57) | collective-permute-done | bytes 90144 | tf_op jit(solution)/shard_map/ppermute | solution.py:424
  426.6 3.3 collective-permute-done.58
  433.1 2.6 collective-permute-start.52
  437.7 15.0 %shard_map.103 = (bf16[11264,256]{1,0:T(8,128)(2,1)}, bf16[128,256]{1,0:T(8,128)(2,1)}) custom-call(s32[128]{0:T(128)} %slice_bitcast_fusion.2.bins, s32[128]{0:T(128)} %concatenate.9.seconds, s32[128]{0:T(128)S(1)} %compare_select_fusion.pivots, bf16[128,2,128,128]{3,2,1,0:T(8,128)(2,1)} %all-to-all-done.7.refs_1_.x_ref, bf16[16,4,128,128]{3,2,1,0:T(8,128)(2,1)} %copy-done, ...), custom_call_target="tpu_custom_call" | custom-call | flops 8388608 | bytes 22544384 | tf_op jit(solution)/shard_map/pallas_call | solution.py:185
  452.7 11.2 %shard_map.102 = (bf16[11264,128]{1,0:T(8,128)(2,1)}, bf16[128,128]{1,0:T(8,128)(2,1)}) custom-call(s32[128]{0:T(128)} %slice_bitcast_fusion.2.bins, s32[128]{0:T(128)} %concatenate.9.seconds, s32[128]{0:T(128)S(1)} %compare_select_fusion.pivots, bf16[128,1,128,128]{3,2,1,0:T(8,128)(2,1)} %all-to-all-done.8.x_ref, bf16[16,4,128,128]{3,2,1,0:T(8,128)(2,1)} %copy-done, ...), custom_call_target="tpu_custom_call" | custom-call | flops 4194304 | bytes 11272192 | tf_op jit(solution)/shard_map/pallas_call | solution.py:185
  480.8 4.9 collective-permute-start.65
  487.9 2.6 collective-permute-done.56
  492.0 16.8 %conditional.1 = (bf16[11264,512]{1,0:T(8,128)(2,1)}) conditional(s32[]{:T(128)} %convert_element_type.22, (s32[1]{0:T(128)}, bf16[11264,128]{1,0:T(8,128)(2,1)S(1)}, bf16[11264,128]{1,0:T(8,128)(2,1)}, bf16[11264,256]{1,0:T(8,128)(2,1)}, bf16[4,4,352,128]{3,2,1,0:T(8,128)(2,1)S(1)}, /*index=5*/bf16[4,4,352,128]{3,2,1,0:T(8,128)(2,1)S(1)}, ...), branch_computations={%region_10.12_spmd, %region_11.13_spmd} | conditional | flops 6164389888 | bytes 266769728 | solution.py:560
  492.1 16.8 %branch_0_fun.1 = bf16[11264,512]{1,0:T(8,128)(2,1)} custom-call(s32[1]{0:T(128)} %get-tuple-element.56.my_pcol, bf16[11264,128]{1,0:T(8,128)(2,1)S(1)} %get-tuple-element.58.refs_0_, bf16[11264,128]{1,0:T(8,128)(2,1)} %get-tuple-element.59.refs_1_, bf16[11264,256]{1,0:T(8,128)(2,1)} %get-tuple-element.60.refs_2_, ...), custom_call_target="tpu_custom_call" | custom-call | flops 1845493760 | bytes 23068672 | tf_op jit(solution)/shard_map/cond/branch_0_fun/pallas_call | solution.py:346
  (181 shorter events, 78.0 us)
Async XLA Ops:
  53.9 45.7 %collective-permute-start.27 = (bf16[16,4,128,128]{3,2,1,0:T(8,128)(2,1)S(1)}, bf16[16,4,128,128]{3,2,1,0:T(8,128)(2,1)}, u32[]{:S(2)}, u32[]{:S(2)}) collective-permute-start(bf16[16,4,128,128]{3,2,1,0:T(8,128)(2,1)S(1)} %all_to_all.41.refs_1_.refs_0_.refs_2_), channel_id=1, source_target_pairs={{0,32},{16,48},{32,64},{48,80},{64,96},{80,112},{96,0},{112,16},{1... | collective-permute-start | bytes 6291464 | tf_op jit(solution)/shard_map/ppermute | solution.py:392
  55.1 44.5 %collective-permute-start.28 = (bf16[16,4,128,128]{3,2,1,0:T(8,128)(2,1)S(1)}, bf16[16,4,128,128]{3,2,1,0:T(8,128)(2,1)}, u32[]{:S(2)}, u32[]{:S(2)}) collective-permute-start(bf16[16,4,128,128]{3,2,1,0:T(8,128)(2,1)S(1)} %all_to_all.41.refs_1_.refs_0_.refs_2_), channel_id=1, source_target_pairs={{0,96},{16,112},{32,0},{48,16},{64,32},{80,48},{96,64},{112,80},{1... | collective-permute-start | bytes 6291464 | tf_op jit(solution)/shard_map/ppermute | solution.py:392
  99.7 82.5 %all-to-all-start.6 = ((bf16[128,1,128,128]{3,2,1,0:T(8,128)(2,1)}), bf16[128,1,128,128]{3,2,1,0:T(8,128)(2,1)}, u32[]{:S(2)}, u32[]{:S(2)}) async-start(bf16[128,1,128,128]{3,2,1,0:T(8,128)(2,1)} %bitcast.120), calls=%async_computation.6 | async-start | bytes 8388608 | tf_op jit(solution)/shard_map/all_to_all | solution.py:387
  110.4 110.0 %collective-permute-start.31 = (bf16[16,4,128,128]{3,2,1,0:T(8,128)(2,1)S(1)}, bf16[16,4,128,128]{3,2,1,0:T(8,128)(2,1)}, u32[]{:S(2)}, u32[]{:S(2)}) collective-permute-start(bf16[16,4,128,128]{3,2,1,0:T(8,128)(2,1)S(1)} %all_to_all.41.refs_1_.refs_0_.refs_2_), channel_id=1, source_target_pairs={{0,16},{16,0},{32,48},{48,32},{64,80},{80,64},{96,112},{112,96},{1... | collective-permute-start | bytes 6291464 | tf_op jit(solution)/shard_map/ppermute | solution.py:399
  112.9 67.3 %collective-permute-start.29 = (bf16[8,4,128,128]{3,2,1,0:T(8,128)(2,1)S(1)}, bf16[8,4,128,128]{3,2,1,0:T(8,128)(2,1)S(1)}, u32[]{:S(2)}, u32[]{:S(2)}) collective-permute-start(bf16[8,4,128,128]{3,2,1,0:T(8,128)(2,1)S(1)} %slice.218), channel_id=1, source_target_pairs={{0,32},{16,48},{32,64},{48,80},{64,96},{80,112},{96,0},{112,16},{1... | collective-permute-start | bytes 3145736 | tf_op jit(solution)/shard_map/ppermute | solution.py:392
  114.9 66.0 %collective-permute-start.30 = (bf16[8,4,128,128]{3,2,1,0:T(8,128)(2,1)S(1)}, bf16[8,4,128,128]{3,2,1,0:T(8,128)(2,1)}, u32[]{:S(2)}, u32[]{:S(2)}) collective-permute-start(bf16[8,4,128,128]{3,2,1,0:T(8,128)(2,1)S(1)} %slice.219), channel_id=1, source_target_pairs={{0,96},{16,112},{32,0},{48,16},{64,32},{80,48},{96,64},{112,80},{1... | collective-permute-start | bytes 3145736 | tf_op jit(solution)/shard_map/ppermute | solution.py:392
  117.0 103.4 %collective-permute-start.32 = (bf16[16,4,128,128]{3,2,1,0:T(8,128)(2,1)}, bf16[16,4,128,128]{3,2,1,0:T(8,128)(2,1)}, u32[]{:S(2)}, u32[]{:S(2)}) collective-permute-start(bf16[16,4,128,128]{3,2,1,0:T(8,128)(2,1)} %collective-permute-done.27.refs_1_.refs_3_), channel_id=1, source_target_pairs={{0,16},{16,0},{32,48},{48,32},{64,80},{80,64},{96,112},{112,96},{1... | collective-permute-start | bytes 6291464 | tf_op jit(solution)/shard_map/ppermute | solution.py:399
  117.6 102.8 %collective-permute-start.33 = (bf16[16,4,128,128]{3,2,1,0:T(8,128)(2,1)}, bf16[16,4,128,128]{3,2,1,0:T(8,128)(2,1)}, u32[]{:S(2)}, u32[]{:S(2)}) collective-permute-start(bf16[16,4,128,128]{3,2,1,0:T(8,128)(2,1)} %collective-permute-done.28.refs_2_.refs_4_), channel_id=1, source_target_pairs={{0,16},{16,0},{32,48},{48,32},{64,80},{80,64},{96,112},{112,96},{1... | collective-permute-start | bytes 6291464 | tf_op jit(solution)/shard_map/ppermute | solution.py:399
  180.2 40.2 %collective-permute-start.34 = (bf16[8,4,128,128]{3,2,1,0:T(8,128)(2,1)S(1)}, bf16[8,4,128,128]{3,2,1,0:T(8,128)(2,1)}, u32[]{:S(2)}, u32[]{:S(2)}) collective-permute-start(bf16[8,4,128,128]{3,2,1,0:T(8,128)(2,1)S(1)} %collective-permute-done.29.refs_3_.refs_5_), channel_id=1, source_target_pairs={{0,16},{16,0},{32,48},{48,32},{64,80},{80,64},{96,112},{112,96},{1... | collective-permute-start | bytes 3145736 | tf_op jit(solution)/shard_map/ppermute | solution.py:399
  180.9 39.5 %collective-permute-start.35 = (bf16[8,4,128,128]{3,2,1,0:T(8,128)(2,1)}, bf16[8,4,128,128]{3,2,1,0:T(8,128)(2,1)}, u32[]{:S(2)}, u32[]{:S(2)}) collective-permute-start(bf16[8,4,128,128]{3,2,1,0:T(8,128)(2,1)} %collective-permute-done.30.refs_4_.refs_6_), channel_id=1, source_target_pairs={{0,16},{16,0},{32,48},{48,32},{64,80},{80,64},{96,112},{112,96},{1... | collective-permute-start | bytes 3145736 | tf_op jit(solution)/shard_map/ppermute | solution.py:399
  183.0 37.4 %all-to-all-start.5 = ((s32[128,8,128]{2,1,0:T(8,128)}), s32[128,8,128]{2,1,0:T(8,128)}, u32[]{:S(2)}, u32[]{:S(2)}) async-start(s32[128,8,128]{2,1,0:T(8,128)} %broadcast_in_dim.89), calls=%async_computation.5 | async-start | bytes 1048576 | tf_op jit(solution)/shard_map/all_to_all | solution.py:473
  220.4 147.3 %all-to-all-start.7 = ((bf16[128,2,128,128]{3,2,1,0:T(8,128)(2,1)}), bf16[128,2,128,128]{3,2,1,0:T(8,128)(2,1)}, u32[]{:S(2)}, u32[]{:S(2)}) async-start(bf16[128,2,128,128]{3,2,1,0:T(8,128)(2,1)} %bitcast.117), calls=%async_computation.7 | async-start | bytes 16777216 | tf_op jit(solution)/shard_map/all_to_all | solution.py:387
  243.6 79.7 %collective-permute-start.36 = (bf16[704,128]{1,0:T(8,128)(2,1)S(1)}, bf16[704,128]{1,0:T(8,128)(2,1)S(1)}, u32[]{:S(2)}, u32[]{:S(2)}) collective-permute-start(bf16[704,128]{1,0:T(8,128)(2,1)S(1)} %get-tuple-element.190), channel_id=1, source_target_pairs={{0,15},{16,31},{32,47},{48,63},{64,79},{80,95},{96,111},{112,127}} | collective-permute-start | bytes 540680 | tf_op jit(solution)/shard_map/ppermute | solution.py:414
  251.1 79.5 %collective-permute-start.37 = (bf16[704,128]{1,0:T(8,128)(2,1)S(1)}, bf16[704,128]{1,0:T(8,128)(2,1)S(1)}, u32[]{:S(2)}, u32[]{:S(2)}) collective-permute-start(bf16[704,128]{1,0:T(8,128)(2,1)S(1)} %get-tuple-element.189), channel_id=1, source_target_pairs={{0,14},{16,30},{32,46},{48,62},{64,78},{80,94},{96,110},{112,126}} | collective-permute-start | bytes 540680 | tf_op jit(solution)/shard_map/ppermute | solution.py:414
  252.4 82.0 %collective-permute-start.38 = (bf16[704,128]{1,0:T(8,128)(2,1)S(1)}, bf16[704,128]{1,0:T(8,128)(2,1)S(1)}, u32[]{:S(2)}, u32[]{:S(2)}) collective-permute-start(bf16[704,128]{1,0:T(8,128)(2,1)S(1)} %get-tuple-element.188), channel_id=1, source_target_pairs={{0,13},{16,29},{32,45},{48,61},{64,77},{80,93},{96,109},{112,125}} | collective-permute-start | bytes 540680 | tf_op jit(solution)/shard_map/ppermute | solution.py:414
  253.7 84.6 %collective-permute-start.39 = (bf16[704,128]{1,0:T(8,128)(2,1)S(1)}, bf16[704,128]{1,0:T(8,128)(2,1)S(1)}, u32[]{:S(2)}, u32[]{:S(2)}) collective-permute-start(bf16[704,128]{1,0:T(8,128)(2,1)S(1)} %get-tuple-element.187), channel_id=1, source_target_pairs={{0,12},{16,28},{32,44},{48,60},{64,76},{80,92},{96,108},{112,124}} | collective-permute-start | bytes 540680 | tf_op jit(solution)/shard_map/ppermute | solution.py:414
  255.0 84.6 %collective-permute-start.40 = (bf16[704,128]{1,0:T(8,128)(2,1)S(1)}, bf16[704,128]{1,0:T(8,128)(2,1)S(1)}, u32[]{:S(2)}, u32[]{:S(2)}) collective-permute-start(bf16[704,128]{1,0:T(8,128)(2,1)S(1)} %get-tuple-element.186), channel_id=1, source_target_pairs={{0,11},{16,27},{32,43},{48,59},{64,75},{80,91},{96,107},{112,123}} | collective-permute-start | bytes 540680 | tf_op jit(solution)/shard_map/ppermute | solution.py:414
  367.7 85.0 %all-to-all-start.8 = ((bf16[128,1,128,128]{3,2,1,0:T(8,128)(2,1)}), bf16[128,1,128,128]{3,2,1,0:T(8,128)(2,1)}, u32[]{:S(2)}, u32[]{:S(2)}) async-start(bf16[128,1,128,128]{3,2,1,0:T(8,128)(2,1)} %bitcast.119), calls=%async_computation.8 | async-start | bytes 8388608 | tf_op jit(solution)/shard_map/all_to_all | solution.py:387
  378.3 48.3 %collective-permute-start.57 = (bf16[352,128]{1,0:T(8,128)(2,1)S(1)}, bf16[352,128]{1,0:T(8,128)(2,1)S(1)}, u32[]{:S(2)}, u32[]{:S(2)}) collective-permute-start(bf16[352,128]{1,0:T(8,128)(2,1)S(1)} %get-tuple-element.197), channel_id=1, source_target_pairs={{0,4},{1,5},{2,6},{3,7},{4,0},{5,1},{6,2},{7,3},{8,12},{9,13},{10,... | collective-permute-start | bytes 270344 | tf_op jit(solution)/shard_map/ppermute | solution.py:424
  379.7 50.2 %collective-permute-start.58 = (bf16[352,128]{1,0:T(8,128)(2,1)S(1)}, bf16[352,128]{1,0:T(8,128)(2,1)S(1)}, u32[]{:S(2)}, u32[]{:S(2)}) collective-permute-start(bf16[352,128]{1,0:T(8,128)(2,1)S(1)} %get-tuple-element.197), channel_id=1, source_target_pairs={{0,8},{1,9},{2,10},{3,11},{4,12},{5,13},{6,14},{7,15},{8,0},{9,1},... | collective-permute-start | bytes 270344 | tf_op jit(solution)/shard_map/ppermute | solution.py:424
  382.1 47.8 %collective-permute-start.59 = (bf16[352,128]{1,0:T(8,128)(2,1)S(1)}, bf16[352,128]{1,0:T(8,128)(2,1)S(1)}, u32[]{:S(2)}, u32[]{:S(2)}) collective-permute-start(bf16[352,128]{1,0:T(8,128)(2,1)S(1)} %get-tuple-element.197), channel_id=1, source_target_pairs={{0,12},{1,13},{2,14},{3,15},{4,8},{5,9},{6,10},{7,11},{8,4},{9,5},... | collective-permute-start | bytes 270344 | tf_op jit(solution)/shard_map/ppermute | solution.py:424
  430.7 39.0 %collective-permute-start.60 = (bf16[4,352,128]{2,1,0:T(8,128)(2,1)}, bf16[4,352,128]{2,1,0:T(8,128)(2,1)}, u32[]{:S(2)}, u32[]{:S(2)}) collective-permute-start(bf16[4,352,128]{2,1,0:T(8,128)(2,1)} %get-tuple-element.192), channel_id=1, source_target_pairs={{0,1},{1,0},{2,3},{3,2},{4,5},{5,4},{6,7},{7,6},{8,9},{9,8},{10,11... | collective-permute-start | bytes 1081352 | tf_op jit(solution)/shard_map/ppermute | solution.py:424
  433.1 32.3 %collective-permute-start.52 = (bf16[352,128]{1,0:T(8,128)(2,1)}, bf16[352,128]{1,0:T(8,128)(2,1)}, u32[]{:S(2)}, u32[]{:S(2)}) collective-permute-start(bf16[352,128]{1,0:T(8,128)(2,1)} %get-tuple-element.198), channel_id=1, source_target_pairs={{0,2},{1,3},{2,0},{3,1},{4,6},{5,7},{6,4},{7,5},{8,10},{9,11},{10,... | collective-permute-start | bytes 270344 | tf_op jit(solution)/shard_map/ppermute | solution.py:424
  436.9 39.5 %collective-permute-start.61 = (bf16[4,352,128]{2,1,0:T(8,128)(2,1)}, bf16[4,352,128]{2,1,0:T(8,128)(2,1)}, u32[]{:S(2)}, u32[]{:S(2)}) collective-permute-start(bf16[4,352,128]{2,1,0:T(8,128)(2,1)} %get-tuple-element.192), channel_id=1, source_target_pairs={{0,2},{1,3},{2,0},{3,1},{4,6},{5,7},{6,4},{7,5},{8,10},{9,11},{10,... | collective-permute-start | bytes 1081352 | tf_op jit(solution)/shard_map/ppermute | solution.py:424
  (50 other events, 935.5 us)

commit v4 on v3

--- a/solution.py
+++ b/solution.py
@@ -337,10 +337,10 @@
     cols, half = SLOTS * TILE, ROW_BLOCK // 2
 
     def low(i, my_pcol):
-        return (i ^ my_pcol[0]) // 4, (i ^ my_pcol[0]) % 4, 0, 0
+        return (i // 4) ^ (my_pcol[0] % 4), i % 4, 0, 0
 
     def high(i, my_pcol):
-        return (i ^ my_pcol[0]) % 4, (i ^ my_pcol[0]) // 4, 0, 0
+        return (i // 4) ^ (my_pcol[0] // 4), i % 4, 0, 0
 
     whole = lambda *shape: pl.BlockSpec(shape, lambda i, *a: (0,) * len(shape))
     return pl.pallas_call(
@@ -387,15 +387,15 @@
     return lax.all_to_all(parts, axes, split_axis=0, concat_axis=0, tiled=True)
 
 
-def gather_prow(own):
+def gather_prow(own, first):
     def shifted(value, by):
         return lax.ppermute(value, "prow", [(p, (p + 2 * by) % N_PROW) for p in range(N_PROW)])
 
     half = own.shape[0] // 2
-    before, after = shifted(own, 1), shifted(own, -1)
-    far_low = shifted(before[:half], 1)
-    far_high = shifted(after[half:], -1)
-    here = [own, before, after, far_low, far_high]
+    left, right = shifted(own, 1), shifted(own, -1)
+    far_low = shifted(after(left[:half], *first), 1)
+    far_high = shifted(after(right[half:], *first), -1)
+    here = [own, left, right, far_low, far_high]
     there = [lax.ppermute(v, "prow", [(p, p ^ 1) for p in range(N_PROW)]) for v in here]
     named = [(0, 2 * half), (0, 2 * half), (0, 2 * half), (0, half), (half, half)]
     shifts = [0, -1, 1, -2, 2]
@@ -407,29 +407,33 @@
     return here + there, places
 
 
-def scatter_panel(panel, my_pcol):
-    pieces = panel.reshape(N_PCOL, ROW_BLOCK, TILE)
-    piece = pieces[0]
-    for q in range(1, N_PCOL):
-        got = lax.ppermute(pieces[q], "pcol", [(0, q)])
-        piece = jnp.where(my_pcol == q, got, piece)
-    return piece
-
-
-def gather_panel(piece):
+def from_first(values, mine, pairs):
+    result = values[0]
+    for i in range(1, 4):
+        result = jnp.where(mine == i, lax.ppermute(values[i], "pcol", pairs(i)), result)
+    return result
+
+
+def quarter_panel(panel, my_pcol):
+    blocks = panel.reshape(4, 4, ROW_BLOCK, TILE)
+    half = ROW_BLOCK // 2
+    low = from_first(blocks[:, :, :half], my_pcol % 4, lambda i: [(0, i)])
+    high = from_first(blocks[:, :, half:], my_pcol // 4, lambda i: [(0, 4 * i)])
+    return low, high
+
+
+def gather_panel(low, high, my_pcol):
+    low = from_first([low] * 4, my_pcol // 4, lambda i: [(k, 4 * i + k) for k in range(4)])
+    high = from_first([high] * 4, my_pcol % 4, lambda i: [(4 * k, 4 * k + i) for k in range(4)])
+
     def along(value, stride):
-        return jnp.stack(
-            [value]
-            + [
-                lax.ppermute(
-                    value, "pcol", [(q, q ^ (stride * i)) for q in range(N_PCOL)]
-                )
-                for i in range(1, 4)
-            ]
-        )
-
-    half = ROW_BLOCK // 2
-    return along(along(piece[:half], 1), 4), along(along(piece[half:], 4), 1)
+        moved = [
+            lax.ppermute(value, "pcol", [(q, q ^ (stride * i)) for q in range(N_PCOL)])
+            for i in range(1, 4)
+        ]
+        return jnp.stack([value] + moved)
+
+    return along(low, 1), along(high, 4)
 
 
 def on_device(
@@ -464,7 +468,13 @@
     col_line = col_within.reshape(n_src, 1, TILE)
     sent = pack_second(src, present, which, children, col_within, row_within)
     own = exchange(sent.reshape(N_PCOL, SLOTS, TILE, TILE), "pcol")
-    parts, places = gather_prow(own)
+    packed = {
+        first: pack(
+            first, width, 1, src, present, owners, rank, children, col_line, row_within
+        )
+        for first, width in CHUNKS
+    }
+    parts, places = gather_prow(own, [packed[first] for first, _ in CHUNKS[1:]])
 
     code = after(owners * FRONT_TILES + row_local, own)
     codes = jnp.pad(
@@ -508,29 +518,28 @@
     )
 
     fronts, picks = {}, {}
-    panel, ahead = None, parts[1:3]
+    panel, ahead = None, [*parts[1:3], codes]
     for first, width in CHUNKS:
-        sent = pack(
-            first, width, 1, src, present, owners, rank, children, col_line, row_within
-        )
-        if ahead:
-            sent = after(sent, *ahead)
+        sent = after(packed[first], *ahead)
         arrived = exchange(sent.reshape(N_DEV, width, TILE, TILE), ("prow", "pcol"))
         fronts[first], picks[first] = sum_chunk(
             first, width, bins[:, 0], places, pivot_local, arrived, parts
         )
         if first == 0:
-            piece = scatter_panel(fronts[first][:, :TILE], my_pcol)
-            panel = gather_panel(piece)
-            ahead = [arrived, *parts]
+            quarters = quarter_panel(fronts[first][:, :TILE], my_pcol)
+            panel = gather_panel(*quarters, my_pcol)
+            ahead = quarters
         else:
-            ahead = [arrived, piece]
+            ahead = [arrived, *panel]
     fronts = [fronts[k] for k in sorted(fronts)]
     pivots = jnp.concatenate([picks[k] for k in sorted(picks)], axis=1)
-    for bit in (1, 2):
-        pivots = pivots + lax.ppermute(pivots, "prow", [(p, p ^ bit) for p in range(N_PROW)])
+    pivots = pivots + lax.ppermute(pivots, "prow", [(p, p ^ 1) for p in range(N_PROW)])
     pivots = jnp.stack(
-        [pivots, lax.ppermute(pivots, "prow", [(p, p ^ 4) for p in range(N_PROW)])]
+        [pivots]
+        + [
+            lax.ppermute(pivots, "prow", [(p, p ^ bit) for p in range(N_PROW)])
+            for bit in (2, 4, 6)
+        ]
     )
 
     def narrow():
@@ -550,7 +559,7 @@
             front, picked = accumulate(width, bins.reshape(-1), pivot_local, arrived)
             fronts.append(front)
             picks.append(picked)
-        panel = gather_panel(scatter_panel(fronts[0][:, :TILE], my_pcol))
+        panel = gather_panel(*quarter_panel(fronts[0][:, :TILE], my_pcol), my_pcol)
         picked = jnp.concatenate(picks, axis=1)
         pivots = exchange(jnp.broadcast_to(picked[None], (N_PROW,) + picked.shape), "prow")
         return update(

time: 513 us -> 500 us (0.975)
  waiting for transfers between devices: 223 us -> 206 us
  starting transfers between devices: 101 us -> 111 us
    ppermute x4, waiting for transfers between devices: 91.3 us -> 18.6 us  [shifted(): lax.ppermute(value, 'prow', [(p, (p + 2 * by) % N_PROW) for p in range(N_...]
    ppermute x12 -> x6, waiting for transfers between devices: 52.6 us -> 15.4 us  [along(): lax.ppermute(value, 'pcol', [(q, q ^ stride * i) for q in range(N_PCOL)])]
    all_to_all x3, waiting for transfers between devices: 0.01 us -> 36.2 us  [exchange(): return lax.all_to_all(parts, axes, split_axis=0, concat_axis=0, tiled=True)]
    all_to_all x1, waiting for transfers between devices: 0.01 us -> 30.8 us  [on_device(): lax.all_to_all(jnp.broadcast_to(codes[None], (N_DEV, 8, TILE)), ('prow',...]
    ppermute x16 -> x13, waiting for transfers between devices: 78.1 us -> 97.6 us  [the longest x12 96.6 us: from_first(): lax.ppermute(values[i], 'pcol', pairs(i))]
    ppermute x16 -> x13, starting transfers between devices: 33.8 us -> 41.8 us  [the longest x12 40.7 us: from_first(): lax.ppermute(values[i], 'pcol', pairs(i))]
    ppermute x2 -> x3, waiting for transfers between devices: 1.39 us -> 7.27 us  [on_device(): lax.ppermute(pivots, 'prow', [(p, p ^ bit) for p in range(N_PROW)])]
    ppermute x12 -> x6, starting transfers between devices: 15.5 us -> 17 us  [along(): lax.ppermute(value, 'pcol', [(q, q ^ stride * i) for q in range(N_PCOL)])]
  transfers between devices with their start and end apart: 43 -> 35, of which waited for: 11 -> 17; matrix products, arithmetic and copies ran while one was open for 3% -> 2% of each run, Pallas kernels for 18% -> 14%
where the time goes in v4:
time: 500 us; the launch traced here: 498 us
  waiting for transfers between devices  206 us (41%)
  Pallas kernels  125 us (25%)
  starting transfers between devices  111 us (22%)
  blocking collectives  35.2 us (7%)
  local copies, waits for them, and re-layouts  11.6 us (2%)
  other arithmetic  8.18 us (2%)
    ppermute x12, waiting for transfers between devices, from_first(): lax.ppermute(values[i], 'pcol', pairs(i))  96.6 us
    pallas_call x3, Pallas kernels, pack(): pl.pallas_call(functools.partial(pack_kernel, first, ranks), out_shape=ja...  55 us
    ppermute x12, starting transfers between devices, from_first(): lax.ppermute(values[i], 'pcol', pairs(i))  40.7 us
    pallas_call x3, Pallas kernels, sum_chunk(): pl.pallas_call(functools.partial(sum_kernel, width, counts), out_shape=[j...  37.4 us
    all_to_all x3, waiting for transfers between devices, exchange(): return lax.all_to_all(parts, axes, split_axis=0, concat_axis=0, tiled=True)  36.2 us
    all_to_all x1, blocking collectives, exchange(): return lax.all_to_all(parts, axes, split_axis=0, concat_axis=0, tiled=True)  35.2 us
    all_to_all x1, waiting for transfers between devices, on_device(): lax.all_to_all(jnp.broadcast_to(codes[None], (N_DEV, 8, TILE)), ('prow',...  30.8 us
    all_to_all x3, starting transfers between devices, exchange(): return lax.all_to_all(parts, axes, split_axis=0, concat_axis=0, tiled=True)  28.9 us
  transfers between devices with their start and end apart: 35, of which 17 were waited for; matrix products, arithmetic and copies ran while one was open for 2% of the time, Pallas kernels for 14%

profile of v4, /device:TPU:1, one launch (start us, length us, event | category | flops | bytes accessed | tf_op | source)
XLA Modules:
  0.0 497.7 jit_solution(6257887977558454964)
XLA Ops:
  3.8 15.1 %shard_map.93 = bf16[64,128,128]{2,1,0:T(8,128)(2,1)} custom-call(s32[64]{0:T(128)S(1)} %get-tuple-element.150.src, s32[64]{0:T(128)S(1)} %get-tuple-element.149.present, s32[1]{0:T(128)} %bitcast.22.which, bf16[1024,6144]{1,0:T(8,128)(2,1)} %x_ref.7, s32[48,128]{1,0:T(8,128)} %fusion.32.cw_ref, s32[8,128]{1,0:T(8,128)} %rw_ref.7), custom_call_target="tpu_custom_call" | custom-call | flops 536870912 | bytes 4194304 | tf_op jit(solution)/shard_map/pallas_call | solution.py:114
  18.9 35.2 %all_to_all.41.refs_1_.refs_0_ = bf16[16,4,128,128]{3,2,1,0:T(8,128)(2,1)S(1)} all-to-all(bf16[16,4,128,128]{3,2,1,0:T(8,128)(2,1)} %bitcast.142), channel_id=1, replica_groups=mesh['prow'=8,'pcol'=16] {'pcol'}, dimensions={0} | all-to-all | bytes 4194304 | tf_op jit(solution)/shard_map/all_to_all | solution.py:387
  58.8 7.8 %all-to-all-start.5 = ((s32[128,8,128]{2,1,0:T(8,128)}), s32[128,8,128]{2,1,0:T(8,128)S(1)}, u32[]{:S(2)}, u32[]{:S(2)}) async-start(s32[128,8,128]{2,1,0:T(8,128)} %broadcast_in_dim.89), calls=%async_computation.5 | async-start | bytes 1048576 | tf_op jit(solution)/shard_map/all_to_all | solution.py:483
  66.7 13.5 %shard_map.95.refs_0_ = bf16[8,16,1,1,128,128]{5,4,3,2,1,0:T(8,128)(2,1)} custom-call(s32[64]{0:T(128)S(1)} %get-tuple-element.150.src, s32[64]{0:T(128)S(1)} %get-tuple-element.149.present, s32[8]{0:T(128)S(1)} %bitcast.173, s32[8]{0:T(128)S(1)} %convert_reduce_fusion.4.rank, bf16[1024,6144]{1,0:T(8,128)(2,1)} %x_ref.7, s32[48,1,128]{2,1,0:T(1,128)S(1)} %bitcast.152, ...), custom_call_target="tpu_custom_call" | custom-call | flops 1073741824 | bytes 12582912 | tf_op jit(solution)/shard_map/pallas_call | solution.py:68
  80.2 30.8 %all-to-all-done.5 = s32[128,8,128]{2,1,0:T(8,128)S(1)} async-done(((s32[128,8,128]{2,1,0:T(8,128)}), s32[128,8,128]{2,1,0:T(8,128)S(1)}, u32[]{:S(2)}, u32[]{:S(2)}) %all-to-all-start.5) | async-done | bytes 524320 | tf_op jit(solution)/shard_map/all_to_all | solution.py:483
  111.6 6.6 %all-to-all-start.6 = ((bf16[128,1,128,128]{3,2,1,0:T(8,128)(2,1)}), bf16[128,1,128,128]{3,2,1,0:T(8,128)(2,1)}, u32[]{:S(2)}, u32[]{:S(2)}) async-start(bf16[128,1,128,128]{3,2,1,0:T(8,128)(2,1)} %bitcast.135), calls=%async_computation.6 | async-start | bytes 8388608 | tf_op jit(solution)/shard_map/all_to_all | solution.py:387
  118.2 14.5 %shard_map.98.refs_2_.refs_0_ = bf16[8,16,1,1,128,128]{5,4,3,2,1,0:T(8,128)(2,1)} custom-call(s32[64]{0:T(128)S(1)} %get-tuple-element.150.src, s32[64]{0:T(128)S(1)} %get-tuple-element.149.present, s32[8]{0:T(128)S(1)} %bitcast.174, s32[8]{0:T(128)S(1)} %convert_reduce_fusion.4.rank, bf16[1024,6144]{1,0:T(8,128)(2,1)} %x_ref.7, ...), custom_call_target="tpu_custom_call" | custom-call | flops 1073741824 | bytes 12582912 | tf_op jit(solution)/shard_map/pallas_call | solution.py:68
  132.7 27.1 %shard_map.97.refs_1_.refs_0_ = bf16[8,16,1,2,128,128]{5,4,3,2,1,0:T(8,128)(2,1)} custom-call(s32[64]{0:T(128)S(1)} %get-tuple-element.150.src, s32[64]{0:T(128)S(1)} %get-tuple-element.149.present, s32[8]{0:T(128)S(1)} %bitcast.175, s32[8]{0:T(128)S(1)} %convert_reduce_fusion.4.rank, bf16[1024,6144]{1,0:T(8,128)(2,1)} %x_ref.7, ...), custom_call_target="tpu_custom_call" | custom-call | flops 2147483648 | bytes 25165824 | tf_op jit(solution)/shard_map/pallas_call | solution.py:68
  169.5 17.5 %collective-permute-done.20.refs_3_ = bf16[8,4,128,128]{3,2,1,0:T(8,128)(2,1)S(1)} collective-permute-done((bf16[8,4,128,128]{3,2,1,0:T(8,128)(2,1)}, bf16[8,4,128,128]{3,2,1,0:T(8,128)(2,1)S(1)}, u32[]{:S(2)}, u32[]{:S(2)}) %collective-permute-start.20) | collective-permute-done | bytes 1048608 | tf_op jit(solution)/shard_map/ppermute | solution.py:392
  194.4 10.3 %shard_map.101 = (bf16[11264,128]{1,0:T(8,128)(2,1)S(1)}, bf16[128,128]{1,0:T(8,128)(2,1)}) custom-call(s32[128]{0:T(128)} %slice_bitcast_fusion.16.bins, s32[128]{0:T(128)} %concatenate.9.seconds, s32[128]{0:T(128)S(1)} %compare_select_fusion.pivots, bf16[128,1,128,128]{3,2,1,0:T(8,128)(2,1)} %all-to-all-done.6.x_ref, bf16[16,4,128,128]{3,2,1,0:T(8,128)(2,1)} %copy-done, ...), custom_call_target="tpu_custom_call" | custom-call | flops 4194304 | bytes 11272192 | tf_op jit(solution)/shard_map/pallas_call | solution.py:185
  221.2 6.9 %collective-permute-done.29 = bf16[4,352,128]{2,1,0:T(8,128)(2,1)} collective-permute-done((bf16[4,352,128]{2,1,0:T(8,128)(2,1)}, bf16[4,352,128]{2,1,0:T(8,128)(2,1)}, u32[]{:S(2)}, u32[]{:S(2)}) %collective-permute-start.29) | collective-permute-done | bytes 360480 | tf_op jit(solution)/shard_map/ppermute | solution.py:413
  235.2 7.7 %all-to-all-start.7 = ((bf16[128,2,128,128]{3,2,1,0:T(8,128)(2,1)}), bf16[128,2,128,128]{3,2,1,0:T(8,128)(2,1)}, u32[]{:S(2)}, u32[]{:S(2)}) async-start(bf16[128,2,128,128]{3,2,1,0:T(8,128)(2,1)} %bitcast.132), calls=%async_computation.7 | async-start | bytes 16777216 | tf_op jit(solution)/shard_map/all_to_all | solution.py:387
  256.7 68.2 %collective-permute-done.39 = bf16[4,352,128]{2,1,0:T(8,128)(2,1)S(1)} collective-permute-done((bf16[4,352,128]{2,1,0:T(8,128)(2,1)S(1)}, bf16[4,352,128]{2,1,0:T(8,128)(2,1)S(1)}, u32[]{:S(2)}, u32[]{:S(2)}) %collective-permute-start.39) | collective-permute-done | bytes 360480 | tf_op jit(solution)/shard_map/ppermute | solution.py:413
  324.9 11.9 %collective-permute-start.35 = (bf16[4,352,128]{2,1,0:T(8,128)(2,1)S(1)}, bf16[4,352,128]{2,1,0:T(8,128)(2,1)S(1)}, u32[]{:S(2)}, u32[]{:S(2)}) collective-permute-start(bf16[4,352,128]{2,1,0:T(8,128)(2,1)S(1)} %copy-done.5), channel_id=1, source_target_pairs={{0,4},{1,5},{2,6},{3,7},{16,20},{17,21},{18,22},{19,23},{32,36},{3... | collective-permute-start | bytes 1081352 | tf_op jit(solution)/shard_map/ppermute | solution.py:413
  336.8 6.9 %collective-permute-done.40 = bf16[4,352,128]{2,1,0:T(8,128)(2,1)S(1)} collective-permute-done((bf16[4,352,128]{2,1,0:T(8,128)(2,1)S(1)}, bf16[4,352,128]{2,1,0:T(8,128)(2,1)S(1)}, u32[]{:S(2)}, u32[]{:S(2)}) %collective-permute-start.40) | collective-permute-done | bytes 360480 | tf_op jit(solution)/shard_map/ppermute | solution.py:413
  343.7 8.4 %collective-permute-done.41 = bf16[4,352,128]{2,1,0:T(8,128)(2,1)S(1)} collective-permute-done((bf16[4,352,128]{2,1,0:T(8,128)(2,1)S(1)}, bf16[4,352,128]{2,1,0:T(8,128)(2,1)S(1)}, u32[]{:S(2)}, u32[]{:S(2)}) %collective-permute-start.41) | collective-permute-done | bytes 360480 | tf_op jit(solution)/shard_map/ppermute | solution.py:413
  362.8 6.4 %collective-permute-start.38 = (bf16[4,352,128]{2,1,0:T(8,128)(2,1)S(1)}, bf16[4,352,128]{2,1,0:T(8,128)(2,1)S(1)}, u32[]{:S(2)}, u32[]{:S(2)}) collective-permute-start(bf16[4,352,128]{2,1,0:T(8,128)(2,1)S(1)} %select_select_fusion.3), channel_id=1, source_target_pairs={{0,3},{1,2},{2,1},{3,0},{4,7},{5,6},{6,5},{7,4},{8,11},{9,10},{10,... | collective-permute-start | bytes 1081352 | tf_op jit(solution)/shard_map/ppermute | solution.py:431
  377.7 7.1 %collective-permute-done.38 = bf16[4,352,128]{2,1,0:T(8,128)(2,1)S(1)} collective-permute-done((bf16[4,352,128]{2,1,0:T(8,128)(2,1)S(1)}, bf16[4,352,128]{2,1,0:T(8,128)(2,1)S(1)}, u32[]{:S(2)}, u32[]{:S(2)}) %collective-permute-start.38) | collective-permute-done | bytes 360480 | tf_op jit(solution)/shard_map/ppermute | solution.py:431
  385.0 14.6 %all-to-all-start.8 = ((bf16[128,1,128,128]{3,2,1,0:T(8,128)(2,1)}), bf16[128,1,128,128]{3,2,1,0:T(8,128)(2,1)}, u32[]{:S(2)}, u32[]{:S(2)}) async-start(bf16[128,1,128,128]{3,2,1,0:T(8,128)(2,1)} %bitcast.133), calls=%async_computation.8 | async-start | bytes 8388608 | tf_op jit(solution)/shard_map/all_to_all | solution.py:387
  399.7 15.8 %shard_map.105 = (bf16[11264,256]{1,0:T(8,128)(2,1)}, bf16[128,256]{1,0:T(8,128)(2,1)}) custom-call(s32[128]{0:T(128)} %slice_bitcast_fusion.16.bins, s32[128]{0:T(128)} %concatenate.9.seconds, s32[128]{0:T(128)S(1)} %compare_select_fusion.pivots, bf16[128,2,128,128]{3,2,1,0:T(8,128)(2,1)} %all-to-all-done.7.refs_1_.x_ref, ...), custom_call_target="tpu_custom_call" | custom-call | flops 8388608 | bytes 22544384 | tf_op jit(solution)/shard_map/pallas_call | solution.py:185
  415.5 36.1 %all-to-all-done.8.x_ref = bf16[128,1,128,128]{3,2,1,0:T(8,128)(2,1)} async-done(((bf16[128,1,128,128]{3,2,1,0:T(8,128)(2,1)}), bf16[128,1,128,128]{3,2,1,0:T(8,128)(2,1)}, u32[]{:S(2)}, u32[]{:S(2)}) %all-to-all-start.8) | async-done | bytes 4194336 | tf_op jit(solution)/shard_map/all_to_all | solution.py:387
  451.7 11.3 %shard_map.104 = (bf16[11264,128]{1,0:T(8,128)(2,1)}, bf16[128,128]{1,0:T(8,128)(2,1)}) custom-call(s32[128]{0:T(128)} %slice_bitcast_fusion.16.bins, s32[128]{0:T(128)} %concatenate.9.seconds, s32[128]{0:T(128)S(1)} %compare_select_fusion.pivots, bf16[128,1,128,128]{3,2,1,0:T(8,128)(2,1)} %all-to-all-done.8.x_ref, bf16[16,4,128,128]{3,2,1,0:T(8,128)(2,1)} %copy-done, ...), custom_call_target="tpu_custom_call" | custom-call | flops 4194304 | bytes 11272192 | tf_op jit(solution)/shard_map/pallas_call | solution.py:185
  480.3 17.4 %conditional.1 = (bf16[11264,512]{1,0:T(8,128)(2,1)}) conditional(s32[]{:T(128)} %convert_element_type.22, (s32[1]{0:T(128)}, bf16[11264,128]{1,0:T(8,128)(2,1)}, bf16[11264,128]{1,0:T(8,128)(2,1)}, bf16[11264,256]{1,0:T(8,128)(2,1)}, bf16[4,4,352,128]{3,2,1,0:T(8,128)(2,1)S(1)}, /*index=5*/bf16[4,4,352,128]{3,2,1,0:T(8,128)(2,1)S(1)}, ...), branch_computations={%region_10.12_spmd, %region_11.13_spmd} | conditional | flops 6164119552 | bytes 271455328 | solution.py:569
  480.3 17.4 %branch_0_fun.1 = bf16[11264,512]{1,0:T(8,128)(2,1)} custom-call(s32[1]{0:T(128)} %get-tuple-element.56.my_pcol, bf16[11264,128]{1,0:T(8,128)(2,1)} %get-tuple-element.58.refs_0_, bf16[11264,128]{1,0:T(8,128)(2,1)} %get-tuple-element.59.refs_1_, bf16[11264,256]{1,0:T(8,128)(2,1)} %get-tuple-element.60.refs_2_, ...), custom_call_target="tpu_custom_call" | custom-call | flops 1845493760 | bytes 23068672 | tf_op jit(solution)/shard_map/cond/branch_0_fun/pallas_call | solution.py:346
  (148 shorter events, 99.4 us)
Async XLA Ops:
  54.1 57.5 %collective-permute-start.18 = (bf16[16,4,128,128]{3,2,1,0:T(8,128)(2,1)S(1)}, bf16[16,4,128,128]{3,2,1,0:T(8,128)(2,1)}, u32[]{:S(2)}, u32[]{:S(2)}) collective-permute-start(bf16[16,4,128,128]{3,2,1,0:T(8,128)(2,1)S(1)} %all_to_all.41.refs_1_.refs_0_), channel_id=1, source_target_pairs={{0,32},{16,48},{32,64},{48,80},{64,96},{80,112},{96,0},{112,16},{1... | collective-permute-start | bytes 6291464 | tf_op jit(solution)/shard_map/ppermute | solution.py:392
  55.3 56.3 %collective-permute-start.19 = (bf16[16,4,128,128]{3,2,1,0:T(8,128)(2,1)S(1)}, bf16[16,4,128,128]{3,2,1,0:T(8,128)(2,1)}, u32[]{:S(2)}, u32[]{:S(2)}) collective-permute-start(bf16[16,4,128,128]{3,2,1,0:T(8,128)(2,1)S(1)} %all_to_all.41.refs_1_.refs_0_), channel_id=1, source_target_pairs={{0,96},{16,112},{32,0},{48,16},{64,32},{80,48},{96,64},{112,80},{1... | collective-permute-start | bytes 6291464 | tf_op jit(solution)/shard_map/ppermute | solution.py:392
  58.8 52.1 %all-to-all-start.5 = ((s32[128,8,128]{2,1,0:T(8,128)}), s32[128,8,128]{2,1,0:T(8,128)S(1)}, u32[]{:S(2)}, u32[]{:S(2)}) async-start(s32[128,8,128]{2,1,0:T(8,128)} %broadcast_in_dim.89), calls=%async_computation.5 | async-start | bytes 1048576 | tf_op jit(solution)/shard_map/all_to_all | solution.py:483
  111.6 82.8 %all-to-all-start.6 = ((bf16[128,1,128,128]{3,2,1,0:T(8,128)(2,1)}), bf16[128,1,128,128]{3,2,1,0:T(8,128)(2,1)}, u32[]{:S(2)}, u32[]{:S(2)}) async-start(bf16[128,1,128,128]{3,2,1,0:T(8,128)(2,1)} %bitcast.135), calls=%async_computation.6 | async-start | bytes 8388608 | tf_op jit(solution)/shard_map/all_to_all | solution.py:387
  162.1 24.9 %collective-permute-start.20 = (bf16[8,4,128,128]{3,2,1,0:T(8,128)(2,1)}, bf16[8,4,128,128]{3,2,1,0:T(8,128)(2,1)S(1)}, u32[]{:S(2)}, u32[]{:S(2)}) collective-permute-start(bf16[8,4,128,128]{3,2,1,0:T(8,128)(2,1)} %shard_map.99), channel_id=1, source_target_pairs={{0,32},{16,48},{32,64},{48,80},{64,96},{80,112},{96,0},{112,16},{1... | collective-permute-start | bytes 3145736 | tf_op jit(solution)/shard_map/ppermute | solution.py:392
  165.8 24.4 %collective-permute-start.21 = (bf16[8,4,128,128]{3,2,1,0:T(8,128)(2,1)}, bf16[8,4,128,128]{3,2,1,0:T(8,128)(2,1)}, u32[]{:S(2)}, u32[]{:S(2)}) collective-permute-start(bf16[8,4,128,128]{3,2,1,0:T(8,128)(2,1)} %shard_map.100), channel_id=1, source_target_pairs={{0,96},{16,112},{32,0},{48,16},{64,32},{80,48},{96,64},{112,80},{1... | collective-permute-start | bytes 3145736 | tf_op jit(solution)/shard_map/ppermute | solution.py:392
  167.4 26.6 %collective-permute-start.22 = (bf16[16,4,128,128]{3,2,1,0:T(8,128)(2,1)S(1)}, bf16[16,4,128,128]{3,2,1,0:T(8,128)(2,1)}, u32[]{:S(2)}, u32[]{:S(2)}) collective-permute-start(bf16[16,4,128,128]{3,2,1,0:T(8,128)(2,1)S(1)} %copy-done.1), channel_id=1, source_target_pairs={{0,16},{16,0},{32,48},{48,32},{64,80},{80,64},{96,112},{112,96},{1... | collective-permute-start | bytes 6291464 | tf_op jit(solution)/shard_map/ppermute | solution.py:399
  168.9 25.5 %collective-permute-start.23 = (bf16[16,4,128,128]{3,2,1,0:T(8,128)(2,1)}, bf16[16,4,128,128]{3,2,1,0:T(8,128)(2,1)}, u32[]{:S(2)}, u32[]{:S(2)}) collective-permute-start(bf16[16,4,128,128]{3,2,1,0:T(8,128)(2,1)} %collective-permute-done.18.refs_1_), channel_id=1, source_target_pairs={{0,16},{16,0},{32,48},{48,32},{64,80},{80,64},{96,112},{112,96},{1... | collective-permute-start | bytes 6291464 | tf_op jit(solution)/shard_map/ppermute | solution.py:399
  168.9 25.5 %collective-permute-start.24 = (bf16[16,4,128,128]{3,2,1,0:T(8,128)(2,1)}, bf16[16,4,128,128]{3,2,1,0:T(8,128)(2,1)}, u32[]{:S(2)}, u32[]{:S(2)}) collective-permute-start(bf16[16,4,128,128]{3,2,1,0:T(8,128)(2,1)} %collective-permute-done.19.refs_2_), channel_id=1, source_target_pairs={{0,16},{16,0},{32,48},{48,32},{64,80},{80,64},{96,112},{112,96},{1... | collective-permute-start | bytes 6291464 | tf_op jit(solution)/shard_map/ppermute | solution.py:399
  213.0 15.0 %collective-permute-start.29 = (bf16[4,352,128]{2,1,0:T(8,128)(2,1)}, bf16[4,352,128]{2,1,0:T(8,128)(2,1)}, u32[]{:S(2)}, u32[]{:S(2)}) collective-permute-start(bf16[4,352,128]{2,1,0:T(8,128)(2,1)} %get-tuple-element.166), channel_id=1, source_target_pairs={{0,1},{16,17},{32,33},{48,49},{64,65},{80,81},{96,97},{112,113}} | collective-permute-start | bytes 1081352 | tf_op jit(solution)/shard_map/ppermute | solution.py:413
  219.1 15.1 %collective-permute-start.32 = (bf16[4,352,128]{2,1,0:T(8,128)(2,1)}, bf16[4,352,128]{2,1,0:T(8,128)(2,1)}, u32[]{:S(2)}, u32[]{:S(2)}) collective-permute-start(bf16[4,352,128]{2,1,0:T(8,128)(2,1)} %get-tuple-element.163), channel_id=1, source_target_pairs={{0,4},{16,20},{32,36},{48,52},{64,68},{80,84},{96,100},{112,116}} | collective-permute-start | bytes 1081352 | tf_op jit(solution)/shard_map/ppermute | solution.py:413
  235.2 149.8 %all-to-all-start.7 = ((bf16[128,2,128,128]{3,2,1,0:T(8,128)(2,1)}), bf16[128,2,128,128]{3,2,1,0:T(8,128)(2,1)}, u32[]{:S(2)}, u32[]{:S(2)}) async-start(bf16[128,2,128,128]{3,2,1,0:T(8,128)(2,1)} %bitcast.132), calls=%async_computation.7 | async-start | bytes 16777216 | tf_op jit(solution)/shard_map/all_to_all | solution.py:387
  243.0 81.9 %collective-permute-start.39 = (bf16[4,352,128]{2,1,0:T(8,128)(2,1)S(1)}, bf16[4,352,128]{2,1,0:T(8,128)(2,1)S(1)}, u32[]{:S(2)}, u32[]{:S(2)}) collective-permute-start(bf16[4,352,128]{2,1,0:T(8,128)(2,1)S(1)} %copy-done.6), channel_id=1, source_target_pairs={{0,3},{4,7},{8,11},{12,15},{16,19},{20,23},{24,27},{28,31},{32,35}... | collective-permute-start | bytes 1081352 | tf_op jit(solution)/shard_map/ppermute | solution.py:413
  248.2 95.5 %collective-permute-start.40 = (bf16[4,352,128]{2,1,0:T(8,128)(2,1)S(1)}, bf16[4,352,128]{2,1,0:T(8,128)(2,1)S(1)}, u32[]{:S(2)}, u32[]{:S(2)}) collective-permute-start(bf16[4,352,128]{2,1,0:T(8,128)(2,1)S(1)} %copy-done.6), channel_id=1, source_target_pairs={{0,2},{4,6},{8,10},{12,14},{16,18},{20,22},{24,26},{28,30},{32,34}... | collective-permute-start | bytes 1081352 | tf_op jit(solution)/shard_map/ppermute | solution.py:413
  249.5 102.6 %collective-permute-start.41 = (bf16[4,352,128]{2,1,0:T(8,128)(2,1)S(1)}, bf16[4,352,128]{2,1,0:T(8,128)(2,1)S(1)}, u32[]{:S(2)}, u32[]{:S(2)}) collective-permute-start(bf16[4,352,128]{2,1,0:T(8,128)(2,1)S(1)} %copy-done.6), channel_id=1, source_target_pairs={{0,1},{4,5},{8,9},{12,13},{16,17},{20,21},{24,25},{28,29},{32,33},... | collective-permute-start | bytes 1081352 | tf_op jit(solution)/shard_map/ppermute | solution.py:413
  250.8 106.5 %collective-permute-start.33 = (bf16[4,352,128]{2,1,0:T(8,128)(2,1)S(1)}, bf16[4,352,128]{2,1,0:T(8,128)(2,1)S(1)}, u32[]{:S(2)}, u32[]{:S(2)}) collective-permute-start(bf16[4,352,128]{2,1,0:T(8,128)(2,1)S(1)} %copy-done.5), channel_id=1, source_target_pairs={{0,12},{1,13},{2,14},{3,15},{16,28},{17,29},{18,30},{19,31},{32,44... | collective-permute-start | bytes 1081352 | tf_op jit(solution)/shard_map/ppermute | solution.py:413
  255.3 102.2 %collective-permute-start.34 = (bf16[4,352,128]{2,1,0:T(8,128)(2,1)S(1)}, bf16[4,352,128]{2,1,0:T(8,128)(2,1)S(1)}, u32[]{:S(2)}, u32[]{:S(2)}) collective-permute-start(bf16[4,352,128]{2,1,0:T(8,128)(2,1)S(1)} %copy-done.5), channel_id=1, source_target_pairs={{0,8},{1,9},{2,10},{3,11},{16,24},{17,25},{18,26},{19,27},{32,40},... | collective-permute-start | bytes 1081352 | tf_op jit(solution)/shard_map/ppermute | solution.py:413
  324.9 32.6 %collective-permute-start.35 = (bf16[4,352,128]{2,1,0:T(8,128)(2,1)S(1)}, bf16[4,352,128]{2,1,0:T(8,128)(2,1)S(1)}, u32[]{:S(2)}, u32[]{:S(2)}) collective-permute-start(bf16[4,352,128]{2,1,0:T(8,128)(2,1)S(1)} %copy-done.5), channel_id=1, source_target_pairs={{0,4},{1,5},{2,6},{3,7},{16,20},{17,21},{18,22},{19,23},{32,36},{3... | collective-permute-start | bytes 1081352 | tf_op jit(solution)/shard_map/ppermute | solution.py:413
  353.8 19.7 %collective-permute-start.43 = (bf16[4,352,128]{2,1,0:T(8,128)(2,1)S(1)}, bf16[4,352,128]{2,1,0:T(8,128)(2,1)S(1)}, u32[]{:S(2)}, u32[]{:S(2)}) collective-permute-start(bf16[4,352,128]{2,1,0:T(8,128)(2,1)S(1)} %select_select_fusion.2), channel_id=1, source_target_pairs={{0,8},{1,9},{2,10},{3,11},{4,12},{5,13},{6,14},{7,15},{8,0},{9,1},... | collective-permute-start | bytes 1081352 | tf_op jit(solution)/shard_map/ppermute | solution.py:431
  357.3 18.3 %collective-permute-start.44 = (bf16[4,352,128]{2,1,0:T(8,128)(2,1)S(1)}, bf16[4,352,128]{2,1,0:T(8,128)(2,1)S(1)}, u32[]{:S(2)}, u32[]{:S(2)}) collective-permute-start(bf16[4,352,128]{2,1,0:T(8,128)(2,1)S(1)} %select_select_fusion.2), channel_id=1, source_target_pairs={{0,12},{1,13},{2,14},{3,15},{4,8},{5,9},{6,10},{7,11},{8,4},{9,5},... | collective-permute-start | bytes 1081352 | tf_op jit(solution)/shard_map/ppermute | solution.py:431
  357.6 18.2 %collective-permute-start.36 = (bf16[4,352,128]{2,1,0:T(8,128)(2,1)S(1)}, bf16[4,352,128]{2,1,0:T(8,128)(2,1)S(1)}, u32[]{:S(2)}, u32[]{:S(2)}) collective-permute-start(bf16[4,352,128]{2,1,0:T(8,128)(2,1)S(1)} %select_select_fusion.3), channel_id=1, source_target_pairs={{0,1},{1,0},{2,3},{3,2},{4,5},{5,4},{6,7},{7,6},{8,9},{9,8},{10,11... | collective-permute-start | bytes 1081352 | tf_op jit(solution)/shard_map/ppermute | solution.py:431
  359.8 17.9 %collective-permute-start.37 = (bf16[4,352,128]{2,1,0:T(8,128)(2,1)S(1)}, bf16[4,352,128]{2,1,0:T(8,128)(2,1)S(1)}, u32[]{:S(2)}, u32[]{:S(2)}) collective-permute-start(bf16[4,352,128]{2,1,0:T(8,128)(2,1)S(1)} %select_select_fusion.3), channel_id=1, source_target_pairs={{0,2},{1,3},{2,0},{3,1},{4,6},{5,7},{6,4},{7,5},{8,10},{9,11},{10,... | collective-permute-start | bytes 1081352 | tf_op jit(solution)/shard_map/ppermute | solution.py:431
  362.8 22.0 %collective-permute-start.38 = (bf16[4,352,128]{2,1,0:T(8,128)(2,1)S(1)}, bf16[4,352,128]{2,1,0:T(8,128)(2,1)S(1)}, u32[]{:S(2)}, u32[]{:S(2)}) collective-permute-start(bf16[4,352,128]{2,1,0:T(8,128)(2,1)S(1)} %select_select_fusion.3), channel_id=1, source_target_pairs={{0,3},{1,2},{2,1},{3,0},{4,7},{5,6},{6,5},{7,4},{8,11},{9,10},{10,... | collective-permute-start | bytes 1081352 | tf_op jit(solution)/shard_map/ppermute | solution.py:431
  385.0 66.6 %all-to-all-start.8 = ((bf16[128,1,128,128]{3,2,1,0:T(8,128)(2,1)}), bf16[128,1,128,128]{3,2,1,0:T(8,128)(2,1)}, u32[]{:S(2)}, u32[]{:S(2)}) async-start(bf16[128,1,128,128]{3,2,1,0:T(8,128)(2,1)} %bitcast.133), calls=%async_computation.8 | async-start | bytes 8388608 | tf_op jit(solution)/shard_map/all_to_all | solution.py:387
  (31 other events, 483.5 us)

commit v5 on v4

--- a/solution.py
+++ b/solution.py
@@ -19,7 +19,7 @@
 OWN_TILES = 8
 RANKS = 2
 WIDE_CHUNKS = ((0, 1), (1, 1), (2, 2))
-CHUNKS = ((0, 1), (2, 2), (1, 1))
+CHUNKS = ((0, 1), (1, 2), (3, 1))
 GROUP = 8
 STEPS = 8
 ROW_BLOCK = 704
@@ -387,24 +387,28 @@
     return lax.all_to_all(parts, axes, split_axis=0, concat_axis=0, tiled=True)
 
 
-def gather_prow(own, first):
-    def shifted(value, by):
-        return lax.ppermute(value, "prow", [(p, (p + 2 * by) % N_PROW) for p in range(N_PROW)])
-
-    half = own.shape[0] // 2
+def shifted(value, by):
+    return lax.ppermute(value, "prow", [(p, (p + 2 * by) % N_PROW) for p in range(N_PROW)])
+
+
+def both_cores(here, named):
+    there = [lax.ppermute(v, "prow", [(p, p ^ 1) for p in range(N_PROW)]) for v in here]
+    return here + there, [(flip, *name) for flip in (0, 1) for name in named]
+
+
+def gather_direct(own):
+    n = own.shape[0]
+    here = [own, shifted(own, 1), shifted(own, -1), shifted(own, 2)]
+    return both_cores(here, [(0, 0, n), (-1, 0, n), (1, 0, n), (-2, 0, n)])
+
+
+def gather_relayed(own):
+    n = own.shape[0]
+    half = n // 2
     left, right = shifted(own, 1), shifted(own, -1)
-    far_low = shifted(after(left[:half], *first), 1)
-    far_high = shifted(after(right[half:], *first), -1)
-    here = [own, left, right, far_low, far_high]
-    there = [lax.ppermute(v, "prow", [(p, p ^ 1) for p in range(N_PROW)]) for v in here]
-    named = [(0, 2 * half), (0, 2 * half), (0, 2 * half), (0, half), (half, half)]
-    shifts = [0, -1, 1, -2, 2]
-    places = [
-        (flip, shift, begin, count)
-        for flip in (0, 1)
-        for shift, (begin, count) in zip(shifts, named)
-    ]
-    return here + there, places
+    here = [own, left, right, shifted(left[:half], 1), shifted(right[half:], -1)]
+    named = [(0, 0, n), (-1, 0, n), (1, 0, n), (-2, 0, half), (-2, half, half)]
+    return both_cores(here, named)
 
 
 def from_first(values, mine, pairs):
@@ -422,10 +426,13 @@
     return low, high
 
 
-def gather_panel(low, high, my_pcol):
+def spread_quarters(low, high, my_pcol):
     low = from_first([low] * 4, my_pcol // 4, lambda i: [(k, 4 * i + k) for k in range(4)])
     high = from_first([high] * 4, my_pcol % 4, lambda i: [(4 * k, 4 * k + i) for k in range(4)])
-
+    return low, high
+
+
+def gather_panel(low, high):
     def along(value, stride):
         moved = [
             lax.ppermute(value, "pcol", [(q, q ^ (stride * i)) for q in range(N_PCOL)])
@@ -474,7 +481,9 @@
         )
         for first, width in CHUNKS
     }
-    parts, places = gather_prow(own, [packed[first] for first, _ in CHUNKS[1:]])
+    near_parts, near_places = gather_direct(own[:, :1])
+    far_own = after(own[:, 1:], *[packed[first] for first, _ in CHUNKS[1:]])
+    far_parts, far_places = gather_relayed(far_own)
 
     code = after(owners * FRONT_TILES + row_local, own)
     codes = jnp.pad(
@@ -508,27 +517,31 @@
     ).astype(jnp.int32)
     pcol_line = my_pcol.astype(jnp.int32).reshape(1)
     pivot_line = pivot_local.reshape(1, TILE)
-    places = jnp.concatenate(
-        [
-            jnp.take(seconds, ((my_prow ^ flip) + 2 * shift) % N_PROW, axis=0)[
-                begin : begin + count
+
+    def bins_of(places):
+        return jnp.concatenate(
+            [
+                jnp.take(seconds, ((my_prow ^ flip) + 2 * shift) % N_PROW, axis=0)[
+                    begin : begin + count
+                ]
+                for flip, shift, begin, count in places
             ]
-            for flip, shift, begin, count in places
-        ]
-    )
+        )
 
     fronts, picks = {}, {}
-    panel, ahead = None, [*parts[1:3], codes]
+    panel, ahead = None, [*near_parts[1:4], codes]
     for first, width in CHUNKS:
         sent = after(packed[first], *ahead)
         arrived = exchange(sent.reshape(N_DEV, width, TILE, TILE), ("prow", "pcol"))
+        parts, places = (near_parts, near_places) if first == 0 else (far_parts, far_places)
         fronts[first], picks[first] = sum_chunk(
-            first, width, bins[:, 0], places, pivot_local, arrived, parts
+            max(first - 1, 0), width, bins[:, 0], bins_of(places), pivot_local, arrived, parts
         )
         if first == 0:
             quarters = quarter_panel(fronts[first][:, :TILE], my_pcol)
-            panel = gather_panel(*quarters, my_pcol)
-            ahead = quarters
+            spread = spread_quarters(*quarters, my_pcol)
+            panel = gather_panel(*spread)
+            ahead = [*spread, *far_parts[3:5]]
         else:
             ahead = [arrived, *panel]
     fronts = [fronts[k] for k in sorted(fronts)]
@@ -559,7 +572,8 @@
             front, picked = accumulate(width, bins.reshape(-1), pivot_local, arrived)
             fronts.append(front)
             picks.append(picked)
-        panel = gather_panel(*quarter_panel(fronts[0][:, :TILE], my_pcol), my_pcol)
+        quarters = quarter_panel(fronts[0][:, :TILE], my_pcol)
+        panel = gather_panel(*spread_quarters(*quarters, my_pcol))
         picked = jnp.concatenate(picks, axis=1)
         pivots = exchange(jnp.broadcast_to(picked[None], (N_PROW,) + picked.shape), "prow")
         return update(

time: 500 us -> 472 us (0.944)
  blocking collectives: 35.2 us -> 0 us
  local copies, waits for them, and re-layouts: 11.6 us -> 20.9 us
    ppermute x6, waiting for transfers between devices: 15.4 us -> 107 us  [along(): lax.ppermute(value, 'pcol', [(q, q ^ stride * i) for q in range(N_PCOL)])]
    ppermute x12, waiting for transfers between devices: 96.6 us -> 25.2 us  [from_first(): lax.ppermute(values[i], 'pcol', pairs(i))]
    all_to_all x1 -> x0, blocking collectives: 35.2 us -> none  [exchange(): return lax.all_to_all(parts, axes, split_axis=0, concat_axis=0, tiled=True)]
    all_to_all x1, waiting for transfers between devices: 30.8 us -> 6.19 us  [on_device(): lax.all_to_all(jnp.broadcast_to(codes[None], (N_DEV, 8, TILE)), ('prow',...]
    ppermute x4 -> x7, waiting for transfers between devices: 18.6 us -> 0.02 us  [shifted(): lax.ppermute(value, 'prow', [(p, (p + 2 * by) % N_PROW) for p in range(N_...]
    ppermute x12, starting transfers between devices: 40.7 us -> 26.8 us  [from_first(): lax.ppermute(values[i], 'pcol', pairs(i))]
    all_to_all x3 -> x4, starting transfers between devices: 28.9 us -> 42.5 us  [exchange(): return lax.all_to_all(parts, axes, split_axis=0, concat_axis=0, tiled=True)]
    all_to_all x3 -> x4, waiting for transfers between devices: 36.2 us -> 49.1 us  [exchange(): return lax.all_to_all(parts, axes, split_axis=0, concat_axis=0, tiled=True)]
  transfers between devices with their start and end apart: 35 -> 43, of which waited for: 17 -> 18; matrix products, arithmetic and copies ran while one was open for 2% -> 3% of each run, Pallas kernels for 14% -> 17%
where the time goes in v5:
time: 472 us; the launch traced here: 470 us
  waiting for transfers between devices  205 us (43%)
  Pallas kernels  123 us (26%)
  starting transfers between devices  111 us (24%)
  local copies, waits for them, and re-layouts  20.9 us (4%)
  other arithmetic  9.35 us (2%)
    ppermute x6, waiting for transfers between devices, along(): lax.ppermute(value, 'pcol', [(q, q ^ stride * i) for q in range(N_PCOL)])  107 us
    pallas_call x3, Pallas kernels, pack(): pl.pallas_call(functools.partial(pack_kernel, first, ranks), out_shape=ja...  54.9 us
    all_to_all x4, waiting for transfers between devices, exchange(): return lax.all_to_all(parts, axes, split_axis=0, concat_axis=0, tiled=True)  49.1 us
    all_to_all x4, starting transfers between devices, exchange(): return lax.all_to_all(parts, axes, split_axis=0, concat_axis=0, tiled=True)  42.5 us
    pallas_call x3, Pallas kernels, sum_chunk(): pl.pallas_call(functools.partial(sum_kernel, width, counts), out_shape=[j...  35.9 us
    ppermute x12, starting transfers between devices, from_first(): lax.ppermute(values[i], 'pcol', pairs(i))  26.8 us
    ppermute x12, waiting for transfers between devices, from_first(): lax.ppermute(values[i], 'pcol', pairs(i))  25.2 us
    pallas_call x1, Pallas kernels, update(): pl.pallas_call(functools.partial(update_kernel, len(fronts)), out_shape=j...  16.8 us
  transfers between devices with their start and end apart: 43, of which 18 were waited for; matrix products, arithmetic and copies ran while one was open for 3% of the time, Pallas kernels for 17%

profile of v5, /device:TPU:1, one launch (start us, length us, event | category | flops | bytes accessed | tf_op | source)
XLA Modules:
  0.0 469.7 jit_solution(7893457783269174394)
XLA Ops:
  3.7 15.0 %shard_map.93 = bf16[64,128,128]{2,1,0:T(8,128)(2,1)} custom-call(s32[64]{0:T(128)S(1)} %get-tuple-element.150.src, s32[64]{0:T(128)S(1)} %get-tuple-element.149.present, s32[1]{0:T(128)} %bitcast.22.which, bf16[1024,6144]{1,0:T(8,128)(2,1)} %x_ref.7, s32[48,128]{1,0:T(8,128)} %fusion.30.cw_ref, s32[8,128]{1,0:T(8,128)} %rw_ref.7), custom_call_target="tpu_custom_call" | custom-call | flops 536870912 | bytes 4194304 | tf_op jit(solution)/shard_map/pallas_call | solution.py:114
  18.7 8.7 %all-to-all-start.4 = ((bf16[16,4,128,128]{3,2,1,0:T(8,128)(2,1)}), bf16[16,4,128,128]{3,2,1,0:T(8,128)(2,1)S(1)}, u32[]{:S(2)}, u32[]{:S(2)}) async-start(bf16[16,4,128,128]{3,2,1,0:T(8,128)(2,1)} %bitcast.136), calls=%async_computation.4 | async-start | bytes 4194304 | tf_op jit(solution)/shard_map/all_to_all | solution.py:387
  28.0 27.3 %all-to-all-done.4.refs_1_ = bf16[16,4,128,128]{3,2,1,0:T(8,128)(2,1)S(1)} async-done(((bf16[16,4,128,128]{3,2,1,0:T(8,128)(2,1)}), bf16[16,4,128,128]{3,2,1,0:T(8,128)(2,1)S(1)}, u32[]{:S(2)}, u32[]{:S(2)}) %all-to-all-start.4) | async-done | bytes 2097184 | tf_op jit(solution)/shard_map/all_to_all | solution.py:387
  61.9 8.5 %all-to-all-start.5 = ((s32[128,8,128]{2,1,0:T(8,128)}), s32[128,8,128]{2,1,0:T(8,128)S(1)}, u32[]{:S(2)}, u32[]{:S(2)}) async-start(s32[128,8,128]{2,1,0:T(8,128)} %broadcast_in_dim.89), calls=%async_computation.5 | async-start | bytes 1048576 | tf_op jit(solution)/shard_map/all_to_all | solution.py:492
  70.5 14.3 %shard_map.95.refs_0_ = bf16[8,16,1,1,128,128]{5,4,3,2,1,0:T(8,128)(2,1)} custom-call(s32[64]{0:T(128)S(1)} %get-tuple-element.150.src, s32[64]{0:T(128)S(1)} %get-tuple-element.149.present, s32[8]{0:T(128)S(1)} %bitcast.167, s32[8]{0:T(128)S(1)} %convert_reduce_fusion.4.rank, bf16[1024,6144]{1,0:T(8,128)(2,1)} %x_ref.7, s32[48,1,128]{2,1,0:T(1,128)S(1)} %bitcast.146, ...), custom_call_target="tpu_custom_call" | custom-call | flops 1073741824 | bytes 12582912 | tf_op jit(solution)/shard_map/pallas_call | solution.py:68
  84.8 6.2 %all-to-all-done.5 = s32[128,8,128]{2,1,0:T(8,128)S(1)} async-done(((s32[128,8,128]{2,1,0:T(8,128)}), s32[128,8,128]{2,1,0:T(8,128)S(1)}, u32[]{:S(2)}, u32[]{:S(2)}) %all-to-all-start.5) | async-done | bytes 524320 | tf_op jit(solution)/shard_map/all_to_all | solution.py:492
  92.7 6.0 %all-to-all-start.6 = ((bf16[128,1,128,128]{3,2,1,0:T(8,128)(2,1)}), bf16[128,1,128,128]{3,2,1,0:T(8,128)(2,1)}, u32[]{:S(2)}, u32[]{:S(2)}) async-start(bf16[128,1,128,128]{3,2,1,0:T(8,128)(2,1)} %bitcast.129), calls=%async_computation.6 | async-start | bytes 8388608 | tf_op jit(solution)/shard_map/all_to_all | solution.py:387
  98.9 14.3 %shard_map.99.refs_2_.refs_0_ = bf16[8,16,1,1,128,128]{5,4,3,2,1,0:T(8,128)(2,1)} custom-call(s32[64]{0:T(128)S(1)} %get-tuple-element.150.src, s32[64]{0:T(128)S(1)} %get-tuple-element.149.present, s32[8]{0:T(128)S(1)} %bitcast.168, s32[8]{0:T(128)S(1)} %convert_reduce_fusion.4.rank, bf16[1024,6144]{1,0:T(8,128)(2,1)} %x_ref.7, ...), custom_call_target="tpu_custom_call" | custom-call | flops 1073741824 | bytes 12582912 | tf_op jit(solution)/shard_map/pallas_call | solution.py:68
  113.2 26.3 %shard_map.98.refs_1_.refs_0_ = bf16[8,16,1,2,128,128]{5,4,3,2,1,0:T(8,128)(2,1)} custom-call(s32[64]{0:T(128)S(1)} %get-tuple-element.150.src, s32[64]{0:T(128)S(1)} %get-tuple-element.149.present, s32[8]{0:T(128)S(1)} %bitcast.169, s32[8]{0:T(128)S(1)} %convert_reduce_fusion.4.rank, bf16[1024,6144]{1,0:T(8,128)(2,1)} %x_ref.7, ...), custom_call_target="tpu_custom_call" | custom-call | flops 2147483648 | bytes 25165824 | tf_op jit(solution)/shard_map/pallas_call | solution.py:68
  150.9 10.0 %shard_map.97 = (bf16[11264,128]{1,0:T(8,128)(2,1)S(1)}, bf16[128,128]{1,0:T(8,128)(2,1)}) custom-call(s32[128]{0:T(128)} %slice_bitcast_fusion.16.bins, s32[128]{0:T(128)} %concatenate.11.seconds, s32[128]{0:T(128)S(1)} %compare_select_fusion.pivots, bf16[128,1,128,128]{3,2,1,0:T(8,128)(2,1)} %all-to-all-done.6.x_ref, ...), custom_call_target="tpu_custom_call" | custom-call | flops 4194304 | bytes 11272192 | tf_op jit(solution)/shard_map/pallas_call | solution.py:185
  162.0 5.0 %collective-permute-start.25 = (bf16[4,352,128]{2,1,0:T(8,128)(2,1)S(1)}, bf16[4,352,128]{2,1,0:T(8,128)(2,1)S(1)}, u32[]{:S(2)}, u32[]{:S(2)}) collective-permute-start(bf16[4,352,128]{2,1,0:T(8,128)(2,1)S(1)} %get-tuple-element.168), channel_id=1, source_target_pairs={{0,3},{16,19},{32,35},{48,51},{64,67},{80,83},{96,99},{112,115}} | collective-permute-start | bytes 1081352 | tf_op jit(solution)/shard_map/ppermute | solution.py:417
  178.2 5.0 %collective-permute-done.27 = bf16[4,352,128]{2,1,0:T(8,128)(2,1)} collective-permute-done((bf16[4,352,128]{2,1,0:T(8,128)(2,1)S(1)}, bf16[4,352,128]{2,1,0:T(8,128)(2,1)}, u32[]{:S(2)}, u32[]{:S(2)}) %collective-permute-start.27) | collective-permute-done | bytes 360480 | tf_op jit(solution)/shard_map/ppermute | solution.py:417
  185.2 7.4 %collective-permute-done.33 = bf16[4,352,128]{2,1,0:T(8,128)(2,1)} collective-permute-done((bf16[4,352,128]{2,1,0:T(8,128)(2,1)}, bf16[4,352,128]{2,1,0:T(8,128)(2,1)}, u32[]{:S(2)}, u32[]{:S(2)}) %collective-permute-start.33) | collective-permute-done | bytes 360480 | tf_op jit(solution)/shard_map/ppermute | solution.py:417
  204.6 5.0 %collective-permute-done.36 = bf16[4,352,128]{2,1,0:T(8,128)(2,1)S(1)} collective-permute-done((bf16[4,352,128]{2,1,0:T(8,128)(2,1)S(1)}, bf16[4,352,128]{2,1,0:T(8,128)(2,1)S(1)}, u32[]{:S(2)}, u32[]{:S(2)}) %collective-permute-start.36) | collective-permute-done | bytes 360480 | tf_op jit(solution)/shard_map/ppermute | solution.py:417
  209.6 5.1 %collective-permute-start.30 = (bf16[4,352,128]{2,1,0:T(8,128)(2,1)S(1)}, bf16[4,352,128]{2,1,0:T(8,128)(2,1)S(1)}, u32[]{:S(2)}, u32[]{:S(2)}) collective-permute-start(bf16[4,352,128]{2,1,0:T(8,128)(2,1)S(1)} %get-tuple-element.162), channel_id=1, source_target_pairs={{0,4},{1,5},{2,6},{3,7},{16,20},{17,21},{18,22},{19,23},{32,36},{3... | collective-permute-start | bytes 1081352 | tf_op jit(solution)/shard_map/ppermute | solution.py:417
  222.9 11.4 %all-to-all-start.7 = ((bf16[128,2,128,128]{3,2,1,0:T(8,128)(2,1)}), bf16[128,2,128,128]{3,2,1,0:T(8,128)(2,1)}, u32[]{:S(2)}, u32[]{:S(2)}) async-start(bf16[128,2,128,128]{3,2,1,0:T(8,128)(2,1)} %bitcast.126), calls=%async_computation.7 | async-start | bytes 16777216 | tf_op jit(solution)/shard_map/all_to_all | solution.py:387
  242.8 99.4 %collective-permute-done.49 = bf16[4,352,128]{2,1,0:T(8,128)(2,1)S(1)} collective-permute-done((bf16[4,352,128]{2,1,0:T(8,128)(2,1)S(1)}, bf16[4,352,128]{2,1,0:T(8,128)(2,1)S(1)}, u32[]{:S(2)}, u32[]{:S(2)}) %collective-permute-start.49) | collective-permute-done | bytes 360480 | tf_op jit(solution)/shard_map/ppermute | solution.py:438
  348.0 6.5 %collective-permute-done.48 = bf16[4,352,128]{2,1,0:T(8,128)(2,1)S(1)} collective-permute-done((bf16[4,352,128]{2,1,0:T(8,128)(2,1)S(1)}, bf16[4,352,128]{2,1,0:T(8,128)(2,1)S(1)}, u32[]{:S(2)}, u32[]{:S(2)}) %collective-permute-start.48) | collective-permute-done | bytes 360480 | tf_op jit(solution)/shard_map/ppermute | solution.py:438
  355.8 16.3 %all-to-all-start.8 = ((bf16[128,1,128,128]{3,2,1,0:T(8,128)(2,1)}), bf16[128,1,128,128]{3,2,1,0:T(8,128)(2,1)}, u32[]{:S(2)}, u32[]{:S(2)}) async-start(bf16[128,1,128,128]{3,2,1,0:T(8,128)(2,1)} %bitcast.128), calls=%async_computation.8 | async-start | bytes 8388608 | tf_op jit(solution)/shard_map/all_to_all | solution.py:387
  386.6 14.9 %shard_map.102 = (bf16[11264,256]{1,0:T(8,128)(2,1)}, bf16[128,256]{1,0:T(8,128)(2,1)}) custom-call(s32[128]{0:T(128)} %slice_bitcast_fusion.16.bins, s32[128]{0:T(128)} %concatenate.11.seconds, s32[128]{0:T(128)S(1)} %compare_select_fusion.pivots, bf16[128,2,128,128]{3,2,1,0:T(8,128)(2,1)} %all-to-all-done.7.x_ref.refs_1_, ...), custom_call_target="tpu_custom_call" | custom-call | flops 8388608 | bytes 22544384 | tf_op jit(solution)/shard_map/pallas_call | solution.py:185
  402.4 21.7 %all-to-all-done.8.x_ref = bf16[128,1,128,128]{3,2,1,0:T(8,128)(2,1)} async-done(((bf16[128,1,128,128]{3,2,1,0:T(8,128)(2,1)}), bf16[128,1,128,128]{3,2,1,0:T(8,128)(2,1)}, u32[]{:S(2)}, u32[]{:S(2)}) %all-to-all-start.8) | async-done | bytes 4194336 | tf_op jit(solution)/shard_map/all_to_all | solution.py:387
  424.1 11.1 %shard_map.104 = (bf16[11264,128]{1,0:T(8,128)(2,1)}, bf16[128,128]{1,0:T(8,128)(2,1)}) custom-call(s32[128]{0:T(128)} %slice_bitcast_fusion.16.bins, s32[128]{0:T(128)} %concatenate.11.seconds, s32[128]{0:T(128)S(1)} %compare_select_fusion.pivots, bf16[128,1,128,128]{3,2,1,0:T(8,128)(2,1)} %all-to-all-done.8.x_ref, ...), custom_call_target="tpu_custom_call" | custom-call | flops 4194304 | bytes 11272192 | tf_op jit(solution)/shard_map/pallas_call | solution.py:185
  452.8 16.8 %conditional.1 = (bf16[11264,512]{1,0:T(8,128)(2,1)}) conditional(s32[]{:T(128)} %convert_element_type.22, (s32[1]{0:T(128)}, bf16[11264,128]{1,0:T(8,128)(2,1)}, bf16[11264,256]{1,0:T(8,128)(2,1)}, bf16[11264,128]{1,0:T(8,128)(2,1)}, bf16[4,4,352,128]{3,2,1,0:T(8,128)(2,1)S(1)}, /*index=5*/bf16[4,4,352,128]{3,2,1,0:T(8,128)(2,1)S(1)}, ...), branch_computations={%region_10.12_spmd, %region_11.13_spmd} | conditional | flops 6164119552 | bytes 271985984 | solution.py:583
  452.9 16.8 %branch_0_fun.1 = bf16[11264,512]{1,0:T(8,128)(2,1)} custom-call(s32[1]{0:T(128)} %get-tuple-element.56.my_pcol, bf16[11264,128]{1,0:T(8,128)(2,1)} %get-tuple-element.58.refs_0_, bf16[11264,256]{1,0:T(8,128)(2,1)} %get-tuple-element.59.refs_1_, bf16[11264,128]{1,0:T(8,128)(2,1)} %get-tuple-element.60.refs_2_, ...), custom_call_target="tpu_custom_call" | custom-call | flops 1845493760 | bytes 23068672 | tf_op jit(solution)/shard_map/cond/branch_0_fun/pallas_call | solution.py:346
  (211 shorter events, 105.8 us)
Async XLA Ops:
  18.7 36.6 %all-to-all-start.4 = ((bf16[16,4,128,128]{3,2,1,0:T(8,128)(2,1)}), bf16[16,4,128,128]{3,2,1,0:T(8,128)(2,1)S(1)}, u32[]{:S(2)}, u32[]{:S(2)}) async-start(bf16[16,4,128,128]{3,2,1,0:T(8,128)(2,1)} %bitcast.136), calls=%async_computation.4 | async-start | bytes 4194304 | tf_op jit(solution)/shard_map/all_to_all | solution.py:387
  56.3 35.4 %collective-permute-start.18 = (bf16[16,1,128,128]{3,2,1,0:T(8,128)(2,1)}, bf16[16,1,128,128]{3,2,1,0:T(8,128)(2,1)S(1)}, u32[]{:S(2)}, u32[]{:S(2)}) collective-permute-start(bf16[16,1,128,128]{3,2,1,0:T(8,128)(2,1)} %slice.144.refs_0_), channel_id=1, source_target_pairs={{0,32},{16,48},{32,64},{48,80},{64,96},{80,112},{96,0},{112,16},{1... | collective-permute-start | bytes 1572872 | tf_op jit(solution)/shard_map/ppermute | solution.py:391
  57.5 34.2 %collective-permute-start.19 = (bf16[16,1,128,128]{3,2,1,0:T(8,128)(2,1)}, bf16[16,1,128,128]{3,2,1,0:T(8,128)(2,1)S(1)}, u32[]{:S(2)}, u32[]{:S(2)}) collective-permute-start(bf16[16,1,128,128]{3,2,1,0:T(8,128)(2,1)} %slice.144.refs_0_), channel_id=1, source_target_pairs={{0,96},{16,112},{32,0},{48,16},{64,32},{80,48},{96,64},{112,80},{1... | collective-permute-start | bytes 1572872 | tf_op jit(solution)/shard_map/ppermute | solution.py:391
  58.9 32.8 %collective-permute-start.20 = (bf16[16,1,128,128]{3,2,1,0:T(8,128)(2,1)}, bf16[16,1,128,128]{3,2,1,0:T(8,128)(2,1)}, u32[]{:S(2)}, u32[]{:S(2)}) collective-permute-start(bf16[16,1,128,128]{3,2,1,0:T(8,128)(2,1)} %slice.144.refs_0_), channel_id=1, source_target_pairs={{0,64},{16,80},{32,96},{48,112},{64,0},{80,16},{96,32},{112,48},{1... | collective-permute-start | bytes 1572872 | tf_op jit(solution)/shard_map/ppermute | solution.py:391
  61.9 29.1 %all-to-all-start.5 = ((s32[128,8,128]{2,1,0:T(8,128)}), s32[128,8,128]{2,1,0:T(8,128)S(1)}, u32[]{:S(2)}, u32[]{:S(2)}) async-start(s32[128,8,128]{2,1,0:T(8,128)} %broadcast_in_dim.89), calls=%async_computation.5 | async-start | bytes 1048576 | tf_op jit(solution)/shard_map/all_to_all | solution.py:492
  92.7 58.2 %all-to-all-start.6 = ((bf16[128,1,128,128]{3,2,1,0:T(8,128)(2,1)}), bf16[128,1,128,128]{3,2,1,0:T(8,128)(2,1)}, u32[]{:S(2)}, u32[]{:S(2)}) async-start(bf16[128,1,128,128]{3,2,1,0:T(8,128)(2,1)} %bitcast.129), calls=%async_computation.6 | async-start | bytes 8388608 | tf_op jit(solution)/shard_map/all_to_all | solution.py:387
  142.2 54.5 %collective-permute-start.37 = (bf16[16,3,128,128]{3,2,1,0:T(8,128)(2,1)}, bf16[16,3,128,128]{3,2,1,0:T(8,128)(2,1)}, u32[]{:S(2)}, u32[]{:S(2)}) collective-permute-start(bf16[16,3,128,128]{3,2,1,0:T(8,128)(2,1)} %shard_map.100.refs_0_), channel_id=1, source_target_pairs={{0,32},{16,48},{32,64},{48,80},{64,96},{80,112},{96,0},{112,16},{1... | collective-permute-start | bytes 4718600 | tf_op jit(solution)/shard_map/ppermute | solution.py:391
  145.9 53.0 %collective-permute-start.39 = (bf16[16,3,128,128]{3,2,1,0:T(8,128)(2,1)}, bf16[16,3,128,128]{3,2,1,0:T(8,128)(2,1)}, u32[]{:S(2)}, u32[]{:S(2)}) collective-permute-start(bf16[16,3,128,128]{3,2,1,0:T(8,128)(2,1)} %shard_map.100.refs_0_), channel_id=1, source_target_pairs={{0,96},{16,112},{32,0},{48,16},{64,32},{80,48},{96,64},{112,80},{1... | collective-permute-start | bytes 4718600 | tf_op jit(solution)/shard_map/ppermute | solution.py:391
  162.0 12.1 %collective-permute-start.25 = (bf16[4,352,128]{2,1,0:T(8,128)(2,1)S(1)}, bf16[4,352,128]{2,1,0:T(8,128)(2,1)S(1)}, u32[]{:S(2)}, u32[]{:S(2)}) collective-permute-start(bf16[4,352,128]{2,1,0:T(8,128)(2,1)S(1)} %get-tuple-element.168), channel_id=1, source_target_pairs={{0,3},{16,19},{32,35},{48,51},{64,67},{80,83},{96,99},{112,115}} | collective-permute-start | bytes 1081352 | tf_op jit(solution)/shard_map/ppermute | solution.py:417
  169.1 14.1 %collective-permute-start.27 = (bf16[4,352,128]{2,1,0:T(8,128)(2,1)S(1)}, bf16[4,352,128]{2,1,0:T(8,128)(2,1)}, u32[]{:S(2)}, u32[]{:S(2)}) collective-permute-start(bf16[4,352,128]{2,1,0:T(8,128)(2,1)S(1)} %get-tuple-element.166), channel_id=1, source_target_pairs={{0,1},{16,17},{32,33},{48,49},{64,65},{80,81},{96,97},{112,113}} | collective-permute-start | bytes 1081352 | tf_op jit(solution)/shard_map/ppermute | solution.py:417
  174.1 11.1 %collective-permute-start.31 = (bf16[4,352,128]{2,1,0:T(8,128)(2,1)}, bf16[4,352,128]{2,1,0:T(8,128)(2,1)}, u32[]{:S(2)}, u32[]{:S(2)}) collective-permute-start(bf16[4,352,128]{2,1,0:T(8,128)(2,1)} %get-tuple-element.165), channel_id=1, source_target_pairs={{0,12},{16,28},{32,44},{48,60},{64,76},{80,92},{96,108},{112,124}} | collective-permute-start | bytes 1081352 | tf_op jit(solution)/shard_map/ppermute | solution.py:417
  195.4 14.2 %collective-permute-start.36 = (bf16[4,352,128]{2,1,0:T(8,128)(2,1)S(1)}, bf16[4,352,128]{2,1,0:T(8,128)(2,1)S(1)}, u32[]{:S(2)}, u32[]{:S(2)}) collective-permute-start(bf16[4,352,128]{2,1,0:T(8,128)(2,1)S(1)} %get-tuple-element.161), channel_id=1, source_target_pairs={{0,1},{4,5},{8,9},{12,13},{16,17},{20,21},{24,25},{28,29},{32,33},... | collective-permute-start | bytes 1081352 | tf_op jit(solution)/shard_map/ppermute | solution.py:417
  197.9 23.2 %collective-permute-start.38 = (bf16[8,3,128,128]{3,2,1,0:T(8,128)(2,1)S(1)}, bf16[8,3,128,128]{3,2,1,0:T(8,128)(2,1)S(1)}, u32[]{:S(2)}, u32[]{:S(2)}) collective-permute-start(bf16[8,3,128,128]{3,2,1,0:T(8,128)(2,1)S(1)} %slice.154), channel_id=1, source_target_pairs={{0,32},{16,48},{32,64},{48,80},{64,96},{80,112},{96,0},{112,16},{1... | collective-permute-start | bytes 2359304 | tf_op jit(solution)/shard_map/ppermute | solution.py:391
  200.1 21.1 %collective-permute-start.40 = (bf16[8,3,128,128]{3,2,1,0:T(8,128)(2,1)S(1)}, bf16[8,3,128,128]{3,2,1,0:T(8,128)(2,1)S(1)}, u32[]{:S(2)}, u32[]{:S(2)}) collective-permute-start(bf16[8,3,128,128]{3,2,1,0:T(8,128)(2,1)S(1)} %slice.155), channel_id=1, source_target_pairs={{0,96},{16,112},{32,0},{48,16},{64,32},{80,48},{96,64},{112,80},{1... | collective-permute-start | bytes 2359304 | tf_op jit(solution)/shard_map/ppermute | solution.py:391
  202.0 13.6 %collective-permute-start.28 = (bf16[4,352,128]{2,1,0:T(8,128)(2,1)S(1)}, bf16[4,352,128]{2,1,0:T(8,128)(2,1)S(1)}, u32[]{:S(2)}, u32[]{:S(2)}) collective-permute-start(bf16[4,352,128]{2,1,0:T(8,128)(2,1)S(1)} %get-tuple-element.162), channel_id=1, source_target_pairs={{0,12},{1,13},{2,14},{3,15},{16,28},{17,29},{18,30},{19,31},{32,44... | collective-permute-start | bytes 1081352 | tf_op jit(solution)/shard_map/ppermute | solution.py:417
  203.3 12.3 %collective-permute-start.29 = (bf16[4,352,128]{2,1,0:T(8,128)(2,1)S(1)}, bf16[4,352,128]{2,1,0:T(8,128)(2,1)S(1)}, u32[]{:S(2)}, u32[]{:S(2)}) collective-permute-start(bf16[4,352,128]{2,1,0:T(8,128)(2,1)S(1)} %get-tuple-element.162), channel_id=1, source_target_pairs={{0,8},{1,9},{2,10},{3,11},{16,24},{17,25},{18,26},{19,27},{32,40},... | collective-permute-start | bytes 1081352 | tf_op jit(solution)/shard_map/ppermute | solution.py:417
  222.9 131.8 %all-to-all-start.7 = ((bf16[128,2,128,128]{3,2,1,0:T(8,128)(2,1)}), bf16[128,2,128,128]{3,2,1,0:T(8,128)(2,1)}, u32[]{:S(2)}, u32[]{:S(2)}) async-start(bf16[128,2,128,128]{3,2,1,0:T(8,128)(2,1)} %bitcast.126), calls=%async_computation.7 | async-start | bytes 16777216 | tf_op jit(solution)/shard_map/all_to_all | solution.py:387
  234.4 107.8 %collective-permute-start.49 = (bf16[4,352,128]{2,1,0:T(8,128)(2,1)S(1)}, bf16[4,352,128]{2,1,0:T(8,128)(2,1)S(1)}, u32[]{:S(2)}, u32[]{:S(2)}) collective-permute-start(bf16[4,352,128]{2,1,0:T(8,128)(2,1)S(1)} %copy-done.12), channel_id=1, source_target_pairs={{0,4},{1,5},{2,6},{3,7},{4,0},{5,1},{6,2},{7,3},{8,12},{9,13},{10,... | collective-permute-start | bytes 1081352 | tf_op jit(solution)/shard_map/ppermute | solution.py:438
  235.8 111.8 %collective-permute-start.50 = (bf16[4,352,128]{2,1,0:T(8,128)(2,1)S(1)}, bf16[4,352,128]{2,1,0:T(8,128)(2,1)S(1)}, u32[]{:S(2)}, u32[]{:S(2)}) collective-permute-start(bf16[4,352,128]{2,1,0:T(8,128)(2,1)S(1)} %copy-done.12), channel_id=1, source_target_pairs={{0,8},{1,9},{2,10},{3,11},{4,12},{5,13},{6,14},{7,15},{8,0},{9,1},... | collective-permute-start | bytes 1081352 | tf_op jit(solution)/shard_map/ppermute | solution.py:438
  238.3 109.3 %collective-permute-start.51 = (bf16[4,352,128]{2,1,0:T(8,128)(2,1)S(1)}, bf16[4,352,128]{2,1,0:T(8,128)(2,1)S(1)}, u32[]{:S(2)}, u32[]{:S(2)}) collective-permute-start(bf16[4,352,128]{2,1,0:T(8,128)(2,1)S(1)} %copy-done.12), channel_id=1, source_target_pairs={{0,12},{1,13},{2,14},{3,15},{4,8},{5,9},{6,10},{7,11},{8,4},{9,5},... | collective-permute-start | bytes 1081352 | tf_op jit(solution)/shard_map/ppermute | solution.py:438
  238.3 109.5 %collective-permute-start.46 = (bf16[4,352,128]{2,1,0:T(8,128)(2,1)S(1)}, bf16[4,352,128]{2,1,0:T(8,128)(2,1)S(1)}, u32[]{:S(2)}, u32[]{:S(2)}) collective-permute-start(bf16[4,352,128]{2,1,0:T(8,128)(2,1)S(1)} %copy-done.13), channel_id=1, source_target_pairs={{0,1},{1,0},{2,3},{3,2},{4,5},{5,4},{6,7},{7,6},{8,9},{9,8},{10,11... | collective-permute-start | bytes 1081352 | tf_op jit(solution)/shard_map/ppermute | solution.py:438
  239.8 108.2 %collective-permute-start.47 = (bf16[4,352,128]{2,1,0:T(8,128)(2,1)S(1)}, bf16[4,352,128]{2,1,0:T(8,128)(2,1)S(1)}, u32[]{:S(2)}, u32[]{:S(2)}) collective-permute-start(bf16[4,352,128]{2,1,0:T(8,128)(2,1)S(1)} %copy-done.13), channel_id=1, source_target_pairs={{0,2},{1,3},{2,0},{3,1},{4,6},{5,7},{6,4},{7,5},{8,10},{9,11},{10,... | collective-permute-start | bytes 1081352 | tf_op jit(solution)/shard_map/ppermute | solution.py:438
  342.2 12.3 %collective-permute-start.48 = (bf16[4,352,128]{2,1,0:T(8,128)(2,1)S(1)}, bf16[4,352,128]{2,1,0:T(8,128)(2,1)S(1)}, u32[]{:S(2)}, u32[]{:S(2)}) collective-permute-start(bf16[4,352,128]{2,1,0:T(8,128)(2,1)S(1)} %copy-done.13), channel_id=1, source_target_pairs={{0,3},{1,2},{2,1},{3,0},{4,7},{5,6},{6,5},{7,4},{8,11},{9,10},{10,... | collective-permute-start | bytes 1081352 | tf_op jit(solution)/shard_map/ppermute | solution.py:438
  355.8 68.3 %all-to-all-start.8 = ((bf16[128,1,128,128]{3,2,1,0:T(8,128)(2,1)}), bf16[128,1,128,128]{3,2,1,0:T(8,128)(2,1)}, u32[]{:S(2)}, u32[]{:S(2)}) async-start(bf16[128,1,128,128]{3,2,1,0:T(8,128)(2,1)} %bitcast.128), calls=%async_computation.8 | async-start | bytes 8388608 | tf_op jit(solution)/shard_map/all_to_all | solution.py:387
  (64 other events, 1220.5 us)

commit v6 on v5

--- a/solution.py
+++ b/solution.py
@@ -481,11 +481,11 @@
         )
         for first, width in CHUNKS
     }
-    near_parts, near_places = gather_direct(own[:, :1])
+    near_parts, near_places = gather_direct(after(own[:, :1], packed[0]))
     far_own = after(own[:, 1:], *[packed[first] for first, _ in CHUNKS[1:]])
     far_parts, far_places = gather_relayed(far_own)
 
-    code = after(owners * FRONT_TILES + row_local, own)
+    code = after(owners * FRONT_TILES + row_local, own, packed[0])
     codes = jnp.pad(
         code[None, :], ((0, 0), (0, TILE - OWN_TILES))
     )

time: 472 us -> 474 us (level)
  blocking collectives: 0 us -> 29.9 us
  waiting for transfers between devices: 205 us -> 181 us
    all_to_all x0 -> x1, blocking collectives: none -> 29.9 us  [on_device(): lax.all_to_all(jnp.broadcast_to(codes[None], (N_DEV, 8, TILE)), ('prow',...]
    all_to_all x4, waiting for transfers between devices: 49.1 us -> 35.3 us  [exchange(): return lax.all_to_all(parts, axes, split_axis=0, concat_axis=0, tiled=True)]
    all_to_all x1 -> x0, starting transfers between devices: 8.54 us -> none  [on_device(): lax.all_to_all(jnp.broadcast_to(codes[None], (N_DEV, 8, TILE)), ('prow',...]
    all_to_all x1 -> x0, waiting for transfers between devices: 6.19 us -> none  [on_device(): lax.all_to_all(jnp.broadcast_to(codes[None], (N_DEV, 8, TILE)), ('prow',...]
    unnamed x92 -> x94, local copies, waits for them, and re-layouts: 10.6 us -> 10.3 us
  transfers between devices with their start and end apart: 43 -> 42, of which waited for: 18 -> 18; matrix products, arithmetic and copies ran while one was open for 3% -> 3% of each run, Pallas kernels for 17% -> 17%
where the time goes in v6:
time: 474 us; the launch traced here: 471 us
  waiting for transfers between devices  181 us (38%)
  Pallas kernels  123 us (26%)
  starting transfers between devices  107 us (23%)
  blocking collectives  29.9 us (6%)
  local copies, waits for them, and re-layouts  19.7 us (4%)
  other arithmetic  9.43 us (2%)
    ppermute x6, waiting for transfers between devices, along(): lax.ppermute(value, 'pcol', [(q, q ^ stride * i) for q in range(N_PCOL)])  107 us
    pallas_call x3, Pallas kernels, pack(): pl.pallas_call(functools.partial(pack_kernel, first, ranks), out_shape=ja...  55.5 us
    all_to_all x4, starting transfers between devices, exchange(): return lax.all_to_all(parts, axes, split_axis=0, concat_axis=0, tiled=True)  45.3 us
    pallas_call x3, Pallas kernels, sum_chunk(): pl.pallas_call(functools.partial(sum_kernel, width, counts), out_shape=[j...  35.8 us
    all_to_all x4, waiting for transfers between devices, exchange(): return lax.all_to_all(parts, axes, split_axis=0, concat_axis=0, tiled=True)  35.3 us
    all_to_all x1, blocking collectives, on_device(): lax.all_to_all(jnp.broadcast_to(codes[None], (N_DEV, 8, TILE)), ('prow',...  29.9 us
    ppermute x12, starting transfers between devices, from_first(): lax.ppermute(values[i], 'pcol', pairs(i))  26.3 us
    ppermute x12, waiting for transfers between devices, from_first(): lax.ppermute(values[i], 'pcol', pairs(i))  21.5 us
  transfers between devices with their start and end apart: 42, of which 18 were waited for; matrix products, arithmetic and copies ran while one was open for 3% of the time, Pallas kernels for 17%

profile of v6, /device:TPU:1, one launch (start us, length us, event | category | flops | bytes accessed | tf_op | source)
XLA Modules:
  0.0 471.3 jit_solution(13275919619790004217)
XLA Ops:
  3.8 15.0 %shard_map.93 = bf16[64,128,128]{2,1,0:T(8,128)(2,1)} custom-call(s32[64]{0:T(128)S(1)} %get-tuple-element.150.src, s32[64]{0:T(128)S(1)} %get-tuple-element.149.present, s32[1]{0:T(128)} %bitcast.22.which, bf16[1024,6144]{1,0:T(8,128)(2,1)} %x_ref.7, s32[48,128]{1,0:T(8,128)} %fusion.30.cw_ref, s32[8,128]{1,0:T(8,128)} %rw_ref.7), custom_call_target="tpu_custom_call" | custom-call | flops 536870912 | bytes 4194304 | tf_op jit(solution)/shard_map/pallas_call | solution.py:114
  18.8 8.7 %all-to-all-start.4 = ((bf16[16,4,128,128]{3,2,1,0:T(8,128)(2,1)}), bf16[16,4,128,128]{3,2,1,0:T(8,128)(2,1)S(1)}, u32[]{:S(2)}, u32[]{:S(2)}) async-start(bf16[16,4,128,128]{3,2,1,0:T(8,128)(2,1)} %bitcast.136), calls=%async_computation.4 | async-start | bytes 4194304 | tf_op jit(solution)/shard_map/all_to_all | solution.py:387
  27.6 14.3 %shard_map.94.refs_2_.refs_1_.refs_0_ = bf16[8,16,1,1,128,128]{5,4,3,2,1,0:T(8,128)(2,1)} custom-call(s32[64]{0:T(128)S(1)} %get-tuple-element.150.src, s32[64]{0:T(128)S(1)} %get-tuple-element.149.present, s32[8]{0:T(128)S(1)} %bitcast.167, s32[8]{0:T(128)S(1)} %convert_reduce_fusion.4.rank, bf16[1024,6144]{1,0:T(8,128)(2,1)} %x_ref.7, ...), custom_call_target="tpu_custom_call" | custom-call | flops 1073741824 | bytes 12582912 | tf_op jit(solution)/shard_map/pallas_call | solution.py:68
  42.4 13.0 %all-to-all-done.4.refs_1_ = bf16[16,4,128,128]{3,2,1,0:T(8,128)(2,1)S(1)} async-done(((bf16[16,4,128,128]{3,2,1,0:T(8,128)(2,1)}), bf16[16,4,128,128]{3,2,1,0:T(8,128)(2,1)S(1)}, u32[]{:S(2)}, u32[]{:S(2)}) %all-to-all-start.4) | async-done | bytes 2097184 | tf_op jit(solution)/shard_map/all_to_all | solution.py:387
  61.7 29.9 %all_to_all.41 = s32[128,8,128]{2,1,0:T(8,128)S(1)} all-to-all(s32[128,8,128]{2,1,0:T(8,128)S(1)} %broadcast_in_dim.89), channel_id=1, replica_groups=mesh['prow'=8,'pcol'=16] {'prow','pcol'}, dimensions={0} | all-to-all | bytes 1048576 | tf_op jit(solution)/shard_map/all_to_all | solution.py:492
  93.5 6.0 %all-to-all-start.6 = ((bf16[128,1,128,128]{3,2,1,0:T(8,128)(2,1)}), bf16[128,1,128,128]{3,2,1,0:T(8,128)(2,1)}, u32[]{:S(2)}, u32[]{:S(2)}) async-start(bf16[128,1,128,128]{3,2,1,0:T(8,128)(2,1)} %bitcast.127), calls=%async_computation.6 | async-start | bytes 8388608 | tf_op jit(solution)/shard_map/all_to_all | solution.py:387
  99.7 14.0 %shard_map.100.refs_2_.refs_0_ = bf16[8,16,1,1,128,128]{5,4,3,2,1,0:T(8,128)(2,1)} custom-call(s32[64]{0:T(128)S(1)} %get-tuple-element.150.src, s32[64]{0:T(128)S(1)} %get-tuple-element.149.present, s32[8]{0:T(128)S(1)} %bitcast.168, s32[8]{0:T(128)S(1)} %convert_reduce_fusion.4.rank, bf16[1024,6144]{1,0:T(8,128)(2,1)} %x_ref.7, ...), custom_call_target="tpu_custom_call" | custom-call | flops 1073741824 | bytes 12582912 | tf_op jit(solution)/shard_map/pallas_call | solution.py:68
  113.8 27.2 %shard_map.99.refs_1_.refs_0_ = bf16[8,16,1,2,128,128]{5,4,3,2,1,0:T(8,128)(2,1)} custom-call(s32[64]{0:T(128)S(1)} %get-tuple-element.150.src, s32[64]{0:T(128)S(1)} %get-tuple-element.149.present, s32[8]{0:T(128)S(1)} %bitcast.169, s32[8]{0:T(128)S(1)} %convert_reduce_fusion.4.rank, bf16[1024,6144]{1,0:T(8,128)(2,1)} %x_ref.7, ...), custom_call_target="tpu_custom_call" | custom-call | flops 2147483648 | bytes 25165824 | tf_op jit(solution)/shard_map/pallas_call | solution.py:68
  151.5 9.9 %shard_map.98 = (bf16[11264,128]{1,0:T(8,128)(2,1)S(1)}, bf16[128,128]{1,0:T(8,128)(2,1)}) custom-call(s32[128]{0:T(128)} %slice_bitcast_fusion.16.bins, s32[128]{0:T(128)} %concatenate.11.seconds, s32[128]{0:T(128)S(1)} %compare_select_fusion.pivots, bf16[128,1,128,128]{3,2,1,0:T(8,128)(2,1)} %all-to-all-done.6.x_ref, ...), custom_call_target="tpu_custom_call" | custom-call | flops 4194304 | bytes 11272192 | tf_op jit(solution)/shard_map/pallas_call | solution.py:185
  177.6 5.0 %collective-permute-done.27 = bf16[4,352,128]{2,1,0:T(8,128)(2,1)} collective-permute-done((bf16[4,352,128]{2,1,0:T(8,128)(2,1)S(1)}, bf16[4,352,128]{2,1,0:T(8,128)(2,1)}, u32[]{:S(2)}, u32[]{:S(2)}) %collective-permute-start.27) | collective-permute-done | bytes 360480 | tf_op jit(solution)/shard_map/ppermute | solution.py:417
  184.6 6.7 %collective-permute-done.33 = bf16[4,352,128]{2,1,0:T(8,128)(2,1)} collective-permute-done((bf16[4,352,128]{2,1,0:T(8,128)(2,1)}, bf16[4,352,128]{2,1,0:T(8,128)(2,1)}, u32[]{:S(2)}, u32[]{:S(2)}) %collective-permute-start.33) | collective-permute-done | bytes 360480 | tf_op jit(solution)/shard_map/ppermute | solution.py:417
  207.7 5.1 %collective-permute-start.30 = (bf16[4,352,128]{2,1,0:T(8,128)(2,1)S(1)}, bf16[4,352,128]{2,1,0:T(8,128)(2,1)S(1)}, u32[]{:S(2)}, u32[]{:S(2)}) collective-permute-start(bf16[4,352,128]{2,1,0:T(8,128)(2,1)S(1)} %get-tuple-element.162), channel_id=1, source_target_pairs={{0,4},{1,5},{2,6},{3,7},{16,20},{17,21},{18,22},{19,23},{32,36},{3... | collective-permute-start | bytes 1081352 | tf_op jit(solution)/shard_map/ppermute | solution.py:417
  213.6 5.5 %collective-permute-done.30 = bf16[4,352,128]{2,1,0:T(8,128)(2,1)S(1)} collective-permute-done((bf16[4,352,128]{2,1,0:T(8,128)(2,1)S(1)}, bf16[4,352,128]{2,1,0:T(8,128)(2,1)S(1)}, u32[]{:S(2)}, u32[]{:S(2)}) %collective-permute-start.30) | collective-permute-done | bytes 360480 | tf_op jit(solution)/shard_map/ppermute | solution.py:417
  221.8 14.3 %all-to-all-start.7 = ((bf16[128,2,128,128]{3,2,1,0:T(8,128)(2,1)}), bf16[128,2,128,128]{3,2,1,0:T(8,128)(2,1)}, u32[]{:S(2)}, u32[]{:S(2)}) async-start(bf16[128,2,128,128]{3,2,1,0:T(8,128)(2,1)} %bitcast.126), calls=%async_computation.7 | async-start | bytes 16777216 | tf_op jit(solution)/shard_map/all_to_all | solution.py:387
  244.4 99.4 %collective-permute-done.49 = bf16[4,352,128]{2,1,0:T(8,128)(2,1)S(1)} collective-permute-done((bf16[4,352,128]{2,1,0:T(8,128)(2,1)S(1)}, bf16[4,352,128]{2,1,0:T(8,128)(2,1)S(1)}, u32[]{:S(2)}, u32[]{:S(2)}) %collective-permute-start.49) | collective-permute-done | bytes 360480 | tf_op jit(solution)/shard_map/ppermute | solution.py:438
  343.9 4.7 %collective-permute-start.48 = (bf16[4,352,128]{2,1,0:T(8,128)(2,1)S(1)}, bf16[4,352,128]{2,1,0:T(8,128)(2,1)S(1)}, u32[]{:S(2)}, u32[]{:S(2)}) collective-permute-start(bf16[4,352,128]{2,1,0:T(8,128)(2,1)S(1)} %copy-done.14), channel_id=1, source_target_pairs={{0,3},{1,2},{2,1},{3,0},{4,7},{5,6},{6,5},{7,4},{8,11},{9,10},{10,... | collective-permute-start | bytes 1081352 | tf_op jit(solution)/shard_map/ppermute | solution.py:438
  349.7 6.5 %collective-permute-done.48 = bf16[4,352,128]{2,1,0:T(8,128)(2,1)S(1)} collective-permute-done((bf16[4,352,128]{2,1,0:T(8,128)(2,1)S(1)}, bf16[4,352,128]{2,1,0:T(8,128)(2,1)S(1)}, u32[]{:S(2)}, u32[]{:S(2)}) %collective-permute-start.48) | collective-permute-done | bytes 360480 | tf_op jit(solution)/shard_map/ppermute | solution.py:438
  357.5 16.3 %all-to-all-start.8 = ((bf16[128,1,128,128]{3,2,1,0:T(8,128)(2,1)}), bf16[128,1,128,128]{3,2,1,0:T(8,128)(2,1)}, u32[]{:S(2)}, u32[]{:S(2)}) async-start(bf16[128,1,128,128]{3,2,1,0:T(8,128)(2,1)} %bitcast.129), calls=%async_computation.8 | async-start | bytes 8388608 | tf_op jit(solution)/shard_map/all_to_all | solution.py:387
  388.3 14.8 %shard_map.103 = (bf16[11264,256]{1,0:T(8,128)(2,1)}, bf16[128,256]{1,0:T(8,128)(2,1)}) custom-call(s32[128]{0:T(128)} %slice_bitcast_fusion.16.bins, s32[128]{0:T(128)} %concatenate.11.seconds, s32[128]{0:T(128)S(1)} %compare_select_fusion.pivots, bf16[128,2,128,128]{3,2,1,0:T(8,128)(2,1)} %all-to-all-done.7.x_ref.refs_1_, ...), custom_call_target="tpu_custom_call" | custom-call | flops 8388608 | bytes 22544384 | tf_op jit(solution)/shard_map/pallas_call | solution.py:185
  404.0 21.8 %all-to-all-done.8.x_ref = bf16[128,1,128,128]{3,2,1,0:T(8,128)(2,1)} async-done(((bf16[128,1,128,128]{3,2,1,0:T(8,128)(2,1)}), bf16[128,1,128,128]{3,2,1,0:T(8,128)(2,1)}, u32[]{:S(2)}, u32[]{:S(2)}) %all-to-all-start.8) | async-done | bytes 4194336 | tf_op jit(solution)/shard_map/all_to_all | solution.py:387
  425.8 11.0 %shard_map.105 = (bf16[11264,128]{1,0:T(8,128)(2,1)}, bf16[128,128]{1,0:T(8,128)(2,1)}) custom-call(s32[128]{0:T(128)} %slice_bitcast_fusion.16.bins, s32[128]{0:T(128)} %concatenate.11.seconds, s32[128]{0:T(128)S(1)} %compare_select_fusion.pivots, bf16[128,1,128,128]{3,2,1,0:T(8,128)(2,1)} %all-to-all-done.8.x_ref, ...), custom_call_target="tpu_custom_call" | custom-call | flops 4194304 | bytes 11272192 | tf_op jit(solution)/shard_map/pallas_call | solution.py:185
  445.4 4.8 %collective-permute-done.54 = bf16[128,512]{1,0:T(8,128)(2,1)S(1)} collective-permute-done((bf16[128,512]{1,0:T(8,128)(2,1)S(1)}, bf16[128,512]{1,0:T(8,128)(2,1)S(1)}, u32[]{:S(2)}, u32[]{:S(2)}) %collective-permute-start.54) | collective-permute-done | bytes 131104 | tf_op jit(solution)/shard_map/ppermute | solution.py:553
  454.5 16.8 %conditional.1 = (bf16[11264,512]{1,0:T(8,128)(2,1)}) conditional(s32[]{:T(128)} %convert_element_type.22, (s32[1]{0:T(128)}, bf16[11264,128]{1,0:T(8,128)(2,1)}, bf16[11264,256]{1,0:T(8,128)(2,1)}, bf16[11264,128]{1,0:T(8,128)(2,1)}, bf16[4,4,352,128]{3,2,1,0:T(8,128)(2,1)S(1)}, /*index=5*/bf16[4,4,352,128]{3,2,1,0:T(8,128)(2,1)S(1)}, ...), branch_computations={%region_10.12_spmd, %region_11.13_spmd} | conditional | flops 6164119552 | bytes 271985984 | solution.py:583
  454.5 16.8 %branch_0_fun.1 = bf16[11264,512]{1,0:T(8,128)(2,1)} custom-call(s32[1]{0:T(128)} %get-tuple-element.56.my_pcol, bf16[11264,128]{1,0:T(8,128)(2,1)} %get-tuple-element.58.refs_0_, bf16[11264,256]{1,0:T(8,128)(2,1)} %get-tuple-element.59.refs_1_, bf16[11264,128]{1,0:T(8,128)(2,1)} %get-tuple-element.60.refs_2_, ...), custom_call_target="tpu_custom_call" | custom-call | flops 1845493760 | bytes 23068672 | tf_op jit(solution)/shard_map/cond/branch_0_fun/pallas_call | solution.py:346
  (213 shorter events, 98.9 us)
Async XLA Ops:
  18.8 36.6 %all-to-all-start.4 = ((bf16[16,4,128,128]{3,2,1,0:T(8,128)(2,1)}), bf16[16,4,128,128]{3,2,1,0:T(8,128)(2,1)S(1)}, u32[]{:S(2)}, u32[]{:S(2)}) async-start(bf16[16,4,128,128]{3,2,1,0:T(8,128)(2,1)} %bitcast.136), calls=%async_computation.4 | async-start | bytes 4194304 | tf_op jit(solution)/shard_map/all_to_all | solution.py:387
  56.9 35.4 %collective-permute-start.18 = (bf16[16,1,128,128]{3,2,1,0:T(8,128)(2,1)}, bf16[16,1,128,128]{3,2,1,0:T(8,128)(2,1)S(1)}, u32[]{:S(2)}, u32[]{:S(2)}) collective-permute-start(bf16[16,1,128,128]{3,2,1,0:T(8,128)(2,1)} %shard_map.96.refs_0_), channel_id=1, source_target_pairs={{0,32},{16,48},{32,64},{48,80},{64,96},{80,112},{96,0},{112,16},{1... | collective-permute-start | bytes 1572872 | tf_op jit(solution)/shard_map/ppermute | solution.py:391
  58.1 34.2 %collective-permute-start.19 = (bf16[16,1,128,128]{3,2,1,0:T(8,128)(2,1)}, bf16[16,1,128,128]{3,2,1,0:T(8,128)(2,1)S(1)}, u32[]{:S(2)}, u32[]{:S(2)}) collective-permute-start(bf16[16,1,128,128]{3,2,1,0:T(8,128)(2,1)} %shard_map.96.refs_0_), channel_id=1, source_target_pairs={{0,96},{16,112},{32,0},{48,16},{64,32},{80,48},{96,64},{112,80},{1... | collective-permute-start | bytes 1572872 | tf_op jit(solution)/shard_map/ppermute | solution.py:391
  59.6 32.8 %collective-permute-start.20 = (bf16[16,1,128,128]{3,2,1,0:T(8,128)(2,1)}, bf16[16,1,128,128]{3,2,1,0:T(8,128)(2,1)S(1)}, u32[]{:S(2)}, u32[]{:S(2)}) collective-permute-start(bf16[16,1,128,128]{3,2,1,0:T(8,128)(2,1)} %shard_map.96.refs_0_), channel_id=1, source_target_pairs={{0,64},{16,80},{32,96},{48,112},{64,0},{80,16},{96,32},{112,48},{1... | collective-permute-start | bytes 1572872 | tf_op jit(solution)/shard_map/ppermute | solution.py:391
  93.5 58.0 %all-to-all-start.6 = ((bf16[128,1,128,128]{3,2,1,0:T(8,128)(2,1)}), bf16[128,1,128,128]{3,2,1,0:T(8,128)(2,1)}, u32[]{:S(2)}, u32[]{:S(2)}) async-start(bf16[128,1,128,128]{3,2,1,0:T(8,128)(2,1)} %bitcast.127), calls=%async_computation.6 | async-start | bytes 8388608 | tf_op jit(solution)/shard_map/all_to_all | solution.py:387
  143.7 51.8 %collective-permute-start.37 = (bf16[16,3,128,128]{3,2,1,0:T(8,128)(2,1)}, bf16[16,3,128,128]{3,2,1,0:T(8,128)(2,1)}, u32[]{:S(2)}, u32[]{:S(2)}) collective-permute-start(bf16[16,3,128,128]{3,2,1,0:T(8,128)(2,1)} %shard_map.101.refs_0_), channel_id=1, source_target_pairs={{0,32},{16,48},{32,64},{48,80},{64,96},{80,112},{96,0},{112,16},{1... | collective-permute-start | bytes 4718600 | tf_op jit(solution)/shard_map/ppermute | solution.py:391
  147.5 50.5 %collective-permute-start.39 = (bf16[16,3,128,128]{3,2,1,0:T(8,128)(2,1)}, bf16[16,3,128,128]{3,2,1,0:T(8,128)(2,1)}, u32[]{:S(2)}, u32[]{:S(2)}) collective-permute-start(bf16[16,3,128,128]{3,2,1,0:T(8,128)(2,1)} %shard_map.101.refs_0_), channel_id=1, source_target_pairs={{0,96},{16,112},{32,0},{48,16},{64,32},{80,48},{96,64},{112,80},{1... | collective-permute-start | bytes 4718600 | tf_op jit(solution)/shard_map/ppermute | solution.py:391
  162.6 10.9 %collective-permute-start.25 = (bf16[4,352,128]{2,1,0:T(8,128)(2,1)S(1)}, bf16[4,352,128]{2,1,0:T(8,128)(2,1)S(1)}, u32[]{:S(2)}, u32[]{:S(2)}) collective-permute-start(bf16[4,352,128]{2,1,0:T(8,128)(2,1)S(1)} %get-tuple-element.168), channel_id=1, source_target_pairs={{0,3},{16,19},{32,35},{48,51},{64,67},{80,83},{96,99},{112,115}} | collective-permute-start | bytes 1081352 | tf_op jit(solution)/shard_map/ppermute | solution.py:417
  169.2 13.4 %collective-permute-start.27 = (bf16[4,352,128]{2,1,0:T(8,128)(2,1)S(1)}, bf16[4,352,128]{2,1,0:T(8,128)(2,1)}, u32[]{:S(2)}, u32[]{:S(2)}) collective-permute-start(bf16[4,352,128]{2,1,0:T(8,128)(2,1)S(1)} %get-tuple-element.166), channel_id=1, source_target_pairs={{0,1},{16,17},{32,33},{48,49},{64,65},{80,81},{96,97},{112,113}} | collective-permute-start | bytes 1081352 | tf_op jit(solution)/shard_map/ppermute | solution.py:417
  173.5 11.1 %collective-permute-start.31 = (bf16[4,352,128]{2,1,0:T(8,128)(2,1)}, bf16[4,352,128]{2,1,0:T(8,128)(2,1)}, u32[]{:S(2)}, u32[]{:S(2)}) collective-permute-start(bf16[4,352,128]{2,1,0:T(8,128)(2,1)} %get-tuple-element.165), channel_id=1, source_target_pairs={{0,12},{16,28},{32,44},{48,60},{64,76},{80,92},{96,108},{112,124}} | collective-permute-start | bytes 1081352 | tf_op jit(solution)/shard_map/ppermute | solution.py:417
  191.5 11.7 %collective-permute-start.34 = (bf16[4,352,128]{2,1,0:T(8,128)(2,1)S(1)}, bf16[4,352,128]{2,1,0:T(8,128)(2,1)S(1)}, u32[]{:S(2)}, u32[]{:S(2)}) collective-permute-start(bf16[4,352,128]{2,1,0:T(8,128)(2,1)S(1)} %get-tuple-element.161), channel_id=1, source_target_pairs={{0,3},{4,7},{8,11},{12,15},{16,19},{20,23},{24,27},{28,31},{32,35}... | collective-permute-start | bytes 1081352 | tf_op jit(solution)/shard_map/ppermute | solution.py:417
  192.8 11.6 %collective-permute-start.35 = (bf16[4,352,128]{2,1,0:T(8,128)(2,1)S(1)}, bf16[4,352,128]{2,1,0:T(8,128)(2,1)S(1)}, u32[]{:S(2)}, u32[]{:S(2)}) collective-permute-start(bf16[4,352,128]{2,1,0:T(8,128)(2,1)S(1)} %get-tuple-element.161), channel_id=1, source_target_pairs={{0,2},{4,6},{8,10},{12,14},{16,18},{20,22},{24,26},{28,30},{32,34}... | collective-permute-start | bytes 1081352 | tf_op jit(solution)/shard_map/ppermute | solution.py:417
  194.1 13.5 %collective-permute-start.36 = (bf16[4,352,128]{2,1,0:T(8,128)(2,1)S(1)}, bf16[4,352,128]{2,1,0:T(8,128)(2,1)S(1)}, u32[]{:S(2)}, u32[]{:S(2)}) collective-permute-start(bf16[4,352,128]{2,1,0:T(8,128)(2,1)S(1)} %get-tuple-element.161), channel_id=1, source_target_pairs={{0,1},{4,5},{8,9},{12,13},{16,17},{20,21},{24,25},{28,29},{32,33},... | collective-permute-start | bytes 1081352 | tf_op jit(solution)/shard_map/ppermute | solution.py:417
  196.7 23.3 %collective-permute-start.38 = (bf16[8,3,128,128]{3,2,1,0:T(8,128)(2,1)S(1)}, bf16[8,3,128,128]{3,2,1,0:T(8,128)(2,1)S(1)}, u32[]{:S(2)}, u32[]{:S(2)}) collective-permute-start(bf16[8,3,128,128]{3,2,1,0:T(8,128)(2,1)S(1)} %slice.154), channel_id=1, source_target_pairs={{0,32},{16,48},{32,64},{48,80},{64,96},{80,112},{96,0},{112,16},{1... | collective-permute-start | bytes 2359304 | tf_op jit(solution)/shard_map/ppermute | solution.py:391
  199.2 20.8 %collective-permute-start.40 = (bf16[8,3,128,128]{3,2,1,0:T(8,128)(2,1)S(1)}, bf16[8,3,128,128]{3,2,1,0:T(8,128)(2,1)S(1)}, u32[]{:S(2)}, u32[]{:S(2)}) collective-permute-start(bf16[8,3,128,128]{3,2,1,0:T(8,128)(2,1)S(1)} %slice.155), channel_id=1, source_target_pairs={{0,96},{16,112},{32,0},{48,16},{64,32},{80,48},{96,64},{112,80},{1... | collective-permute-start | bytes 2359304 | tf_op jit(solution)/shard_map/ppermute | solution.py:391
  207.7 11.5 %collective-permute-start.30 = (bf16[4,352,128]{2,1,0:T(8,128)(2,1)S(1)}, bf16[4,352,128]{2,1,0:T(8,128)(2,1)S(1)}, u32[]{:S(2)}, u32[]{:S(2)}) collective-permute-start(bf16[4,352,128]{2,1,0:T(8,128)(2,1)S(1)} %get-tuple-element.162), channel_id=1, source_target_pairs={{0,4},{1,5},{2,6},{3,7},{16,20},{17,21},{18,22},{19,23},{32,36},{3... | collective-permute-start | bytes 1081352 | tf_op jit(solution)/shard_map/ppermute | solution.py:417
  221.8 134.6 %all-to-all-start.7 = ((bf16[128,2,128,128]{3,2,1,0:T(8,128)(2,1)}), bf16[128,2,128,128]{3,2,1,0:T(8,128)(2,1)}, u32[]{:S(2)}, u32[]{:S(2)}) async-start(bf16[128,2,128,128]{3,2,1,0:T(8,128)(2,1)} %bitcast.126), calls=%async_computation.7 | async-start | bytes 16777216 | tf_op jit(solution)/shard_map/all_to_all | solution.py:387
  236.0 107.8 %collective-permute-start.49 = (bf16[4,352,128]{2,1,0:T(8,128)(2,1)S(1)}, bf16[4,352,128]{2,1,0:T(8,128)(2,1)S(1)}, u32[]{:S(2)}, u32[]{:S(2)}) collective-permute-start(bf16[4,352,128]{2,1,0:T(8,128)(2,1)S(1)} %copy-done.13), channel_id=1, source_target_pairs={{0,4},{1,5},{2,6},{3,7},{4,0},{5,1},{6,2},{7,3},{8,12},{9,13},{10,... | collective-permute-start | bytes 1081352 | tf_op jit(solution)/shard_map/ppermute | solution.py:438
  237.5 111.8 %collective-permute-start.50 = (bf16[4,352,128]{2,1,0:T(8,128)(2,1)S(1)}, bf16[4,352,128]{2,1,0:T(8,128)(2,1)S(1)}, u32[]{:S(2)}, u32[]{:S(2)}) collective-permute-start(bf16[4,352,128]{2,1,0:T(8,128)(2,1)S(1)} %copy-done.13), channel_id=1, source_target_pairs={{0,8},{1,9},{2,10},{3,11},{4,12},{5,13},{6,14},{7,15},{8,0},{9,1},... | collective-permute-start | bytes 1081352 | tf_op jit(solution)/shard_map/ppermute | solution.py:438
  240.0 109.3 %collective-permute-start.51 = (bf16[4,352,128]{2,1,0:T(8,128)(2,1)S(1)}, bf16[4,352,128]{2,1,0:T(8,128)(2,1)S(1)}, u32[]{:S(2)}, u32[]{:S(2)}) collective-permute-start(bf16[4,352,128]{2,1,0:T(8,128)(2,1)S(1)} %copy-done.13), channel_id=1, source_target_pairs={{0,12},{1,13},{2,14},{3,15},{4,8},{5,9},{6,10},{7,11},{8,4},{9,5},... | collective-permute-start | bytes 1081352 | tf_op jit(solution)/shard_map/ppermute | solution.py:438
  240.0 109.5 %collective-permute-start.46 = (bf16[4,352,128]{2,1,0:T(8,128)(2,1)S(1)}, bf16[4,352,128]{2,1,0:T(8,128)(2,1)S(1)}, u32[]{:S(2)}, u32[]{:S(2)}) collective-permute-start(bf16[4,352,128]{2,1,0:T(8,128)(2,1)S(1)} %copy-done.14), channel_id=1, source_target_pairs={{0,1},{1,0},{2,3},{3,2},{4,5},{5,4},{6,7},{7,6},{8,9},{9,8},{10,11... | collective-permute-start | bytes 1081352 | tf_op jit(solution)/shard_map/ppermute | solution.py:438
  241.5 108.2 %collective-permute-start.47 = (bf16[4,352,128]{2,1,0:T(8,128)(2,1)S(1)}, bf16[4,352,128]{2,1,0:T(8,128)(2,1)S(1)}, u32[]{:S(2)}, u32[]{:S(2)}) collective-permute-start(bf16[4,352,128]{2,1,0:T(8,128)(2,1)S(1)} %copy-done.14), channel_id=1, source_target_pairs={{0,2},{1,3},{2,0},{3,1},{4,6},{5,7},{6,4},{7,5},{8,10},{9,11},{10,... | collective-permute-start | bytes 1081352 | tf_op jit(solution)/shard_map/ppermute | solution.py:438
  343.9 12.3 %collective-permute-start.48 = (bf16[4,352,128]{2,1,0:T(8,128)(2,1)S(1)}, bf16[4,352,128]{2,1,0:T(8,128)(2,1)S(1)}, u32[]{:S(2)}, u32[]{:S(2)}) collective-permute-start(bf16[4,352,128]{2,1,0:T(8,128)(2,1)S(1)} %copy-done.14), channel_id=1, source_target_pairs={{0,3},{1,2},{2,1},{3,0},{4,7},{5,6},{6,5},{7,4},{8,11},{9,10},{10,... | collective-permute-start | bytes 1081352 | tf_op jit(solution)/shard_map/ppermute | solution.py:438
  357.5 68.3 %all-to-all-start.8 = ((bf16[128,1,128,128]{3,2,1,0:T(8,128)(2,1)}), bf16[128,1,128,128]{3,2,1,0:T(8,128)(2,1)}, u32[]{:S(2)}, u32[]{:S(2)}) async-start(bf16[128,1,128,128]{3,2,1,0:T(8,128)(2,1)} %bitcast.129), calls=%async_computation.8 | async-start | bytes 8388608 | tf_op jit(solution)/shard_map/all_to_all | solution.py:387
  (64 other events, 1278.3 us)
